TPU v7x, 32 devices: a whole 2x2x4 slice. The times are simulated.
32 devices in a mesh: grp: 2 (over x), tm: 16 (over z, y, core).
Axes of the slice: x: 2, y: 2, z: 4, core: 2. Of those that a mesh axis runs over, the one named last changes fastest.
Arguments:
- dyn_a: float32 [128, 4, 64, 64], P('tm', 'grp'), parts along dimension 1, may hold values from -1 to 1
- dyn_b: float32 [128, 4, 64, 32], P('tm', 'grp'), parts along dimension 1, may hold values from -0.109375 to 0.109375
- gains: float32 [128, 4, 32, 64], P('tm', 'grp'), parts along dimension 1, may hold values from -0.2 to 0.2
- defects: float32 [128, 4, 64], P('tm', 'grp'), parts along dimension 1, may hold values from -6 to 6
- state_grad: float32 [128, 4, 64], P('tm', 'grp'), parts along dimension 1, may hold values from -6 to 6
- control_grad: float32 [128, 4, 32], P('tm', 'grp'), parts along dimension 1, may hold values from -1.5 to 1.5
- cost_factor: float32 [64, 64], replicated, may hold values from -0.75 to 0.75
- control_factor: float32 [32, 32], replicated, may hold values from -1 to 1
- init_state: float32 [4, 64], P('grp'), parts along dimension 0, may hold values from -6 to 6
Outputs:
- new_gains: float32 [128, 4, 32, 64], P('tm', 'grp'), parts along dimension 1
- feedforward: float32 [128, 4, 32], P('tm', 'grp'), parts along dimension 1
- states: float32 [128, 4, 64], P('tm', 'grp'), parts along dimension 1
- controls: float32 [128, 4, 32], P('tm', 'grp'), parts along dimension 1
- decrease: float32 [4], P('grp'), parts along dimension 0
There are 2 independent parts, one for each index of `grp`. A program takes and returns all parts, laid end to end along the dimension named above; an argument that names none is the same for every part. Nothing has to cross between parts.
All inputs are finite; a program needn't handle non-finite values.
Results may differ from a plain program's by a relative error of at most 0.0003.
Values sent between devices are 32-bit elements; how exact they have to be, the bound alone decides.
No kernel may reach another device: no remote copies, remote signals or barrier semaphores. Data moves between devices by JAX's collectives and lax.ppermute only.
A program may use at most 64 MiB of HBM per device.

v0:
```python
import math

import jax
import jax.numpy as jnp
from jax import lax
from jax.sharding import PartitionSpec as P


def carried_in(part, axis, combine, identity, reverse):
    count = lax.axis_size(axis)
    place = lax.axis_index(axis)
    ahead = count - 1 - place if reverse else place
    gathered = jax.tree.map(lambda a: lax.all_gather(a, axis), part)
    state = jax.tree.map(lambda a, e: jnp.zeros_like(a) + jnp.asarray(e, a.dtype), part, identity)

    def one(turn, state):
        source = count - 1 - turn if reverse else turn
        return combine(
            state, jax.tree.map(lambda a: lax.dynamic_index_in_dim(a, source, 0, False), gathered)
        )

    return lax.fori_loop(0, ahead, one, state)


def product(left, right):
    return jnp.matmul(left, right, precision=lax.Precision.HIGHEST)


def flipped(matrix):
    return jnp.swapaxes(matrix, -1, -2)


def apply_vec(matrix, vector):
    return product(matrix, vector[..., None])[..., 0]


def spd_solve(matrix, right_side):
    factor = jnp.linalg.cholesky(matrix)
    inner = jax.scipy.linalg.solve_triangular(factor, right_side, lower=True)
    return jax.scipy.linalg.solve_triangular(factor, inner, lower=True, trans=1)


def compose_value(later, earlier):
    f_late, q_late, h_late, g_late = later
    f_early, q_early, h_early, g_early = earlier
    merged_f = product(f_early, f_late)
    merged_q = product(flipped(f_late), product(q_early, f_late)) + q_late
    merged_h = h_early + apply_vec(f_early, h_late)
    merged_g = apply_vec(flipped(f_late), g_early + apply_vec(q_early, h_late)) + g_late
    return (merged_f, merged_q, merged_h, merged_g)


def value_combine(earlier, later):
    return compose_value(later, earlier)


def compose_state(earlier, later):
    m_early, c_early = earlier
    m_late, c_late = later
    return (product(m_late, m_early), apply_vec(m_late, c_early) + c_late)


def value_joined(lower, higher):
    return compose_value(lower, higher)


def state_joined(lower, higher):
    return compose_state(lower, higher)


def fold_tree(elems, joined):
    while elems[0].shape[0] > 1:
        count = elems[0].shape[0]
        half = count // 2
        lower = tuple((item[0 : 2 * half : 2] for item in elems))
        higher = tuple((item[1 : 2 * half : 2] for item in elems))
        merged = joined(lower, higher)
        elems = merged
    return tuple((item[0] for item in elems))


def fold_local(elems, joined):
    return fold_tree(elems, joined)


def shards(
    dyn_a, dyn_b, gains, defects, state_grad, control_grad, cost_factor, control_factor, init_state
):
    local_knots, trajs, width, controls_n = dyn_b.shape
    knots = local_knots * lax.axis_size("tm")
    scale = 1.0 / math.sqrt(knots)
    term_q = jnp.eye(width, dtype=jnp.float32) + product(cost_factor, flipped(cost_factor))
    run_q = term_q / knots
    run_r = jnp.eye(controls_n, dtype=jnp.float32) + product(
        control_factor, flipped(control_factor)
    )
    drift = defects * scale
    closed = dyn_a + product(dyn_b, gains)
    section_q = run_q + product(flipped(gains), product(run_r, gains))
    section_g = state_grad * scale + apply_vec(flipped(gains), control_grad)
    summary = fold_local((closed, section_q, drift, section_g), value_joined)
    count = trajs - 0
    identity = (
        jnp.broadcast_to(jnp.eye(width, dtype=jnp.float32), (count, width, width)),
        jnp.zeros((count, width, width), jnp.float32),
        jnp.zeros((count, width), jnp.float32),
        jnp.zeros((count, width), jnp.float32),
    )
    pre_f, pre_q, pre_h, pre_g = carried_in(summary, "tm", value_combine, identity, True)
    end_mat = product(flipped(pre_f), product(term_q, pre_f)) + pre_q
    end_vec = apply_vec(flipped(pre_f), apply_vec(term_q, pre_h)) + pre_g

    def back_step(carry, item):
        value_mat, value_vec = carry
        a_mat, b_mat, f_mat, q_mat, d_vec, g_vec, r_vec = item
        value_b = product(value_mat, b_mat)
        hess = run_r + product(flipped(b_mat), value_b)
        cross = product(flipped(value_b), a_mat)
        lin = r_vec + apply_vec(flipped(b_mat), apply_vec(value_mat, d_vec) + value_vec)
        solved = spd_solve(hess, jnp.concatenate([cross, lin[..., None]], -1))
        new_gain = -solved[..., :width]
        feed = -solved[..., width]
        change = jnp.sum(feed * lin, -1) + 0.5 * jnp.sum(feed * apply_vec(hess, feed), -1)
        step_m = a_mat + product(b_mat, new_gain)
        step_c = apply_vec(b_mat, feed) + d_vec
        next_mat = product(flipped(f_mat), product(value_mat, f_mat)) + q_mat
        next_vec = apply_vec(flipped(f_mat), value_vec + apply_vec(value_mat, d_vec)) + g_vec
        return ((next_mat, next_vec), (new_gain, feed, change, step_m, step_c))

    items = (dyn_a, dyn_b, closed, section_q, drift, section_g, control_grad)
    _, results = lax.scan(back_step, (end_mat, end_vec), items, reverse=True)
    new_gains, feedforward, changes, step_m, step_c = results
    decrease = lax.psum(jnp.sum(changes, 0), "tm") / knots
    state_summary = fold_local((step_m, step_c), state_joined)
    state_identity = (
        jnp.broadcast_to(jnp.eye(width, dtype=jnp.float32), (trajs, width, width)),
        jnp.zeros((trajs, width), jnp.float32),
    )
    prefix_m, prefix_c = carried_in(state_summary, "tm", compose_state, state_identity, False)
    start_state = apply_vec(prefix_m, init_state) + prefix_c

    def forward_step(state, item):
        a_mat, b_mat, new_gain, feed, d_vec = item
        control = apply_vec(new_gain, state) + feed
        following = apply_vec(a_mat, state) + apply_vec(b_mat, control) + d_vec
        return (following, (state, control))

    _, (states, controls) = lax.scan(
        forward_step, start_state, (dyn_a, dyn_b, new_gains, feedforward, drift)
    )
    return (new_gains, feedforward, states, controls, decrease)


def solution(mesh):
    in_specs = (
        P("tm", "grp", None, None),
        P("tm", "grp", None, None),
        P("tm", "grp", None, None),
        P("tm", "grp", None),
        P("tm", "grp", None),
        P("tm", "grp", None),
        P(),
        P(),
        P("grp", None),
    )
    out_specs = (
        P("tm", "grp", None, None),
        P("tm", "grp", None),
        P("tm", "grp", None),
        P("tm", "grp", None),
        P("grp"),
    )
    return jax.shard_map(shards, mesh=mesh, in_specs=in_specs, out_specs=out_specs, check_vma=False)
```

profile of v0, /device:TPU:0, one launch (start us, length us, event | category | flops | bytes accessed | tf_op | source)
XLA Modules:
  0.0 338.5 jit_solution(10951159836824277851)
XLA Ops:
  11.0 23.1 %all_gather.21 = f32[16,2,64]{2,1,0:T(2,128)S(1)} all-gather(f32[1,2,64]{2,1,0:T(2,128)S(1)} %slice_add_fusion.9), channel_id=1, replica_groups=mesh['grp'=2,'tm'=16] {'tm'}, dimensions={0}, use_global_device_ids=true | all-gather | bytes 8704 | tf_op jit(solution)/shard_map/all_gather | solution.py:13
  34.7 21.9 %all_gather.19 = f32[16,2,64,64]{3,2,1,0:T(8,128)} all-gather(f32[1,2,64,64]{3,2,1,0:T(8,128)S(1)} %copy.85), channel_id=1, replica_groups=mesh['grp'=2,'tm'=16] {'tm'}, dimensions={0}, use_global_device_ids=true | all-gather | bytes 557056 | tf_op jit(solution)/shard_map/all_gather | solution.py:13
  56.8 19.3 %all_gather.20 = f32[16,2,64]{2,1,0:T(2,128)S(1)} all-gather(f32[1,2,64]{2,1,0:T(2,128)S(1)} %slice_add_fusion.11), channel_id=1, replica_groups=mesh['grp'=2,'tm'=16] {'tm'}, dimensions={0}, use_global_device_ids=true | all-gather | bytes 8704 | tf_op jit(solution)/shard_map/all_gather | solution.py:13
  76.3 20.7 %all-gather = f32[32,64,64]{2,1,0:T(8,128)S(1)} all-gather(f32[2,64,64]{2,1,0:T(8,128)S(1)} %fusion.135), channel_id=2, replica_groups=mesh['grp'=2,'tm'=16] {'tm'}, dimensions={0}, use_global_device_ids=true | all-gather | bytes 557056 | tf_op jit(solution)/shard_map/all_gather | solution.py:13
  97.1 36.0 %while.70 = (s32[]{:T(128)}, f32[2,64,64]{1,2,0:T(8,128)S(1)}, f32[2,64,64]{2,1,0:T(8,128)S(1)}, f32[2,64]{1,0:T(2,128)S(1)}, f32[2,64]{1,0:T(2,128)S(1)}, /*ind...) while((s32[]{:T(128)}, f32[2,64,64]{1,2,0:T(8,128)S(1)}, ...), condition=%wide.region_1.2_spmd, body=%wide.region_0.1_spmd.sunk | while | flops 19177860 | bytes 731335 | solution.py:22
  134.2 117.8 %while.71 = (s32[]{:T(128)}, f32[2,64,64]{2,1,0:T(8,128)S(1)}, f32[2,64]{1,0:T(2,128)S(1)}, f32[8,2,32,64]{3,2,1,0:T(8,128)S(1)}, f32[8,2,32]{2,1,0:T(2,128)S(1)...) while((s32[]{:T(128)}, f32[2,64,64]{2,1,0:T(8,128)S(1)}, ...), condition=%wide.region_7.8_spmd, body=%wide.region_2.7_spmd.sunk | while | flops 27159488 | bytes 1454393 | solution.py:131
  134.8 5.9 %custom-call.25 = f32[2,32,32]{2,1,0:T(8,128)S(1)} custom-call(f32[2,32,32]{2,1,0:T(8,128)S(1)} %fusion.337), custom_call_target="Cholesky" | custom-call | tf_op jit(solution)/shard_map/while/body/eval_jaxpr/jit(cholesky)/cholesky | solution.py:38
  141.0 4.9 %custom-call.26 = f32[2,1,32,32]{2,3,1,0:T(8,128)S(1)} custom-call(f32[2,1,32,32]{3,2,1,0:T(8,128)S(1)} %select_bitcast_fusion.2), custom_call_target="InvertDiagBlocksLowerTriangular" | custom-call | tf_op jit(solution)/shard_map/while/body/eval_jaxpr/jit(_solve_triangular)/vmap()/triangular_solve | solution.py:40
  149.6 5.9 %custom-call.25 = f32[2,32,32]{2,1,0:T(8,128)S(1)} custom-call(f32[2,32,32]{2,1,0:T(8,128)S(1)} %fusion.337), custom_call_target="Cholesky" | custom-call | tf_op jit(solution)/shard_map/while/body/eval_jaxpr/jit(cholesky)/cholesky | solution.py:38
  155.7 4.9 %custom-call.26 = f32[2,1,32,32]{2,3,1,0:T(8,128)S(1)} custom-call(f32[2,1,32,32]{3,2,1,0:T(8,128)S(1)} %select_bitcast_fusion.2), custom_call_target="InvertDiagBlocksLowerTriangular" | custom-call | tf_op jit(solution)/shard_map/while/body/eval_jaxpr/jit(_solve_triangular)/vmap()/triangular_solve | solution.py:40
  164.3 5.9 %custom-call.25 = f32[2,32,32]{2,1,0:T(8,128)S(1)} custom-call(f32[2,32,32]{2,1,0:T(8,128)S(1)} %fusion.337), custom_call_target="Cholesky" | custom-call | tf_op jit(solution)/shard_map/while/body/eval_jaxpr/jit(cholesky)/cholesky | solution.py:38
  170.4 4.9 %custom-call.26 = f32[2,1,32,32]{2,3,1,0:T(8,128)S(1)} custom-call(f32[2,1,32,32]{3,2,1,0:T(8,128)S(1)} %select_bitcast_fusion.2), custom_call_target="InvertDiagBlocksLowerTriangular" | custom-call | tf_op jit(solution)/shard_map/while/body/eval_jaxpr/jit(_solve_triangular)/vmap()/triangular_solve | solution.py:40
  179.0 5.9 %custom-call.25 = f32[2,32,32]{2,1,0:T(8,128)S(1)} custom-call(f32[2,32,32]{2,1,0:T(8,128)S(1)} %fusion.337), custom_call_target="Cholesky" | custom-call | tf_op jit(solution)/shard_map/while/body/eval_jaxpr/jit(cholesky)/cholesky | solution.py:38
  185.1 4.9 %custom-call.26 = f32[2,1,32,32]{2,3,1,0:T(8,128)S(1)} custom-call(f32[2,1,32,32]{3,2,1,0:T(8,128)S(1)} %select_bitcast_fusion.2), custom_call_target="InvertDiagBlocksLowerTriangular" | custom-call | tf_op jit(solution)/shard_map/while/body/eval_jaxpr/jit(_solve_triangular)/vmap()/triangular_solve | solution.py:40
  193.7 5.9 %custom-call.25 = f32[2,32,32]{2,1,0:T(8,128)S(1)} custom-call(f32[2,32,32]{2,1,0:T(8,128)S(1)} %fusion.337), custom_call_target="Cholesky" | custom-call | tf_op jit(solution)/shard_map/while/body/eval_jaxpr/jit(cholesky)/cholesky | solution.py:38
  199.8 4.9 %custom-call.26 = f32[2,1,32,32]{2,3,1,0:T(8,128)S(1)} custom-call(f32[2,1,32,32]{3,2,1,0:T(8,128)S(1)} %select_bitcast_fusion.2), custom_call_target="InvertDiagBlocksLowerTriangular" | custom-call | tf_op jit(solution)/shard_map/while/body/eval_jaxpr/jit(_solve_triangular)/vmap()/triangular_solve | solution.py:40
  208.4 5.9 %custom-call.25 = f32[2,32,32]{2,1,0:T(8,128)S(1)} custom-call(f32[2,32,32]{2,1,0:T(8,128)S(1)} %fusion.337), custom_call_target="Cholesky" | custom-call | tf_op jit(solution)/shard_map/while/body/eval_jaxpr/jit(cholesky)/cholesky | solution.py:38
  214.6 4.9 %custom-call.26 = f32[2,1,32,32]{2,3,1,0:T(8,128)S(1)} custom-call(f32[2,1,32,32]{3,2,1,0:T(8,128)S(1)} %select_bitcast_fusion.2), custom_call_target="InvertDiagBlocksLowerTriangular" | custom-call | tf_op jit(solution)/shard_map/while/body/eval_jaxpr/jit(_solve_triangular)/vmap()/triangular_solve | solution.py:40
  223.2 5.9 %custom-call.25 = f32[2,32,32]{2,1,0:T(8,128)S(1)} custom-call(f32[2,32,32]{2,1,0:T(8,128)S(1)} %fusion.337), custom_call_target="Cholesky" | custom-call | tf_op jit(solution)/shard_map/while/body/eval_jaxpr/jit(cholesky)/cholesky | solution.py:38
  237.9 5.9 %custom-call.25 = f32[2,32,32]{2,1,0:T(8,128)S(1)} custom-call(f32[2,32,32]{2,1,0:T(8,128)S(1)} %fusion.337), custom_call_target="Cholesky" | custom-call | tf_op jit(solution)/shard_map/while/body/eval_jaxpr/jit(cholesky)/cholesky | solution.py:38
  255.2 17.1 %all_gather.23 = f32[16,2,64]{2,1,0:T(2,128)S(1)} all-gather(f32[1,2,64]{2,1,0:T(2,128)S(1)} %slice_add_fusion.8), channel_id=1, replica_groups=mesh['grp'=2,'tm'=16] {'tm'}, dimensions={0}, use_global_device_ids=true | all-gather | bytes 8704 | tf_op jit(solution)/shard_map/all_gather | solution.py:13
  272.5 22.2 %all-gather.1 = f32[32,64,64]{2,1,0:T(8,128)S(1)} all-gather(f32[2,64,64]{2,1,0:T(8,128)S(1)} %fusion.129), channel_id=3, replica_groups=mesh['grp'=2,'tm'=16] {'tm'}, dimensions={0}, use_global_device_ids=true | all-gather | bytes 557056 | tf_op jit(solution)/shard_map/all_gather | solution.py:13
  295.7 4.9 %while.73 = (s32[]{:T(128)}, f32[2,64]{1,0:T(2,128)S(1)}, f32[8,2,64]{2,1,0:T(2,128)S(1)}, f32[8,2,32]{2,1,0:T(2,128)S(1)}, f32[8,2,64,64]{3,2,1,0:T(8,128)S(1)}...) while((s32[]{:T(128)}, f32[2,64]{1,0:T(2,128)S(1)}, ...), condition=%wide.region_11.12_spmd, body=%wide.region_10.11_spmd.sunk | while | flops 196994 | bytes 143489 | solution.py:148
  300.7 37.0 %psum.7 = f32[2]{0:T(128)S(1)} all-reduce(f32[2]{0:T(128)S(1)} %reduce_sum.39), channel_id=1, replica_groups=mesh['grp'=2,'tm'=16] {'tm'}, use_global_device_ids=true, to_apply=%region_13.14 | all-reduce | flops 2 | bytes 16 | tf_op jit(solution)/shard_map/psum | solution.py:133
  (609 shorter events, 97.5 us)
Async XLA Ops:
  0.6 1.0 copy-start
  1.6 0.8 copy-start.4
  2.6 1.1 copy-start.1
  2.7 1.1 copy-start.2
  6.8 0.7 copy-start.5
  7.5 0.7 copy-start.7
  7.5 0.7 copy-start.8
  253.3 0.6 copy-start.9
  253.9 0.7 slice-start
  254.5 0.7 copy-start.10
  294.8 0.7 copy-start.13
  300.7 37.6 %copy-start.3 = (f32[8,2,32,64]{3,2,1,0:T(8,128)}, f32[8,2,32,64]{3,2,1,0:T(8,128)S(1)}, u32[]{:S(2)}) copy-start(f32[8,2,32,64]{3,2,1,0:T(8,128)S(1)} %get-tuple-element.1153) | copy-start | bytes 393220
  300.7 37.6 %copy-start.6 = (f32[8,2,32]{2,1,0:T(2,128)}, f32[8,2,32]{2,1,0:T(2,128)S(1)}, u32[]{:S(2)}) copy-start(f32[8,2,32]{2,1,0:T(2,128)S(1)} %get-tuple-element.1155) | copy-start | bytes 6148
  300.7 37.6 %copy-start.11 = (f32[8,2,32]{2,1,0:T(2,128)}, f32[8,2,32]{2,1,0:T(2,128)S(1)}, u32[]{:S(2)}) copy-start(f32[8,2,32]{2,1,0:T(2,128)S(1)} %get-tuple-element.532) | copy-start | bytes 6148
  300.7 37.6 %copy-start.12 = (f32[8,2,64]{2,1,0:T(2,128)}, f32[8,2,64]{2,1,0:T(2,128)S(1)}, u32[]{:S(2)}) copy-start(f32[8,2,64]{2,1,0:T(2,128)S(1)} %get-tuple-element.531) | copy-start | bytes 12292
where the time goes:
time: 340 us; the launch traced here: 338 us
  blocking collectives  161 us (47%)
  other arithmetic  92.6 us (27%)
  matrix products  74.1 us (22%)
  local copies, waits for them, and re-layouts  7.09 us (2%)
    all_gather x6, blocking collectives, carried_in(): gathered = jax.tree.map(lambda a: lax.all_gather(a, axis), part)  124 us
    dot_general x237, matrix products, product(): return jnp.matmul(left, right, precision=lax.Precision.HIGHEST)  70.7 us
    another operation x32, other arithmetic, spd_solve(): factor = jnp.linalg.cholesky(matrix)  48.2 us
    another operation x24, other arithmetic, spd_solve(): return jax.scipy.linalg.solve_triangular(factor, inner, lower=True, trans=1)  39.9 us
    psum x1, blocking collectives, shards(): decrease = lax.psum(jnp.sum(changes, 0), 'tm') / knots  37 us

commit v1 on v0

v1 whole, which is shorter than its diff:
```python
import functools
import math

import jax
import jax.numpy as jnp
from jax import lax
from jax.experimental import pallas as pl
from jax.experimental.pallas import tpu as pltpu
from jax.sharding import PartitionSpec as P

F32 = jnp.float32
LANES = 128
TAIL = 8


def lane_block(shape, size):
    return lax.broadcasted_iota(jnp.int32, shape, 1) // size


def spread(pair, trajs):
    block = lane_block(pair.shape, pair.shape[1] // trajs)
    return jnp.concatenate([jnp.where(block == j, pair, 0.0) for j in range(trajs)], axis=0)


def split(x):
    high = x.astype(jnp.bfloat16)
    low = (x - high.astype(F32)).astype(jnp.bfloat16)
    return high, low


def prod(left, right, flip=False):
    depth, wide = (1, 0) if flip else (0, 1)
    columns = right.shape[wide]
    if columns % LANES:
        shape = list(right.shape)
        shape[wide] = -columns % LANES
        right = jnp.concatenate([right, jnp.zeros(shape, F32)], axis=wide)
    full = right.shape[wide]
    (lh, ll), (rh, rl) = split(left), split(right)
    rows = left.shape[0]
    both = jnp.concatenate([rh, rl], axis=wide)
    dims = (((1,), (depth,)), ((), ()))
    if left.shape[1] % LANES:
        w = lax.dot_general(jnp.concatenate([lh, ll], axis=0), both, dims, preferred_element_type=F32)
        w = w[:rows] + w[rows:]
    else:
        w = lax.dot_general(
            jnp.concatenate([lh, ll], axis=1), jnp.concatenate([both, both], axis=depth), dims,
            preferred_element_type=F32,
        )
    w = w[:, :full] + w[:, full:]
    return w[:, :columns] if columns < full else w


def tail_of(row):
    shape = (TAIL, row.shape[1])
    return jnp.where(lax.broadcasted_iota(jnp.int32, shape, 0) == 0, jnp.broadcast_to(row, shape), 0.0)


def join(matrix, tail):
    return jnp.concatenate([matrix, tail], axis=0)


def apply_value(x, y, later, trajs, width):
    w = prod(later, spread(x[:width], trajs), flip=True)
    z = prod(x, spread(w[:width], trajs)) + y
    return join(z[:width], z[width:] + w[width:])


def compose_state(first, second, trajs, width):
    z = prod(first, spread(second[:width], trajs))
    return join(z[:width], z[width:] + second[width:])


def compose_value(first, second, trajs, width):
    (x1, y1), (x2, y2) = first, second
    return compose_state(x1, x2, trajs, width), apply_value(x1, y1, y2, trajs, width)


def fold(items, joined):
    while len(items) > 1:
        rest = items[len(items) // 2 * 2 :]
        items = [joined(items[i], items[i + 1]) for i in range(0, len(items) - 1, 2)] + rest
    return items[0]


def prefixes(items, joined):
    items, step = list(items), 1
    while step < len(items):
        items = [items[i] if i < step else joined(items[i - step], items[i]) for i in range(len(items))]
        step *= 2
    return items


def identity_pair(width, trajs):
    rows = lax.broadcasted_iota(jnp.int32, (width, width * trajs), 0)
    lanes = lax.broadcasted_iota(jnp.int32, (width, width * trajs), 1)
    return jnp.where(rows == lanes % width, 1.0, 0.0)


def side_by_side(rows, trajs):
    return jnp.concatenate([rows[:, j] for j in range(trajs)], axis=1)


def term_of(cost_factor, trajs):
    width = cost_factor.shape[0]
    return prod(cost_factor, jnp.concatenate([cost_factor] * trajs, axis=0), flip=True) + identity_pair(width, trajs)


def block_kernel(knots, a_ref, b_ref, g_ref, d_ref, sg_ref, cg_ref, cf_ref, rf_ref, total_ref, own_ref, term_ref):
    count, trajs, width, nu = b_ref.shape
    scale = 1.0 / math.sqrt(knots)
    term = term_of(cf_ref[...], trajs)
    run_q = term / knots
    term_ref[...] = join(term, jnp.zeros((TAIL, width * trajs), F32))
    rows = lax.broadcasted_iota(jnp.int32, (nu, nu), 0)
    lanes = lax.broadcasted_iota(jnp.int32, (nu, nu), 1)
    root = jnp.concatenate([jnp.where(rows == lanes, 1.0, 0.0), rf_ref[...]], axis=1)
    root = spread(jnp.concatenate([root] * trajs, axis=1), trajs)
    drift = side_by_side(d_ref[...], trajs) * scale
    grad = side_by_side(sg_ref[...], trajs) * scale
    cg = cg_ref[...]
    nothing = jnp.zeros((count, nu), F32)
    control = jnp.concatenate([piece for j in range(trajs) for piece in (cg[:, j], nothing)], axis=1)
    maps = []
    for t in range(count):
        at = a_ref[t].reshape(trajs * width, width).T
        bt = b_ref[t].reshape(trajs * width, nu).T
        gt = g_ref[t].reshape(trajs * nu, width).T
        both = prod(gt, jnp.concatenate([spread(bt, trajs), root], axis=1))
        x = join(at + both[:, : trajs * width], tail_of(drift[t : t + 1]))
        z = both[:, trajs * width :]
        y = prod(join(z, tail_of(control[t : t + 1])), spread(z, trajs), flip=True)
        y = y + join(run_q, tail_of(grad[t : t + 1]))
        own_ref[t, 0] = x
        own_ref[t, 1] = y
        maps.append((x, y))
    x, y = fold(maps, lambda a, b: compose_value(a, b, trajs, width))
    total_ref[0] = x
    total_ref[1] = y


def suffix_kernel(own_ref, out_ref, *, trajs, width):
    count = own_ref.shape[0]
    maps = [(own_ref[t, 0], own_ref[t, 1]) for t in reversed(range(1, count))]
    done = prefixes(maps, lambda later, earlier: compose_value(earlier, later, trajs, width))
    for i, (x, y) in enumerate(done):
        out_ref[count - 2 - i, 0] = x
        out_ref[count - 2 - i, 1] = y


def upper(step):
    return lax.rem(lax.axis_index("tm") // step, 2) == 1


def value_step_kernel(step, own_ref, got_ref, seen_ref, total_ref, next_ref, *, trajs, width):
    up = upper(step)
    own, got = (own_ref[0], own_ref[1]), (got_ref[0], got_ref[1])
    first = [jnp.where(up, g, o) for o, g in zip(own, got)]
    second = [jnp.where(up, o, g) for o, g in zip(own, got)]
    x, y = compose_value(first, second, trajs, width)
    total_ref[0] = x
    total_ref[1] = y
    if seen_ref is None:
        nothing = (join(identity_pair(width, trajs), jnp.zeros((TAIL, trajs * width), F32)), jnp.zeros_like(own[0]))
        sx, sy = got
    else:
        nothing = (seen_ref[0], seen_ref[1])
        sx, sy = compose_value(nothing, got, trajs, width)
    next_ref[0] = jnp.where(up, nothing[0], sx)
    next_ref[1] = jnp.where(up, nothing[1], sy)


def value_last_kernel(step, own_ref, got_ref, seen_ref, term_ref, value_ref, next_ref, *, trajs, width):
    up = upper(step)
    own, got = (own_ref[0], own_ref[1]), (got_ref[0], got_ref[1])
    first = [jnp.where(up, g, o) for o, g in zip(own, got)]
    second = [jnp.where(up, o, g) for o, g in zip(own, got)]
    value = apply_value(*second, term_ref[...], trajs, width)
    value_ref[...] = apply_value(*first, value, trajs, width)
    seen = (seen_ref[0], seen_ref[1])
    sx, sy = compose_value(seen, got, trajs, width)
    next_ref[0] = jnp.where(up, seen[0], sx)
    next_ref[1] = jnp.where(up, seen[1], sy)


def solve_kernel(
    knots, step, a_ref, b_ref, d_ref, cg_ref, rf_ref, term_ref, value_ref, seen_ref, suffix_ref,
    gain_ref, feed_ref, total_ref, own_ref, kt_ref,
):
    count, trajs, width, nu = b_ref.shape
    both = trajs * width
    scale = 1.0 / math.sqrt(knots)
    drift = side_by_side(d_ref[...], trajs) * scale
    control = side_by_side(cg_ref[...], trajs)
    control_columns = control.T
    rf = rf_ref[...]
    rows = lax.broadcasted_iota(jnp.int32, (nu, nu), 0)
    lanes = lax.broadcasted_iota(jnp.int32, (nu, nu), 1)
    run_r = prod(rf, rf, flip=True) + jnp.where(rows == lanes, 1.0, 0.0)
    fill = jnp.zeros((nu, both - width - nu), F32)
    run_r = jnp.concatenate([jnp.zeros((nu, width), F32), run_r, fill], axis=1)
    run_r = jnp.concatenate([run_r] * trajs, axis=0)
    lin_lane = lax.broadcasted_iota(jnp.int32, (trajs * nu, both), 1) == width + nu

    end = jnp.where(upper(step), term_ref[...], value_ref[...])
    end = apply_value(seen_ref[0], seen_ref[1], end, trajs, width)
    systems, transposed = [], []
    for t in range(count):
        value = end if t == count - 1 else apply_value(suffix_ref[t, 0], suffix_ref[t, 1], end, trajs, width)
        a = a_ref[t].reshape(both, width)
        b = b_ref[t].reshape(both, nu)
        bt = b.T
        bd = spread(bt, trajs)
        u = prod(join(bt, tail_of(drift[t : t + 1])), spread(value[:width], trajs))
        q = u[nu : nu + 1] + value[width : width + 1]
        ab = jnp.concatenate([a, b, jnp.zeros((both, both - width - nu), F32)], axis=1)
        lin = jnp.sum(bd * q, axis=1, keepdims=True) + control_columns[:, t : t + 1]
        system = prod(spread(u[:nu], trajs), ab) + run_r
        systems.append(jnp.where(lin_lane, lin, system))
        transposed.append((a.T, bd))

    solved = list(systems)
    row_at = lax.broadcasted_iota(jnp.int32, (nu, both), 0)
    for k in range(nu):
        for t in range(count):
            parts = []
            for j in range(trajs):
                s = solved[t][j * nu : (j + 1) * nu]
                pivot = s[k : k + 1]
                pivot = pivot / pivot[:, width + k : width + k + 1]
                s = s - s[:, width + k : width + k + 1] * pivot
                parts.append(jnp.where(row_at == k, pivot, s))
            solved[t] = jnp.concatenate(parts, axis=0)

    decrease = jnp.zeros((1, trajs * nu), F32)
    maps = []
    for t in range(count):
        neg = -solved[t]
        gain_ref[t] = neg[:, :width].reshape(trajs, nu, width)
        flat = neg.T
        feed = flat[width + nu : width + nu + 1]
        for j in range(trajs):
            feed_ref[t : t + 1, j] = feed[:, j * nu : (j + 1) * nu]
        kt = join(flat[:width], tail_of(feed))
        kt_ref[t] = kt
        weighted = neg[:, width + nu : width + nu + 1] * systems[t]
        parts = []
        for j in range(trajs):
            w = jnp.sum(weighted[j * nu : (j + 1) * nu], axis=0, keepdims=True)
            linear = w[:, width + nu : width + nu + 1]
            square = jnp.sum(w[:, width : width + nu] * feed[:, j * nu : (j + 1) * nu], axis=1, keepdims=True)
            parts.append(jnp.broadcast_to(linear + 0.5 * square, (1, nu)))
        decrease = decrease + jnp.concatenate(parts, axis=1)
        at, bd = transposed[t]
        m = prod(kt, bd) + join(at, tail_of(drift[t : t + 1]))
        own_ref[t] = m
        maps.append(m)
    size = width + TAIL
    total_ref[:size] = fold(maps, lambda a, b: compose_state(a, b, trajs, width))
    spare = jnp.zeros((1, both - trajs * nu), F32)
    total_ref[size:] = tail_of(jnp.concatenate([decrease, spare], axis=1))


def prefix_kernel(own_ref, out_ref, *, trajs, width):
    maps = [own_ref[t] for t in range(own_ref.shape[0] - 1)]
    for t, m in enumerate(prefixes(maps, lambda a, b: compose_state(a, b, trajs, width))):
        out_ref[t] = m


def state_step_kernel(step, own_ref, got_ref, seen_ref, total_ref, next_ref, *, trajs, width):
    up = upper(step)
    size = width + TAIL
    own, got = own_ref[:size], got_ref[:size]
    total_ref[:size] = compose_state(jnp.where(up, got, own), jnp.where(up, own, got), trajs, width)
    total_ref[size:] = own_ref[size:] + got_ref[size:]
    if seen_ref is None:
        seen = join(identity_pair(width, trajs), jnp.zeros((TAIL, trajs * width), F32))
        after = got
    else:
        seen = seen_ref[...]
        after = compose_state(got, seen, trajs, width)
    next_ref[...] = jnp.where(up, after, seen)


def state_last_kernel(step, own_ref, got_ref, seen_ref, init_ref, sent_ref, next_ref, *, trajs, width):
    up = upper(step)
    size = width + TAIL
    own, got = own_ref[:size], got_ref[:size]
    total = compose_state(jnp.where(up, got, own), jnp.where(up, own, got), trajs, width)
    init = tail_of(jnp.concatenate([init_ref[j : j + 1] for j in range(trajs)], axis=1))
    sent_ref[:TAIL] = prod(init, spread(total[:width], trajs)) + total[width:]
    sent_ref[TAIL:] = own_ref[size:] + got_ref[size:]
    seen = seen_ref[...]
    next_ref[...] = jnp.where(up, compose_state(got, seen, trajs, width), seen)


def rollout_kernel(knots, step, own_ref, got_ref, seen_ref, init_ref, prefix_ref, kt_ref,
                   state_ref, control_ref, decrease_ref):
    count, trajs, width = state_ref.shape
    nu = control_ref.shape[2]
    init = tail_of(jnp.concatenate([init_ref[j : j + 1] for j in range(trajs)], axis=1))
    start = jnp.where(upper(step), got_ref[:TAIL], init)
    start = prod(start, spread(seen_ref[:width], trajs)) + seen_ref[width:]
    for t in range(count):
        state = start
        if t > 0:
            state = prod(start, spread(prefix_ref[t - 1, :width], trajs)) + prefix_ref[t - 1, width:]
        control = prod(state, spread(kt_ref[t, :width], trajs)) + kt_ref[t, width:]
        for j in range(trajs):
            state_ref[t : t + 1, j] = state[:1, j * width : (j + 1) * width]
            control_ref[t : t + 1, j] = control[:1, j * nu : (j + 1) * nu]
    sums = (own_ref[TAIL : TAIL + 1] + got_ref[TAIL : TAIL + 1]) / knots
    for j in range(trajs):
        decrease_ref[:, j : j + 1] = sums[:, j * nu : j * nu + 1]


def call(body, outs, *args):
    return pl.pallas_call(
        body,
        out_shape=[jax.ShapeDtypeStruct(shape, F32) for shape in outs],
        compiler_params=pltpu.CompilerParams(vmem_limit_bytes=32 * 1024 * 1024),
    )(*args)


def without(body, at):
    @functools.wraps(body)
    def inner(*refs, **named):
        return body(*refs[:at], None, *refs[at:], **named)

    return inner


def shards(dyn_a, dyn_b, gains, defects, state_grad, control_grad, cost_factor, control_factor, init_state):
    count, trajs, width, nu = dyn_b.shape
    devices = lax.axis_size("tm")
    knots = count * devices
    both, size = trajs * width, width + TAIL
    sizes = dict(trajs=trajs, width=width)
    steps = [1 << i for i in range(devices.bit_length() - 1)]

    def exchange(value, step):
        return lax.ppermute(value, "tm", [(i, i ^ step) for i in range(devices)])

    total, own, term = call(
        functools.partial(block_kernel, knots),
        [(2, size, both), (count, 2, size, both), (size, both)],
        dyn_a, dyn_b, gains, defects, state_grad, control_grad, cost_factor, control_factor,
    )
    suffix, = call(functools.partial(suffix_kernel, **sizes), [(count - 1, 2, size, both)], own)
    seen = []
    for step in steps[:-2]:
        body = value_step_kernel if seen else without(value_step_kernel, 3)
        got = exchange(total, step)
        total, after = call(
            functools.partial(body, step, **sizes), [(2, size, both)] * 2, total, got, *seen
        )
        seen = [after]
    got = exchange(total, steps[-2])
    value, after = call(
        functools.partial(value_last_kernel, steps[-2], **sizes),
        [(size, both), (2, size, both)], total, got, *seen, term,
    )
    value = exchange(value, steps[-1])
    new_gains, feedforward, total, own, kt = call(
        functools.partial(solve_kernel, knots, steps[-1]),
        [(count, trajs, nu, width), (count, trajs, nu), (size + TAIL, both), (count, size, both),
         (count, size, trajs * nu)],
        dyn_a, dyn_b, defects, control_grad, control_factor, term, value, after, suffix,
    )
    prefix, = call(functools.partial(prefix_kernel, **sizes), [(count - 1, size, both)], own)
    seen = []
    for step in steps[:-2]:
        body = state_step_kernel if seen else without(state_step_kernel, 3)
        got = exchange(total, step)
        total, after = call(
            functools.partial(body, step, **sizes), [(size + TAIL, both), (size, both)], total, got, *seen
        )
        seen = [after]
    got = exchange(total, steps[-2])
    sent, after = call(
        functools.partial(state_last_kernel, steps[-2], **sizes),
        [(2 * TAIL, both), (size, both)], total, got, *seen, init_state,
    )
    got = exchange(sent, steps[-1])
    states, controls, decrease = call(
        functools.partial(rollout_kernel, knots, steps[-1]),
        [(count, trajs, width), (count, trajs, nu), (1, trajs)],
        sent, got, after, init_state, prefix, kt,
    )
    return new_gains, feedforward, states, controls, decrease.reshape(trajs)


def solution(mesh):
    in_specs = (
        P("tm", "grp", None, None),
        P("tm", "grp", None, None),
        P("tm", "grp", None, None),
        P("tm", "grp", None),
        P("tm", "grp", None),
        P("tm", "grp", None),
        P(),
        P(),
        P("grp", None),
    )
    out_specs = (
        P("tm", "grp", None, None),
        P("tm", "grp", None),
        P("tm", "grp", None),
        P("tm", "grp", None),
        P("grp"),
    )
    return jax.shard_map(shards, mesh=mesh, in_specs=in_specs, out_specs=out_specs, check_vma=False)
```

time: 340 us -> 51.8 us (0.15)
  blocking collectives: 161 us -> 0 us
  other arithmetic: 92.6 us -> 0 us
  matrix products: 74.1 us -> 0 us
  Pallas kernels: 0 us -> 17.7 us
  starting transfers between devices: 0 us -> 14.8 us
  waiting for transfers between devices: 0 us -> 13.3 us
    all_gather x6 -> x0, blocking collectives: 124 us -> none  [carried_in(): gathered = jax.tree.map(lambda a: lax.all_gather(a, axis), part)]
    another operation x56 -> x0, other arithmetic: 88.1 us -> none  [the longest x32 48.2 us: spd_solve(): factor = jnp.linalg.cholesky(matrix)]
    dot_general x237 -> x0, matrix products: 70.7 us -> none  [product(): return jnp.matmul(left, right, precision=lax.Precision.HIGHEST)]
    psum x1 -> x0, blocking collectives: 37 us -> none  [shards(): decrease = lax.psum(jnp.sum(changes, 0), 'tm') / knots]
    pallas_call x0 -> x11, Pallas kernels: none -> 17.7 us  [call(): pl.pallas_call(body, out_shape=[jax.ShapeDtypeStruct(shape, F32) for shap...]
    ppermute x0 -> x8, starting transfers between devices: none -> 14.8 us  [exchange(): return lax.ppermute(value, 'tm', [(i, i ^ step) for i in range(devices)])]
    ppermute x0 -> x8, waiting for transfers between devices: none -> 13.3 us  [exchange(): return lax.ppermute(value, 'tm', [(i, i ^ step) for i in range(devices)])]
    another operation x16 -> x0, matrix products: 3.46 us -> none  [the longest x8 2.16 us: spd_solve(): inner = jax.scipy.linalg.solve_triangular(factor, right_side, lower=True)]
  transfers between devices with their start and end apart: 0 -> 8, of which waited for: 0 -> 8; matrix products, arithmetic and copies ran while one was open for 0% -> 0% of each run, Pallas kernels for 0% -> 4%
where the time goes in v1:
time: 51.8 us; the launch traced here: 51.4 us
  Pallas kernels  17.7 us (34%)
  starting transfers between devices  14.8 us (29%)
  waiting for transfers between devices  13.3 us (26%)
  local copies, waits for them, and re-layouts  4.81 us (9%)
  between operations  0.75 us (1%)
    pallas_call x11, Pallas kernels, call(): pl.pallas_call(body, out_shape=[jax.ShapeDtypeStruct(shape, F32) for shap...  17.7 us
    ppermute x8, starting transfers between devices, exchange(): return lax.ppermute(value, 'tm', [(i, i ^ step) for i in range(devices)])  14.8 us
    ppermute x8, waiting for transfers between devices, exchange(): return lax.ppermute(value, 'tm', [(i, i ^ step) for i in range(devices)])  13.3 us
    unnamed x23, local copies, waits for them, and re-layouts  4.81 us
  transfers between devices with their start and end apart: 8, of which 8 were waited for; matrix products, arithmetic and copies ran while one was open for 0% of the time, Pallas kernels for 4%

profile of v1, /device:TPU:0, one launch (start us, length us, event | category | flops | bytes accessed | tf_op | source)
XLA Modules:
  0.0 51.4 jit_solution(3154738972352412236)
XLA Ops:
  0.7 1.2 %copy.15.b_ref = f32[8,2,64,32]{3,2,1,0:T(8,128)S(1)} copy(f32[8,2,64,32]{2,3,1,0:T(8,128)} %param.10) | data formatting | bytes 262144 | tf_op args[1]
  1.9 0.7 %copy-done.2 = f32[32,32]{1,0:T(8,128)S(1)} copy-done((f32[32,32]{1,0:T(8,128)S(1)}, f32[32,32]{1,0:T(8,128)}, u32[]{:S(2)}) %copy-start.2) | copy-done | bytes 4120
  2.6 0.7 %copy-done.4 = f32[8,2,64]{2,1,0:T(2,128)S(1)} copy-done((f32[8,2,64]{2,1,0:T(2,128)S(1)}, f32[8,2,64]{2,1,0:T(2,128)}, u32[]{:S(2)}) %copy-start.4) | copy-done | bytes 4120
  3.3 0.7 %copy-done.6 = f32[8,2,32]{2,1,0:T(2,128)S(1)} copy-done((f32[8,2,32]{2,1,0:T(2,128)S(1)}, f32[8,2,32]{2,1,0:T(2,128)}, u32[]{:S(2)}) %copy-start.6) | copy-done | bytes 2072
  4.0 0.8 %copy-done.8 = f32[64,64]{1,0:T(8,128)S(1)} copy-done((f32[64,64]{1,0:T(8,128)S(1)}, f32[64,64]{1,0:T(8,128)}, u32[]{:S(2)}) %copy-start.8) | copy-done | bytes 16408
  4.8 0.7 %copy-done.9 = f32[8,2,64]{2,1,0:T(2,128)S(1)} copy-done((f32[8,2,64]{2,1,0:T(2,128)S(1)}, f32[8,2,64]{2,1,0:T(2,128)}, u32[]{:S(2)}) %copy-start.9) | copy-done | bytes 4120
  5.5 1.9 %shard_map.128 = (f32[2,72,128]{2,1,0:T(8,128)S(1)}, f32[8,2,72,128]{3,2,1,0:T(8,128)S(1)}, f32[72,128]{1,0:T(8,128)S(1)}) custom-call(f32[8,2,64,64]{3,2,1,0:T(8,128)S(1)} %copy-done, f32[8,2,64,32]{3,2,1,0:T(8,128)S(1)} %copy.15.b_ref, f32[8,2,32,64]{3,2,1,0:T(8,128)S(1)} %copy-done.1, f32[8,2,64]{2,1,0:T(2,128)S(1)} %copy-done.4, ...), custom_call_target="tpu_custom_call" | custom-call | tf_op jit(solution)/shard_map/pallas_call | solution.py:319
  7.9 0.9 %collective-permute-done.args_1_ = f32[2,72,128]{2,1,0:T(8,128)S(1)} collective-permute-done((f32[2,72,128]{2,1,0:T(8,128)S(1)}, f32[2,72,128]{2,1,0:T(8,128)S(1)}, u32[]{:S(2)}, u32[]{:S(2)}) %collective-permute-start) | collective-permute-done | bytes 73760 | tf_op jit(solution)/shard_map/ppermute | solution.py:343
  9.2 2.9 %collective-permute-start.1 = (f32[2,72,128]{2,1,0:T(8,128)S(1)}, f32[2,72,128]{2,1,0:T(8,128)S(1)}, u32[]{:S(2)}, u32[]{:S(2)}) collective-permute-start(f32[2,72,128]{2,1,0:T(8,128)S(1)} %get-tuple-element.30.own_ref), channel_id=1, source_target_pairs={{0,2},{1,3},{2,0},{3,1},{4,6},{5,7},{6,4},{7,5},{8,10},{9,11},{10,... | collective-permute-start | bytes 221192 | tf_op jit(solution)/shard_map/ppermute | solution.py:343
  12.1 2.6 %collective-permute-done.1.got_ref = f32[2,72,128]{2,1,0:T(8,128)S(1)} collective-permute-done((f32[2,72,128]{2,1,0:T(8,128)S(1)}, f32[2,72,128]{2,1,0:T(8,128)S(1)}, u32[]{:S(2)}, u32[]{:S(2)}) %collective-permute-start.1) | collective-permute-done | bytes 73760 | tf_op jit(solution)/shard_map/ppermute | solution.py:343
  15.2 1.9 %collective-permute-start.2 = (f32[2,72,128]{2,1,0:T(8,128)S(1)}, f32[2,72,128]{2,1,0:T(8,128)S(1)}, u32[]{:S(2)}, u32[]{:S(2)}) collective-permute-start(f32[2,72,128]{2,1,0:T(8,128)S(1)} %get-tuple-element.32.own_ref), channel_id=1, source_target_pairs={{0,4},{1,5},{2,6},{3,7},{4,0},{5,1},{6,2},{7,3},{8,12},{9,13},{10,... | collective-permute-start | bytes 221192 | tf_op jit(solution)/shard_map/ppermute | solution.py:343
  17.1 2.5 %collective-permute-done.2.got_ref = f32[2,72,128]{2,1,0:T(8,128)S(1)} collective-permute-done((f32[2,72,128]{2,1,0:T(8,128)S(1)}, f32[2,72,128]{2,1,0:T(8,128)S(1)}, u32[]{:S(2)}, u32[]{:S(2)}) %collective-permute-start.2) | collective-permute-done | bytes 73760 | tf_op jit(solution)/shard_map/ppermute | solution.py:343
  19.6 0.7 %shard_map.131 = (f32[72,128]{1,0:T(8,128)S(1)}, f32[2,72,128]{2,1,0:T(8,128)S(1)}) custom-call(f32[2,72,128]{2,1,0:T(8,128)S(1)} %get-tuple-element.32.own_ref, f32[2,72,128]{2,1,0:T(8,128)S(1)} %collective-permute-done.2.got_ref, f32[2,72,128]{2,1,0:T(8,128)S(1)} %get-tuple-element.33.seen_ref, f32[72,128]{1,0:T(8,128)S(1)} %get-tuple-element.28.term_ref), custom_call_target="tpu_custom_call" | custom-call | tf_op jit(solution)/shard_map/pallas_call | solution.py:319
  20.3 2.9 %collective-permute-start.3 = (f32[72,128]{1,0:T(8,128)S(1)}, f32[72,128]{1,0:T(8,128)S(1)}, u32[]{:S(2)}, u32[]{:S(2)}) collective-permute-start(f32[72,128]{1,0:T(8,128)S(1)} %get-tuple-element.34), channel_id=1, source_target_pairs={{0,8},{1,9},{2,10},{3,11},{4,12},{5,13},{6,14},{7,15},{8,0},{9,1},... | collective-permute-start | bytes 110600 | tf_op jit(solution)/shard_map/ppermute | solution.py:343
  23.3 1.5 %shard_map.132.suffix_ref = f32[7,2,72,128]{3,2,1,0:T(8,128)S(1)} custom-call(f32[8,2,72,128]{3,2,1,0:T(8,128)S(1)} %get-tuple-element.36.own_ref), custom_call_target="tpu_custom_call" | custom-call | tf_op jit(solution)/shard_map/pallas_call | solution.py:319
  25.3 10.2 %shard_map.133 = (f32[8,2,32,64]{3,2,1,0:T(8,128)}, f32[8,2,32]{2,1,0:T(2,128)}, f32[80,128]{1,0:T(8,128)S(1)}, f32[8,72,128]{2,1,0:T(8,128)S(1)}, f32[8,72,64]{2,1,0:T(8,128)S(1)}) custom-call(f32[8,2,64,64]{3,2,1,0:T(8,128)S(1)} %copy-done, f32[8,2,64,32]{3,2,1,0:T(8,128)S(1)} %copy.15.b_ref, f32[8,2,64]{2,1,0:T(2,128)S(1)} %copy-done.5, ...), custom_call_target="tpu_custom_call" | custom-call | tf_op jit(solution)/shard_map/pallas_call | solution.py:319
  35.4 1.2 %collective-permute-done.4.args_1_ = f32[80,128]{1,0:T(8,128)S(1)} collective-permute-done((f32[80,128]{1,0:T(8,128)S(1)}, f32[80,128]{1,0:T(8,128)S(1)}, u32[]{:S(2)}, u32[]{:S(2)}) %collective-permute-start.4) | collective-permute-done | bytes 40992 | tf_op jit(solution)/shard_map/ppermute | solution.py:343
  36.8 1.8 %collective-permute-start.5 = (f32[80,128]{1,0:T(8,128)S(1)}, f32[80,128]{1,0:T(8,128)S(1)}, u32[]{:S(2)}, u32[]{:S(2)}) collective-permute-start(f32[80,128]{1,0:T(8,128)S(1)} %get-tuple-element.40.own_ref), channel_id=1, source_target_pairs={{0,2},{1,3},{2,0},{3,1},{4,6},{5,7},{6,4},{7,5},{8,10},{9,11},{10,... | collective-permute-start | bytes 122888 | tf_op jit(solution)/shard_map/ppermute | solution.py:343
  38.7 2.2 %collective-permute-done.5.got_ref = f32[80,128]{1,0:T(8,128)S(1)} collective-permute-done((f32[80,128]{1,0:T(8,128)S(1)}, f32[80,128]{1,0:T(8,128)S(1)}, u32[]{:S(2)}, u32[]{:S(2)}) %collective-permute-start.5) | collective-permute-done | bytes 40992 | tf_op jit(solution)/shard_map/ppermute | solution.py:343
  41.1 1.9 %collective-permute-start.6 = (f32[80,128]{1,0:T(8,128)S(1)}, f32[80,128]{1,0:T(8,128)S(1)}, u32[]{:S(2)}, u32[]{:S(2)}) collective-permute-start(f32[80,128]{1,0:T(8,128)S(1)} %get-tuple-element.42.own_ref), channel_id=1, source_target_pairs={{0,4},{1,5},{2,6},{3,7},{4,0},{5,1},{6,2},{7,3},{8,12},{9,13},{10,... | collective-permute-start | bytes 122888 | tf_op jit(solution)/shard_map/ppermute | solution.py:343
  43.0 2.2 %collective-permute-done.6.got_ref = f32[80,128]{1,0:T(8,128)S(1)} collective-permute-done((f32[80,128]{1,0:T(8,128)S(1)}, f32[80,128]{1,0:T(8,128)S(1)}, u32[]{:S(2)}, u32[]{:S(2)}) %collective-permute-start.6) | collective-permute-done | bytes 40992 | tf_op jit(solution)/shard_map/ppermute | solution.py:343
  45.5 2.9 %collective-permute-start.7 = (f32[16,128]{1,0:T(8,128)S(1)}, f32[16,128]{1,0:T(8,128)S(1)}, u32[]{:S(2)}, u32[]{:S(2)}) collective-permute-start(f32[16,128]{1,0:T(8,128)S(1)} %get-tuple-element.44.own_ref), channel_id=1, source_target_pairs={{0,8},{1,9},{2,10},{3,11},{4,12},{5,13},{6,14},{7,15},{8,0},{9,1},... | collective-permute-start | bytes 24584 | tf_op jit(solution)/shard_map/ppermute | solution.py:343
  49.0 1.1 %collective-permute-done.7.got_ref = f32[16,128]{1,0:T(8,128)S(1)} collective-permute-done((f32[16,128]{1,0:T(8,128)S(1)}, f32[16,128]{1,0:T(8,128)S(1)}, u32[]{:S(2)}, u32[]{:S(2)}) %collective-permute-start.7) | collective-permute-done | bytes 8224 | tf_op jit(solution)/shard_map/ppermute | solution.py:343
  50.1 1.3 %shard_map.138 = (f32[8,2,64]{2,1,0:T(2,128)}, f32[8,2,32]{2,1,0:T(2,128)}, f32[1,2]{1,0:T(1,128)}) custom-call(f32[16,128]{1,0:T(8,128)S(1)} %get-tuple-element.44.own_ref, f32[16,128]{1,0:T(8,128)S(1)} %collective-permute-done.7.got_ref, f32[72,128]{1,0:T(8,128)S(1)} %get-tuple-element.45.seen_ref, f32[2,64]{1,0:T(2,128)S(1)} %copy-done.10, ...), custom_call_target="tpu_custom_call" | custom-call | tf_op jit(solution)/shard_map/pallas_call | solution.py:319
  (26 shorter events, 3.2 us)
Async XLA Ops:
  0.6 1.3 %copy-start = (f32[8,2,64,64]{3,2,1,0:T(8,128)S(1)}, f32[8,2,64,64]{3,2,1,0:T(8,128)}, u32[]{:S(2)}) copy-start(f32[8,2,64,64]{3,2,1,0:T(8,128)} %a_ref.3) | copy-start | bytes 786436
  0.6 1.3 %copy-start.1 = (f32[8,2,32,64]{3,2,1,0:T(8,128)S(1)}, f32[8,2,32,64]{3,2,1,0:T(8,128)}, u32[]{:S(2)}) copy-start(f32[8,2,32,64]{3,2,1,0:T(8,128)} %g_ref.1) | copy-start | bytes 393220
  1.9 0.7 %copy-start.2 = (f32[32,32]{1,0:T(8,128)S(1)}, f32[32,32]{1,0:T(8,128)}, u32[]{:S(2)}) copy-start(f32[32,32]{1,0:T(8,128)} %rf_ref.3) | copy-start | bytes 12292
  2.6 0.7 %copy-start.4 = (f32[8,2,64]{2,1,0:T(2,128)S(1)}, f32[8,2,64]{2,1,0:T(2,128)}, u32[]{:S(2)}) copy-start(f32[8,2,64]{2,1,0:T(2,128)} %d_ref.3) | copy-start | bytes 12292
  3.3 0.7 %copy-start.6 = (f32[8,2,32]{2,1,0:T(2,128)S(1)}, f32[8,2,32]{2,1,0:T(2,128)}, u32[]{:S(2)}) copy-start(f32[8,2,32]{2,1,0:T(2,128)} %cg_ref.3) | copy-start | bytes 6148
  4.0 0.8 %copy-start.8 = (f32[64,64]{1,0:T(8,128)S(1)}, f32[64,64]{1,0:T(8,128)}, u32[]{:S(2)}) copy-start(f32[64,64]{1,0:T(8,128)} %cf_ref.1) | copy-start | bytes 49156
  4.8 0.7 %copy-start.9 = (f32[8,2,64]{2,1,0:T(2,128)S(1)}, f32[8,2,64]{2,1,0:T(2,128)}, u32[]{:S(2)}) copy-start(f32[8,2,64]{2,1,0:T(2,128)} %sg_ref.1) | copy-start | bytes 12292
  7.4 1.4 %collective-permute-start = (f32[2,72,128]{2,1,0:T(8,128)S(1)}, f32[2,72,128]{2,1,0:T(8,128)S(1)}, u32[]{:S(2)}, u32[]{:S(2)}) collective-permute-start(f32[2,72,128]{2,1,0:T(8,128)S(1)} %get-tuple-element.29.args_0_), channel_id=1, source_target_pairs={{0,1},{1,0},{2,3},{3,2},{4,5},{5,4},{6,7},{7,6},{8,9},{9,8},{10,11... | collective-permute-start | bytes 221192 | tf_op jit(solution)/shard_map/ppermute | solution.py:343
  9.2 5.5 %collective-permute-start.1 = (f32[2,72,128]{2,1,0:T(8,128)S(1)}, f32[2,72,128]{2,1,0:T(8,128)S(1)}, u32[]{:S(2)}, u32[]{:S(2)}) collective-permute-start(f32[2,72,128]{2,1,0:T(8,128)S(1)} %get-tuple-element.30.own_ref), channel_id=1, source_target_pairs={{0,2},{1,3},{2,0},{3,1},{4,6},{5,7},{6,4},{7,5},{8,10},{9,11},{10,... | collective-permute-start | bytes 221192 | tf_op jit(solution)/shard_map/ppermute | solution.py:343
  15.2 4.4 %collective-permute-start.2 = (f32[2,72,128]{2,1,0:T(8,128)S(1)}, f32[2,72,128]{2,1,0:T(8,128)S(1)}, u32[]{:S(2)}, u32[]{:S(2)}) collective-permute-start(f32[2,72,128]{2,1,0:T(8,128)S(1)} %get-tuple-element.32.own_ref), channel_id=1, source_target_pairs={{0,4},{1,5},{2,6},{3,7},{4,0},{5,1},{6,2},{7,3},{8,12},{9,13},{10,... | collective-permute-start | bytes 221192 | tf_op jit(solution)/shard_map/ppermute | solution.py:343
  20.3 4.9 %collective-permute-start.3 = (f32[72,128]{1,0:T(8,128)S(1)}, f32[72,128]{1,0:T(8,128)S(1)}, u32[]{:S(2)}, u32[]{:S(2)}) collective-permute-start(f32[72,128]{1,0:T(8,128)S(1)} %get-tuple-element.34), channel_id=1, source_target_pairs={{0,8},{1,9},{2,10},{3,11},{4,12},{5,13},{6,14},{7,15},{8,0},{9,1},... | collective-permute-start | bytes 110600 | tf_op jit(solution)/shard_map/ppermute | solution.py:343
  23.2 2.0 %copy-start.3 = (f32[32,32]{1,0:T(8,128)S(1)}, f32[32,32]{1,0:T(8,128)}, u32[]{:S(2)}) copy-start(f32[32,32]{1,0:T(8,128)} %rf_ref.3) | copy-start | bytes 12292
  23.2 2.0 %copy-start.5 = (f32[8,2,64]{2,1,0:T(2,128)S(1)}, f32[8,2,64]{2,1,0:T(2,128)}, u32[]{:S(2)}) copy-start(f32[8,2,64]{2,1,0:T(2,128)} %d_ref.3) | copy-start | bytes 12292
  23.3 2.0 %copy-start.7 = (f32[8,2,32]{2,1,0:T(2,128)S(1)}, f32[8,2,32]{2,1,0:T(2,128)}, u32[]{:S(2)}) copy-start(f32[8,2,32]{2,1,0:T(2,128)} %cg_ref.3) | copy-start | bytes 6148
  35.4 1.2 %collective-permute-start.4 = (f32[80,128]{1,0:T(8,128)S(1)}, f32[80,128]{1,0:T(8,128)S(1)}, u32[]{:S(2)}, u32[]{:S(2)}) collective-permute-start(f32[80,128]{1,0:T(8,128)S(1)} %get-tuple-element.39.args_0_), channel_id=1, source_target_pairs={{0,1},{1,0},{2,3},{3,2},{4,5},{5,4},{6,7},{7,6},{8,9},{9,8},{10,11... | collective-permute-start | bytes 122888 | tf_op jit(solution)/shard_map/ppermute | solution.py:343
  36.8 4.1 %collective-permute-start.5 = (f32[80,128]{1,0:T(8,128)S(1)}, f32[80,128]{1,0:T(8,128)S(1)}, u32[]{:S(2)}, u32[]{:S(2)}) collective-permute-start(f32[80,128]{1,0:T(8,128)S(1)} %get-tuple-element.40.own_ref), channel_id=1, source_target_pairs={{0,2},{1,3},{2,0},{3,1},{4,6},{5,7},{6,4},{7,5},{8,10},{9,11},{10,... | collective-permute-start | bytes 122888 | tf_op jit(solution)/shard_map/ppermute | solution.py:343
  41.1 4.1 %copy-start.10 = (f32[2,64]{1,0:T(2,128)S(1)}, f32[2,64]{1,0:T(2,128)}, u32[]{:S(2)}) copy-start(f32[2,64]{1,0:T(2,128)} %init_ref.3) | copy-start | bytes 1540
  41.1 4.1 %collective-permute-start.6 = (f32[80,128]{1,0:T(8,128)S(1)}, f32[80,128]{1,0:T(8,128)S(1)}, u32[]{:S(2)}, u32[]{:S(2)}) collective-permute-start(f32[80,128]{1,0:T(8,128)S(1)} %get-tuple-element.42.own_ref), channel_id=1, source_target_pairs={{0,4},{1,5},{2,6},{3,7},{4,0},{5,1},{6,2},{7,3},{8,12},{9,13},{10,... | collective-permute-start | bytes 122888 | tf_op jit(solution)/shard_map/ppermute | solution.py:343
  45.5 4.6 %collective-permute-start.7 = (f32[16,128]{1,0:T(8,128)S(1)}, f32[16,128]{1,0:T(8,128)S(1)}, u32[]{:S(2)}, u32[]{:S(2)}) collective-permute-start(f32[16,128]{1,0:T(8,128)S(1)} %get-tuple-element.44.own_ref), channel_id=1, source_target_pairs={{0,8},{1,9},{2,10},{3,11},{4,12},{5,13},{6,14},{7,15},{8,0},{9,1},... | collective-permute-start | bytes 24584 | tf_op jit(solution)/shard_map/ppermute | solution.py:343

commit v2 on v1

v2 whole, which is shorter than its diff:
```python
import functools
import math

import jax
import jax.numpy as jnp
from jax import lax
from jax.experimental import pallas as pl
from jax.experimental.pallas import tpu as pltpu
from jax.sharding import PartitionSpec as P

F32 = jnp.float32
LANES = 128
VMEM = 60
TAIL = 8


def lane_block(shape, size):
    return lax.broadcasted_iota(jnp.int32, shape, 1) // size


def spread(pair, trajs):
    block = lane_block(pair.shape, pair.shape[1] // trajs)
    return jnp.concatenate([jnp.where(block == j, pair, 0.0) for j in range(trajs)], axis=0)


def split(x):
    high = x.astype(jnp.bfloat16)
    low = (x - high.astype(F32)).astype(jnp.bfloat16)
    return high, low


def left_of(x):
    return jnp.concatenate(split(x), axis=1)


def right_of(x, flip=False):
    depth, wide = (1, 0) if flip else (0, 1)
    both = jnp.concatenate(split(x), axis=wide)
    return jnp.concatenate([both, both], axis=depth)


def product_of(left, right, flip=False):
    dims = (((1,), (1 if flip else 0,)), ((), ()))
    w = lax.dot_general(left, right, dims, preferred_element_type=F32)
    full = w.shape[1] // 2
    return w[:, :full] + w[:, full:]


def prod(left, right, flip=False):
    wide = 0 if flip else 1
    columns = right.shape[wide]
    if columns % LANES:
        shape = list(right.shape)
        shape[wide] = -columns % LANES
        right = jnp.concatenate([right, jnp.zeros(shape, F32)], axis=wide)
    if left.shape[1] % LANES:
        rows, full = left.shape[0], right.shape[wide]
        dims = (((1,), (1 if flip else 0,)), ((), ()))
        w = lax.dot_general(
            jnp.concatenate(split(left), axis=0), jnp.concatenate(split(right), axis=wide), dims,
            preferred_element_type=F32,
        )
        w = w[:rows] + w[rows:]
        w = w[:, :full] + w[:, full:]
    else:
        w = product_of(left_of(left), right_of(right, flip), flip)
    return w[:, :columns]


def tail_of(row):
    shape = (TAIL, row.shape[1])
    return jnp.where(lax.broadcasted_iota(jnp.int32, shape, 0) == 0, jnp.broadcast_to(row, shape), 0.0)


def join(matrix, tail):
    return jnp.concatenate([matrix, tail], axis=0)


def apply_values(maps, later, trajs, width):
    ws = [prod(late, spread(x[:width], trajs), flip=True) for (x, _), late in zip(maps, later)]
    zs = [prod(x, spread(w[:width], trajs)) + y for (x, y), w in zip(maps, ws)]
    return [join(z[:width], z[width:] + w[width:]) for z, w in zip(zs, ws)]


def compose_states(pairs, trajs, width):
    zs = [prod(first, spread(second[:width], trajs)) for first, second in pairs]
    return [join(z[:width], z[width:] + second[width:]) for z, (_, second) in zip(zs, pairs)]


def compose_values(pairs, trajs, width):
    ws = [prod(second[1], spread(first[0][:width], trajs), flip=True) for first, second in pairs]
    xs = compose_states([(first[0], second[0]) for first, second in pairs], trajs, width)
    zs = [prod(first[0], spread(w[:width], trajs)) + first[1] for (first, _), w in zip(pairs, ws)]
    return [(x, join(z[:width], z[width:] + w[width:])) for x, z, w in zip(xs, zs, ws)]


def fold(items, joined):
    while len(items) > 1:
        rest = items[len(items) // 2 * 2 :]
        items = joined([(items[i], items[i + 1]) for i in range(0, len(items) - 1, 2)]) + rest
    return items[0]


def prefixes(items, joined):
    items, step = list(items), 1
    while step < len(items):
        items = items[:step] + joined([(items[i - step], items[i]) for i in range(step, len(items))])
        step *= 2
    return items


def identity_pair(width, trajs):
    rows = lax.broadcasted_iota(jnp.int32, (width, width * trajs), 0)
    lanes = lax.broadcasted_iota(jnp.int32, (width, width * trajs), 1)
    return jnp.where(rows == lanes % width, 1.0, 0.0)


def side_by_side(rows, trajs):
    return jnp.concatenate([rows[:, j] for j in range(trajs)], axis=1)


def term_of(cost_factor, trajs):
    width = cost_factor.shape[0]
    return prod(cost_factor, jnp.concatenate([cost_factor] * trajs, axis=0), flip=True) + identity_pair(width, trajs)


def paired(parts):
    return jnp.concatenate([parts[j] for j in range(parts.shape[0])], axis=1)


def block_kernel(knots, *refs):
    sources, (total_ref, *outs), held, kept, sems, out_sems = refs[:8], refs[8:13], refs[13:21], refs[21:25], *refs[25:]
    copies = [pltpu.make_async_copy(a, b, sems.at[i]) for i, (a, b) in enumerate(zip(sources, held))]
    order = (7, 2, 1, 6, 3, 4, 5, 0)
    for i in order:
        copies[i].start()
    leaving = [pltpu.make_async_copy(a, b, out_sems.at[i]) for i, (a, b) in enumerate(zip(kept, outs))]
    a_ref, bt_ref, g_ref, d_ref, sg_ref, cg_ref, cf_ref, rf_ref = held
    own_ref, term_ref, at_ref, btp_ref = kept
    count, trajs, nu, width = bt_ref.shape
    both = trajs * width
    scale = 1.0 / math.sqrt(knots)
    rows = lax.broadcasted_iota(jnp.int32, (nu, nu), 0)
    lanes = lax.broadcasted_iota(jnp.int32, (nu, nu), 1)
    for i in (7, 2, 1):
        copies[i].wait()
    root = jnp.concatenate([jnp.where(rows == lanes, 1.0, 0.0), rf_ref[...]], axis=1)
    root = spread(jnp.concatenate([root] * trajs, axis=1), trajs)
    pushed = []
    for t in range(count):
        gt = g_ref[t].reshape(trajs * nu, width).T
        btp = paired(bt_ref[t])
        btp_ref[t] = btp
        pushed.append(prod(gt, jnp.concatenate([spread(btp, trajs), root], axis=1)))
    leaving[3].start()
    for i in (6, 3, 4, 5):
        copies[i].wait()
    term = term_of(cf_ref[...], trajs)
    run_q = term / knots
    term_ref[...] = join(term, jnp.zeros((TAIL, both), F32))
    leaving[1].start()
    drift = side_by_side(d_ref[...], trajs) * scale
    grad = side_by_side(sg_ref[...], trajs) * scale
    cg = cg_ref[...]
    nothing = jnp.zeros((count, nu), F32)
    control = jnp.concatenate([piece for j in range(trajs) for piece in (cg[:, j], nothing)], axis=1)
    zs = [w[:, both:] for w in pushed]
    ys = [prod(join(z, tail_of(control[t : t + 1])), spread(z, trajs), flip=True) for t, z in enumerate(zs)]
    ys = [y + join(run_q, tail_of(grad[t : t + 1])) for t, y in enumerate(ys)]
    copies[0].wait()
    maps = []
    for t, (w, y) in enumerate(zip(pushed, ys)):
        at = a_ref[t].reshape(both, width).T
        at_ref[t] = at
        x = join(at + w[:, :both], tail_of(drift[t : t + 1]))
        own_ref[t, 0] = x
        own_ref[t, 1] = y
        maps.append((x, y))
    leaving[0].start()
    leaving[2].start()
    x, y = fold(maps, lambda pairs: compose_values(pairs, trajs, width))
    total_ref[0] = x
    total_ref[1] = y
    for copy in leaving:
        copy.wait()


def copy_kernel(source_ref, out_ref, sem):
    copy = pltpu.make_async_copy(source_ref, out_ref, sem)
    copy.start()
    copy.wait()


def suffix_kernel(own_ref, *refs, trajs, width):
    out_ref, count = refs[-1], own_ref.shape[0]
    maps = [(own_ref[t, 0], own_ref[t, 1]) for t in reversed(range(1, count))]
    done = prefixes(maps, lambda pairs: compose_values([(b, a) for a, b in pairs], trajs, width))
    for i, (x, y) in enumerate(done):
        out_ref[count - 2 - i, 0] = x
        out_ref[count - 2 - i, 1] = y


def reach_kernel(suffix_ref, seen_ref, left_ref, right_ref, y_ref, *, trajs, width):
    count = suffix_ref.shape[0] + 1
    seen = (seen_ref[0], seen_ref[1])
    maps = compose_values([((suffix_ref[t, 0], suffix_ref[t, 1]), seen) for t in range(count - 1)], trajs, width)
    for t, (x, y) in enumerate(maps + [seen]):
        left_ref[t] = left_of(join(x, jnp.zeros((left_ref.shape[1] - x.shape[0], x.shape[1]), F32)))
        right_ref[t] = right_of(spread(x[:width], trajs), flip=True)
        y_ref[t] = y


def prepare_kernel(
    knots, at_ref, btp_ref, d_ref, cg_ref, rf_ref, x_ref,
    value_ref, hess_ref, cross_ref, gain_ref, bd_ref, ad_ref, run_r_ref, control_ref, init_ref,
):
    count, nu, both = btp_ref.shape
    trajs, width = x_ref.shape
    stack = trajs * nu
    group = LANES // stack
    init_ref[...] = tail_of(jnp.concatenate([x_ref[j : j + 1] for j in range(trajs)], axis=1))
    drift = side_by_side(d_ref[...], trajs) * (1.0 / math.sqrt(knots))
    control_ref[...] = side_by_side(cg_ref[...], trajs).T
    rf = rf_ref[...]
    rows = lax.broadcasted_iota(jnp.int32, (nu, nu), 0)
    lanes = lax.broadcasted_iota(jnp.int32, (nu, nu), 1)
    run_r = prod(rf, rf, flip=True) + jnp.where(rows == lanes, 1.0, 0.0)
    run_r_ref[...] = jnp.concatenate([run_r] * (LANES // nu), axis=1)
    spare = jnp.zeros((value_ref.shape[1] - nu - TAIL, both), F32)
    bds = []
    for t in range(count):
        at, btp = at_ref[t], btp_ref[t]
        bd = spread(btp, trajs)
        bds.append(bd)
        tail = tail_of(drift[t : t + 1])
        value_ref[t] = left_of(jnp.concatenate([btp, tail, spare], axis=0))
        hess_ref[t] = right_of(
            jnp.concatenate([bd if i == t % group else jnp.zeros_like(bd) for i in range(group)], axis=0), flip=True
        )
        cross_ref[t] = right_of(jnp.concatenate([at, jnp.zeros((-width % LANES, both), F32)], axis=0), flip=True)
        bd_ref[t] = bd
        ad_ref[t] = join(at, tail)
        if len(bds) == group:
            gain_ref[t // group] = right_of(jnp.concatenate(bds, axis=0))
            bds = []


def upper(step):
    return lax.rem(lax.axis_index("tm") // step, 2) == 1


def value_step_kernel(step, own_ref, got_ref, seen_ref, *refs, trajs, width):
    total_ref, next_ref = refs[-2:]
    up = upper(step)
    own, got = (own_ref[0], own_ref[1]), (got_ref[0], got_ref[1])
    first = [jnp.where(up, g, o) for o, g in zip(own, got)]
    second = [jnp.where(up, o, g) for o, g in zip(own, got)]
    if seen_ref is None:
        seen = (join(identity_pair(width, trajs), jnp.zeros((TAIL, trajs * width), F32)), jnp.zeros_like(own[0]))
        (x, y), = compose_values([(first, second)], trajs, width)
        after = got
    else:
        seen = (seen_ref[0], seen_ref[1])
        (x, y), after = compose_values([(first, second), (seen, got)], trajs, width)
    total_ref[0] = x
    total_ref[1] = y
    next_ref[0] = jnp.where(up, seen[0], after[0])
    next_ref[1] = jnp.where(up, seen[1], after[1])


def value_last_kernel(step, own_ref, got_ref, seen_ref, term_ref, *refs, trajs, width):
    up = upper(step)
    own, got = (own_ref[0], own_ref[1]), (got_ref[0], got_ref[1])
    first = [jnp.where(up, g, o) for o, g in zip(own, got)]
    second = [jnp.where(up, o, g) for o, g in zip(own, got)]
    value_ref, next_ref = refs[-2:]
    seen, term = (seen_ref[0], seen_ref[1]), term_ref[...]
    total, (sx, sy) = compose_values([(first, second), (seen, got)], trajs, width)
    value_ref[...], = apply_values([total], [term], trajs, width)
    next_ref[0] = jnp.where(up, seen[0], sx)
    next_ref[1] = jnp.where(up, seen[1], sy)


def inverses(packs, size):
    block, step = 8, 4
    rows = lax.broadcasted_iota(jnp.int32, (block, LANES), 0)
    lanes = lax.broadcasted_iota(jnp.int32, (block, LANES), 1)
    inner = lanes % size
    first = lanes - inner
    packs = [[pack[i : i + block] for i in range(0, size, block)] for pack in packs]
    for k in range(0, size, step):
        at, r = k // block, k % block
        inside = (inner >= k) & (inner < k + step)
        for number, pack in enumerate(packs):
            columns = [[jnp.take_along_axis(x, first + (k + j), axis=1) for x in pack] for j in range(step)]
            p = [[columns[j][at][r + i : r + i + 1] for j in range(step)] for i in range(step)]
            z = [
                jnp.where(inside[:1], jnp.where(inner[:1] == k + i, 1.0, 0.0), pack[at][r + i : r + i + 1])
                for i in range(step)
            ]
            inverse = []
            for i in range(step):
                inverse.append(1.0 / p[i][i])
                for j in range(i + 1, step):
                    ratio = p[j][i] * inverse[i]
                    for c in range(i + 1, step):
                        p[j][c] = p[j][c] - ratio * p[i][c]
                    z[j] = z[j] - ratio * z[i]
            q = [None] * step
            for i in reversed(range(step)):
                v = z[i]
                for j in range(i + 1, step):
                    v = v - p[i][j] * q[j]
                q[i] = v * inverse[i]
            done = []
            for i, x in enumerate(pack):
                y = jnp.where(inside, 0.0, x)
                for j in range(step):
                    y = y - columns[j][i] * q[j]
                if i == at:
                    for j in range(step):
                        y = jnp.where(rows == r + j, q[j], y)
                done.append(y)
            packs[number] = done
    return [jnp.concatenate(pack, axis=0) for pack in packs]


def solve_kernel(
    step, term_ref, end_ref, left_ref, right_ref, y_ref,
    value_ref, hess_ref, cross_ref, gain_ref, bd_ref, ad_ref, run_r_ref, control_ref,
    total_ref, own_ref, system_ref, inverse_ref,
):
    count, stack, both = bd_ref.shape
    size = ad_ref.shape[1]
    width, nu = size - TAIL, run_r_ref.shape[0]
    trajs = both // width
    group = LANES // stack
    lin_lane = lax.broadcasted_iota(jnp.int32, (stack, LANES), 1) == width

    end = jnp.where(upper(step), term_ref[...], end_ref[...])
    end_left = left_of(end)
    ws = [product_of(end_left, right_ref[t], flip=True) for t in range(count)]
    zs = [product_of(left_ref[t], right_of(spread(w[:width], trajs)))[:size] + y_ref[t] for t, w in enumerate(ws)]
    values = [(z[:width], z[width : width + 1] + w[width : width + 1]) for z, w in zip(zs, ws)]

    us = [product_of(value_ref[t], right_of(spread(p, trajs))) for t, (p, _) in enumerate(values)]
    hesses = [product_of(left_of(u[:nu]), hess_ref[t], flip=True) for t, u in enumerate(us)]
    crosses = [product_of(left_of(spread(u[:nu], trajs)), cross_ref[t], flip=True) for t, u in enumerate(us)]
    hesses = [functools.reduce(jnp.add, hesses[t : t + group], run_r_ref[...]) for t in range(0, count, group)]
    systems, columns = [], []
    for t, (u, (_, vector)) in enumerate(zip(us, values)):
        lin = jnp.sum(bd_ref[t] * (vector + u[nu : nu + 1]), axis=1, keepdims=True) + control_ref[:, t : t + 1]
        systems.append(jnp.where(lin_lane, lin, crosses[t]))
        columns.append(lin)

    packs = inverses(hesses, nu)
    lanes = lax.broadcasted_iota(jnp.int32, (1, LANES), 1)
    flats = [jnp.concatenate(systems[t : t + group], axis=0).T[:size] for t in range(0, count, group)]
    solved = [product_of(left_of(spread(pack, LANES // nu)), gain_ref[g]) for g, pack in enumerate(packs)]
    maps = []
    for g, flat in enumerate(flats):
        left = left_of(flat)
        for i in range(group):
            mine = solved[g][i * stack : (i + 1) * stack]
            pieces = [mine if k == i else jnp.zeros_like(mine) for k in range(group)]
            maps.append(ad_ref[g * group + i] - product_of(left, right_of(jnp.concatenate(pieces, axis=0))))
    total_ref[:size] = fold(maps, lambda pairs: compose_states(pairs, trajs, width))
    for t, m in enumerate(maps):
        own_ref[t] = m

    decrease = jnp.zeros((1, LANES), F32)
    for g, (pack, flat) in enumerate(zip(packs, flats)):
        inverse_ref[g] = pack
        system_ref[g] = flat
        linear = jnp.zeros((nu, LANES), F32)
        for i in range(group):
            for j in range(trajs):
                at = i * trajs + j
                column = columns[g * group + i][j * nu : (j + 1) * nu]
                linear = jnp.where((lanes >= at * nu) & (lanes < (at + 1) * nu), column, linear)
        feed = -jnp.sum(linear * pack, axis=0, keepdims=True)
        feed_columns = jnp.broadcast_to(feed, (TAIL, LANES)).T
        weights = jnp.zeros((nu, LANES), F32)
        for at in range(LANES // nu):
            column = feed_columns[at * nu : (at + 1) * nu, :1]
            weights = jnp.where((lanes >= at * nu) & (lanes < (at + 1) * nu), column, weights)
        pushed = jnp.sum(weights * hesses[g], axis=0, keepdims=True)
        decrease = decrease + feed * flat[width : width + 1] + 0.5 * (feed * pushed)
    total_ref[size:] = tail_of(decrease)


def expand_kernel(
    own_ref, system_ref, inverse_ref, gain_ref, feed_ref, map_ref, *, trajs, width
):
    count, size, both = own_ref.shape
    groups, nu, _ = inverse_ref.shape
    group, stack = count // groups, trajs * nu
    gains = []
    kts = [-prod(system_ref[g], spread(inverse_ref[g], LANES // nu)) for g in range(groups)]
    for g, kt in enumerate(kts):
        spare = jnp.zeros((LANES - size, LANES), F32)
        natural = join(kt, spare).T
        for i in range(group):
            t = g * group + i
            gain_ref[t] = natural[i * stack : (i + 1) * stack, :width].reshape(trajs, nu, width)
            for j in range(trajs):
                at = i * stack + j * nu
                feed_ref[t : t + 1, j] = kt[width : width + 1, at : at + nu]
            gains.append(kt[:, i * stack : (i + 1) * stack])
    maps = [own_ref[t] for t in range(count - 1)]
    done = prefixes(maps, lambda pairs: compose_states(pairs, trajs, width))
    start = join(identity_pair(width, trajs), jnp.zeros((TAIL, both), F32))
    controls = [prod(m, spread(kt[:width], trajs)) for m, kt in zip(done, gains[1:])]
    controls = [join(u[:width], u[width:] + kt[width:]) for u, kt in zip(controls, gains[1:])]
    for t, (m, control) in enumerate(zip([start] + done, gains[:1] + controls)):
        map_ref[t] = jnp.concatenate([m, control, jnp.zeros((size, -stack % LANES), F32)], axis=1)


def reach_state_kernel(map_ref, seen_ref, out_ref, offset_ref, *, trajs, width, nu):
    seen = seen_ref[...]
    rows = jnp.concatenate([seen[:, j * width : (j + 1) * width] for j in range(trajs)], axis=0)
    size, both = seen.shape
    tails = map_ref[:, width:]
    products = [prod(rows, map_ref[t, :width]) for t in range(map_ref.shape[0])]
    for t, w in enumerate(products):
        lane = lax.broadcasted_iota(jnp.int32, (size, w.shape[1]), 1)
        owner = jnp.where(lane < both, lane // width, (lane - both) // nu)
        full = w[:size]
        for j in range(1, trajs):
            full = jnp.where(owner >= j, w[j * size : (j + 1) * size], full)
        out_ref[t] = jnp.concatenate(split(full[:width]), axis=1)
        offset_ref[t] = full[width:] + tails[t]


def state_step_kernel(step, own_ref, got_ref, seen_ref, total_ref, next_ref, *, trajs, width):
    up = upper(step)
    size = width + TAIL
    own, got = own_ref[:size], got_ref[:size]
    total_ref[size:] = own_ref[size:] + got_ref[size:]
    pair = (jnp.where(up, got, own), jnp.where(up, own, got))
    if seen_ref is None:
        seen = join(identity_pair(width, trajs), jnp.zeros((TAIL, trajs * width), F32))
        total_ref[:size], = compose_states([pair], trajs, width)
        after = got
    else:
        seen = seen_ref[...]
        total_ref[:size], after = compose_states([pair, (got, seen)], trajs, width)
    next_ref[...] = jnp.where(up, after, seen)


def state_last_kernel(step, own_ref, got_ref, seen_ref, init_ref, *refs, trajs, width):
    sent_ref, next_ref = refs[-2:]
    up = upper(step)
    size = width + TAIL
    own, got = own_ref[:size], got_ref[:size]
    seen = seen_ref[...]
    pair = (jnp.where(up, got, own), jnp.where(up, own, got))
    total, after = compose_states([pair, (got, seen)], trajs, width)
    sent_ref[:TAIL] = prod(init_ref[...], spread(total[:width], trajs)) + total[width:]
    sent_ref[TAIL:] = own_ref[size:] + got_ref[size:]
    next_ref[...] = jnp.where(up, after, seen)


def rows_times(row, right, trajs):
    width = right.shape[0]
    rows = jnp.concatenate([row[:1, j * width : (j + 1) * width] for j in range(trajs)], axis=0)
    left = jnp.concatenate(split(rows), axis=0)
    w = lax.dot_general(left, right, (((1,), (0,)), ((), ())), preferred_element_type=F32)
    w = w[:trajs] + w[trajs:]
    full = w.shape[1] // 2
    return w[:, :full] + w[:, full:]


def rollout_kernel(knots, step, own_ref, got_ref, init_ref, map_ref, offset_ref,
                   state_ref, control_ref, decrease_ref):
    count, trajs, width = state_ref.shape
    nu = control_ref.shape[2]
    both = trajs * width
    start = jnp.where(upper(step), got_ref[:1], init_ref[:1])
    for t in range(count):
        w = rows_times(start, map_ref[t], trajs) + offset_ref[t, :1]
        for j in range(trajs):
            state_ref[t : t + 1, j] = w[j : j + 1, j * width : (j + 1) * width]
            control_ref[t : t + 1, j] = w[j : j + 1, both + j * nu : both + (j + 1) * nu]
    sums = (own_ref[TAIL : TAIL + 1] + got_ref[TAIL : TAIL + 1]) / knots
    lane = lax.broadcasted_iota(jnp.int32, sums.shape, 1) // nu % trajs
    for j in range(trajs):
        decrease_ref[:, j : j + 1] = jnp.sum(jnp.where(lane == j, sums, 0.0), axis=1, keepdims=True)


def call(body, outs, *args, vmem=32, **named):
    return pl.pallas_call(
        body,
        out_shape=[
            jax.ShapeDtypeStruct(shape, F32) if isinstance(shape, tuple) else shape for shape in outs
        ],
        compiler_params=pltpu.CompilerParams(vmem_limit_bytes=vmem * 1024 * 1024),
        **named,
    )(*args)


def halves(*shape):
    return jax.ShapeDtypeStruct(shape, jnp.bfloat16)


def without(body, at):
    @functools.wraps(body)
    def inner(*refs, **named):
        return body(*refs[:at], None, *refs[at:], **named)

    return inner


def unread(wanted, *values):
    return values if wanted else ()


def shards(dyn_a, dyn_b, gains, defects, state_grad, control_grad, cost_factor, control_factor, init_state):
    count, trajs, width, nu = dyn_b.shape
    devices = lax.axis_size("tm")
    knots = count * devices
    both, size = trajs * width, width + TAIL
    sizes = dict(trajs=trajs, width=width)
    steps = [1 << i for i in range(devices.bit_length() - 1)]

    def exchange(value, step):
        return lax.ppermute(value, "tm", [(i, i ^ step) for i in range(devices)])

    stack = trajs * nu
    groups, up16 = count * stack // LANES, lambda n: -(-n // 16) * 16
    bt = jnp.swapaxes(dyn_b, 2, 3)
    inputs = (dyn_a, bt, gains, defects, state_grad, control_grad, cost_factor, control_factor)
    outs = [(2, size, both), (count, 2, size, both), (size, both), (count, width, both), (count, nu, both)]
    total, own, term, at, btp = call(
        functools.partial(block_kernel, knots), outs, *inputs,
        vmem=VMEM,
        in_specs=[pl.BlockSpec(memory_space=pl.ANY)] * len(inputs),
        out_specs=[pl.BlockSpec(memory_space=pltpu.VMEM)] + [pl.BlockSpec(memory_space=pl.ANY)] * 4,
        scratch_shapes=[pltpu.VMEM(x.shape, F32) for x in inputs] + [pltpu.VMEM(shape, F32) for shape in outs[1:]]
        + [pltpu.SemaphoreType.DMA((len(inputs),)), pltpu.SemaphoreType.DMA((4,))],
    )
    suffix, = call(functools.partial(suffix_kernel, **sizes), [(count - 1, 2, size, both)], own)
    *ready, init = call(
        functools.partial(prepare_kernel, knots),
        [halves(count, up16(nu + TAIL), 2 * both), halves(count, 2 * LANES, 2 * both),
         halves(count, 2 * LANES, 2 * both), halves(groups, 2 * LANES, 2 * both), (count, stack, both),
         (count, size, both), (nu, LANES), (stack, count), (TAIL, both)],
        at, btp, defects, control_grad, control_factor, init_state,
    )
    got = exchange(total, steps[0])
    total, = call(
        copy_kernel, [(2, size, both)], total,
        in_specs=[pl.BlockSpec(memory_space=pl.ANY)], scratch_shapes=[pltpu.SemaphoreType.DMA],
    )
    total, after = call(
        functools.partial(without(value_step_kernel, 3), steps[0], **sizes), [(2, size, both)] * 2, total, got
    )
    for i, step in enumerate(steps[1:-2]):
        got = exchange(total, step)
        total, after = call(
            functools.partial(value_step_kernel, step, **sizes), [(2, size, both)] * 2,
            total, got, after, *unread(i == 0, init),
        )
    got = exchange(total, steps[-2])
    value, after = call(
        functools.partial(value_last_kernel, steps[-2], **sizes),
        [(size, both), (2, size, both)], total, got, after, term, suffix,
    )
    reach = call(
        functools.partial(reach_kernel, **sizes),
        [halves(count, up16(size), 2 * both), halves(count, 2 * both, 2 * both), (count, size, both)], suffix, after,
    )
    value = exchange(value, steps[-1])
    total, own, system, inverse = call(
        functools.partial(solve_kernel, steps[-1]),
        [(size + TAIL, both), (count, size, both), (groups, size, LANES), (groups, nu, LANES)],
        term, value, *reach, *ready,
    )
    wide = both + -(-stack // LANES) * LANES
    new_gains, feedforward, maps = call(
        functools.partial(expand_kernel, **sizes),
        [(count, trajs, nu, width), (count, trajs, nu), (count, size, wide)], own, system, inverse,
    )
    seen = []
    for step in steps[:-2]:
        body = state_step_kernel if seen else without(state_step_kernel, 3)
        got = exchange(total, step)
        total, after = call(
            functools.partial(body, step, **sizes), [(size + TAIL, both), (size, both)], total, got, *seen
        )
        seen = [after]
    got = exchange(total, steps[-2])
    sent, after = call(
        functools.partial(state_last_kernel, steps[-2], **sizes),
        [(2 * TAIL, both), (size, both)], total, got, *seen, init, maps,
    )
    maps, offsets = call(
        functools.partial(reach_state_kernel, **sizes, nu=nu),
        [halves(count, width, 2 * wide), (count, TAIL, wide)], maps, after,
    )
    got = exchange(sent, steps[-1])
    states, controls, decrease = call(
        functools.partial(rollout_kernel, knots, steps[-1]),
        [(count, trajs, width), (count, trajs, nu), (1, trajs)],
        sent, got, init, maps, offsets,
    )
    return new_gains, feedforward, states, controls, decrease.reshape(trajs)


def solution(mesh):
    in_specs = (
        P("tm", "grp", None, None),
        P("tm", "grp", None, None),
        P("tm", "grp", None, None),
        P("tm", "grp", None),
        P("tm", "grp", None),
        P("tm", "grp", None),
        P(),
        P(),
        P("grp", None),
    )
    out_specs = (
        P("tm", "grp", None, None),
        P("tm", "grp", None),
        P("tm", "grp", None),
        P("tm", "grp", None),
        P("grp"),
    )
    return jax.shard_map(shards, mesh=mesh, in_specs=in_specs, out_specs=out_specs, check_vma=False)
```

time: 51.8 us -> 42.1 us (0.81)
  waiting for transfers between devices: 13.3 us -> 8.33 us
  Pallas kernels: 17.7 us -> 15.2 us
  local copies, waits for them, and re-layouts: 4.81 us -> 2.76 us
    ppermute x8, waiting for transfers between devices: 13.3 us -> 8.33 us  [exchange(): return lax.ppermute(value, 'tm', [(i, i ^ step) for i in range(devices)])]
    pallas_call x11 -> x15, Pallas kernels: 17.7 us -> 15.2 us  [call(): pl.pallas_call(body, out_shape=[jax.ShapeDtypeStruct(shape, F32) if isins...]
    unnamed x23 -> x18, local copies, waits for them, and re-layouts: 4.81 us -> 2.76 us
  transfers between devices with their start and end apart: 8 -> 8, of which waited for: 8 -> 8; matrix products, arithmetic and copies ran while one was open for 0% -> 0% of each run, Pallas kernels for 4% -> 11%
where the time goes in v2:
time: 42.1 us; the launch traced here: 41.9 us
  Pallas kernels  15.2 us (36%)
  starting transfers between devices  14.9 us (35%)
  waiting for transfers between devices  8.33 us (20%)
  local copies, waits for them, and re-layouts  2.76 us (7%)
  between operations  0.78 us (2%)
    pallas_call x15, Pallas kernels, call(): pl.pallas_call(body, out_shape=[jax.ShapeDtypeStruct(shape, F32) if isins...  15.2 us
    ppermute x8, starting transfers between devices, exchange(): return lax.ppermute(value, 'tm', [(i, i ^ step) for i in range(devices)])  14.9 us
    ppermute x8, waiting for transfers between devices, exchange(): return lax.ppermute(value, 'tm', [(i, i ^ step) for i in range(devices)])  8.33 us
    unnamed x18, local copies, waits for them, and re-layouts  2.76 us
  transfers between devices with their start and end apart: 8, of which 8 were waited for; matrix products, arithmetic and copies ran while one was open for 0% of the time, Pallas kernels for 11%

profile of v2, /device:TPU:0, one launch (start us, length us, event | category | flops | bytes accessed | tf_op | source)
XLA Modules:
  0.0 41.9 jit_solution(11045840688743920953)
XLA Ops:
  0.7 4.2 %shard_map.128 = (f32[2,72,128]{2,1,0:T(8,128)}, f32[8,2,72,128]{3,2,1,0:T(8,128)}, f32[72,128]{1,0:T(8,128)}, f32[8,64,128]{2,1,0:T(8,128)}, f32[8,32,128]{2,1,0:T(8,128)}) custom-call(f32[8,2,64,64]{3,2,1,0:T(8,128)} %refs_0_.1, f32[8,2,32,64]{3,2,1,0:T(8,128)} %bitcast.2, f32[8,2,32,64]{3,2,1,0:T(8,128)} %refs_2_.1, f32[8,2,64]{2,1,0:T(2,128)} %d_ref.1, ...), custom_call_target="tpu_custom_call" | custom-call | tf_op jit(solution)/shard_map/pallas_call | solution.py:492
  4.9 0.5 %collective-permute-start = (f32[2,72,128]{2,1,0:T(8,128)}, f32[2,72,128]{2,1,0:T(8,128)S(1)}, u32[]{:S(2)}, u32[]{:S(2)}) collective-permute-start(f32[2,72,128]{2,1,0:T(8,128)} %get-tuple-element.47.source_ref), channel_id=1, source_target_pairs={{0,1},{1,0},{2,3},{3,2},{4,5},{5,4},{6,7},{7,6},{8,9},{9,8},{10,11... | collective-permute-start | bytes 221192 | tf_op jit(solution)/shard_map/ppermute | solution.py:527
  5.4 0.9 %copy-done.4 = f32[2,72,128]{2,1,0:T(8,128)S(1)} copy-done((f32[2,72,128]{2,1,0:T(8,128)S(1)}, f32[2,72,128]{2,1,0:T(8,128)}, u32[]{:S(2)}) %copy-start.4) | copy-done | bytes 73752
  6.9 2.9 %collective-permute-start.1 = (f32[2,72,128]{2,1,0:T(8,128)S(1)}, f32[2,72,128]{2,1,0:T(8,128)S(1)}, u32[]{:S(2)}, u32[]{:S(2)}) collective-permute-start(f32[2,72,128]{2,1,0:T(8,128)S(1)} %get-tuple-element.48.own_ref), channel_id=1, source_target_pairs={{0,2},{1,3},{2,0},{3,1},{4,6},{5,7},{6,4},{7,5},{8,10},{9,11},{10,... | collective-permute-start | bytes 221192 | tf_op jit(solution)/shard_map/ppermute | solution.py:527
  9.8 0.9 %copy-done.1 = f32[8,64,128]{2,1,0:T(8,128)S(1)} copy-done((f32[8,64,128]{2,1,0:T(8,128)S(1)}, f32[8,64,128]{2,1,0:T(8,128)}, u32[]{:S(2)}) %copy-start.1) | copy-done | bytes 262168
  10.8 0.9 %copy-done.3 = f32[8,32,128]{2,1,0:T(8,128)S(1)} copy-done((f32[8,32,128]{2,1,0:T(8,128)S(1)}, f32[8,32,128]{2,1,0:T(8,128)}, u32[]{:S(2)}) %copy-start.3) | copy-done | bytes 131096
  12.8 1.9 %collective-permute-start.2 = (f32[2,72,128]{2,1,0:T(8,128)S(1)}, f32[2,72,128]{2,1,0:T(8,128)S(1)}, u32[]{:S(2)}, u32[]{:S(2)}) collective-permute-start(f32[2,72,128]{2,1,0:T(8,128)S(1)} %get-tuple-element.53.own_ref), channel_id=1, source_target_pairs={{0,4},{1,5},{2,6},{3,7},{4,0},{5,1},{6,2},{7,3},{8,12},{9,13},{10,... | collective-permute-start | bytes 221192 | tf_op jit(solution)/shard_map/ppermute | solution.py:527
  14.7 1.4 %shard_map.133.refs_0_.suffix_ref = f32[7,2,72,128]{3,2,1,0:T(8,128)S(1)} custom-call(f32[8,2,72,128]{3,2,1,0:T(8,128)S(1)} %copy-done), custom_call_target="tpu_custom_call" | custom-call | tf_op jit(solution)/shard_map/pallas_call | solution.py:492
  16.1 1.1 %collective-permute-done.2.got_ref = f32[2,72,128]{2,1,0:T(8,128)S(1)} collective-permute-done((f32[2,72,128]{2,1,0:T(8,128)S(1)}, f32[2,72,128]{2,1,0:T(8,128)S(1)}, u32[]{:S(2)}, u32[]{:S(2)}) %collective-permute-start.2) | collective-permute-done | bytes 73760 | tf_op jit(solution)/shard_map/ppermute | solution.py:527
  17.2 0.6 %shard_map.134 = (f32[72,128]{1,0:T(8,128)S(1)}, f32[2,72,128]{2,1,0:T(8,128)S(1)}) custom-call(f32[2,72,128]{2,1,0:T(8,128)S(1)} %get-tuple-element.53.own_ref, f32[2,72,128]{2,1,0:T(8,128)S(1)} %collective-permute-done.2.got_ref, f32[2,72,128]{2,1,0:T(8,128)S(1)} %get-tuple-element.54.seen_ref, f32[72,128]{1,0:T(8,128)S(1)} %copy-done.2, ...), custom_call_target="tpu_custom_call" | custom-call | tf_op jit(solution)/shard_map/pallas_call | solution.py:492
  17.9 2.9 %collective-permute-start.3 = (f32[72,128]{1,0:T(8,128)S(1)}, f32[72,128]{1,0:T(8,128)S(1)}, u32[]{:S(2)}, u32[]{:S(2)}) collective-permute-start(f32[72,128]{1,0:T(8,128)S(1)} %get-tuple-element.56), channel_id=1, source_target_pairs={{0,8},{1,9},{2,10},{3,11},{4,12},{5,13},{6,14},{7,15},{8,0},{9,1},... | collective-permute-start | bytes 110600 | tf_op jit(solution)/shard_map/ppermute | solution.py:527
  20.8 0.7 %shard_map.135 = (bf16[8,80,256]{2,1,0:T(8,128)(2,1)S(1)}, bf16[8,256,256]{2,1,0:T(8,128)(2,1)S(1)}, f32[8,72,128]{2,1,0:T(8,128)S(1)}) custom-call(f32[7,2,72,128]{3,2,1,0:T(8,128)S(1)} %shard_map.133.refs_0_.suffix_ref, f32[2,72,128]{2,1,0:T(8,128)S(1)} %get-tuple-element.57.seen_ref), custom_call_target="tpu_custom_call" | custom-call | tf_op jit(solution)/shard_map/pallas_call | solution.py:492
  21.5 1.3 %collective-permute-done.3.end_ref = f32[72,128]{1,0:T(8,128)S(1)} collective-permute-done((f32[72,128]{1,0:T(8,128)S(1)}, f32[72,128]{1,0:T(8,128)S(1)}, u32[]{:S(2)}, u32[]{:S(2)}) %collective-permute-start.3) | collective-permute-done | bytes 36896 | tf_op jit(solution)/shard_map/ppermute | solution.py:527
  22.8 3.5 %shard_map.136 = (f32[80,128]{1,0:T(8,128)S(1)}, f32[8,72,128]{2,1,0:T(8,128)S(1)}, f32[4,72,128]{2,1,0:T(8,128)S(1)}, f32[4,32,128]{2,1,0:T(8,128)S(1)}) custom-call(f32[72,128]{1,0:T(8,128)S(1)} %copy-done.2, f32[72,128]{1,0:T(8,128)S(1)} %collective-permute-done.3.end_ref, bf16[8,80,256]{2,1,0:T(8,128)(2,1)S(1)} %get-tuple-element.58.left_ref, ...), custom_call_target="tpu_custom_call" | custom-call | tf_op jit(solution)/shard_map/pallas_call | solution.py:492
  26.4 1.2 %collective-permute-done.4.args_1_ = f32[80,128]{1,0:T(8,128)S(1)} collective-permute-done((f32[80,128]{1,0:T(8,128)S(1)}, f32[80,128]{1,0:T(8,128)S(1)}, u32[]{:S(2)}, u32[]{:S(2)}) %collective-permute-start.4) | collective-permute-done | bytes 40992 | tf_op jit(solution)/shard_map/ppermute | solution.py:527
  27.8 1.8 %collective-permute-start.5 = (f32[80,128]{1,0:T(8,128)S(1)}, f32[80,128]{1,0:T(8,128)S(1)}, u32[]{:S(2)}, u32[]{:S(2)}) collective-permute-start(f32[80,128]{1,0:T(8,128)S(1)} %get-tuple-element.75.own_ref), channel_id=1, source_target_pairs={{0,2},{1,3},{2,0},{3,1},{4,6},{5,7},{6,4},{7,5},{8,10},{9,11},{10,... | collective-permute-start | bytes 122888 | tf_op jit(solution)/shard_map/ppermute | solution.py:527
  29.6 2.2 %collective-permute-done.5.got_ref = f32[80,128]{1,0:T(8,128)S(1)} collective-permute-done((f32[80,128]{1,0:T(8,128)S(1)}, f32[80,128]{1,0:T(8,128)S(1)}, u32[]{:S(2)}, u32[]{:S(2)}) %collective-permute-start.5) | collective-permute-done | bytes 40992 | tf_op jit(solution)/shard_map/ppermute | solution.py:527
  32.0 1.9 %collective-permute-start.6 = (f32[80,128]{1,0:T(8,128)S(1)}, f32[80,128]{1,0:T(8,128)S(1)}, u32[]{:S(2)}, u32[]{:S(2)}) collective-permute-start(f32[80,128]{1,0:T(8,128)S(1)} %get-tuple-element.77.own_ref), channel_id=1, source_target_pairs={{0,4},{1,5},{2,6},{3,7},{4,0},{5,1},{6,2},{7,3},{8,12},{9,13},{10,... | collective-permute-start | bytes 122888 | tf_op jit(solution)/shard_map/ppermute | solution.py:527
  33.9 1.2 %shard_map.137 = (f32[8,2,32,64]{3,2,1,0:T(8,128)}, f32[8,2,32]{2,1,0:T(2,128)}, f32[8,72,256]{2,1,0:T(8,128)S(1)}) custom-call(f32[8,72,128]{2,1,0:T(8,128)S(1)} %get-tuple-element.69.own_ref, f32[4,72,128]{2,1,0:T(8,128)S(1)} %get-tuple-element.70.system_ref, f32[4,32,128]{2,1,0:T(8,128)S(1)} %get-tuple-element.71.inverse_ref), custom_call_target="tpu_custom_call" | custom-call | tf_op jit(solution)/shard_map/pallas_call | solution.py:492
  35.1 1.0 %collective-permute-done.6.got_ref = f32[80,128]{1,0:T(8,128)S(1)} collective-permute-done((f32[80,128]{1,0:T(8,128)S(1)}, f32[80,128]{1,0:T(8,128)S(1)}, u32[]{:S(2)}, u32[]{:S(2)}) %collective-permute-start.6) | collective-permute-done | bytes 40992 | tf_op jit(solution)/shard_map/ppermute | solution.py:527
  36.4 2.9 %collective-permute-start.7 = (f32[16,128]{1,0:T(8,128)S(1)}, f32[16,128]{1,0:T(8,128)S(1)}, u32[]{:S(2)}, u32[]{:S(2)}) collective-permute-start(f32[16,128]{1,0:T(8,128)S(1)} %get-tuple-element.80.own_ref), channel_id=1, source_target_pairs={{0,8},{1,9},{2,10},{3,11},{4,12},{5,13},{6,14},{7,15},{8,0},{9,1},... | collective-permute-start | bytes 24584 | tf_op jit(solution)/shard_map/ppermute | solution.py:527
  39.3 0.8 %shard_map.141 = (bf16[8,64,512]{2,1,0:T(8,128)(2,1)S(1)}, f32[8,8,256]{2,1,0:T(8,128)S(1)}) custom-call(f32[8,72,256]{2,1,0:T(8,128)S(1)} %get-tuple-element.79.refs_0_.map_ref, f32[72,128]{1,0:T(8,128)S(1)} %get-tuple-element.81.seen_ref), custom_call_target="tpu_custom_call" | custom-call | tf_op jit(solution)/shard_map/pallas_call | solution.py:492
  40.1 0.9 %collective-permute-done.7.got_ref = f32[16,128]{1,0:T(8,128)S(1)} collective-permute-done((f32[16,128]{1,0:T(8,128)S(1)}, f32[16,128]{1,0:T(8,128)S(1)}, u32[]{:S(2)}, u32[]{:S(2)}) %collective-permute-start.7) | collective-permute-done | bytes 8224 | tf_op jit(solution)/shard_map/ppermute | solution.py:527
  41.0 0.9 %shard_map.142 = (f32[8,2,64]{2,1,0:T(2,128)}, f32[8,2,32]{2,1,0:T(2,128)}, f32[1,2]{1,0:T(1,128)}) custom-call(f32[16,128]{1,0:T(8,128)S(1)} %get-tuple-element.80.own_ref, f32[16,128]{1,0:T(8,128)S(1)} %collective-permute-done.7.got_ref, f32[8,128]{1,0:T(8,128)S(1)} %get-tuple-element.52.refs_0_.init_ref, ...), custom_call_target="tpu_custom_call" | custom-call | tf_op jit(solution)/shard_map/pallas_call | solution.py:492
  (25 shorter events, 2.5 us)
Async XLA Ops:
  0.6 9.2 %copy-start.5 = (f32[32,32]{1,0:T(8,128)S(1)}, f32[32,32]{1,0:T(8,128)}, u32[]{:S(2)}) copy-start(f32[32,32]{1,0:T(8,128)} %rf_ref.1) | copy-start | bytes 12292
  0.6 9.2 %copy-start.6 = (f32[8,2,64]{2,1,0:T(2,128)S(1)}, f32[8,2,64]{2,1,0:T(2,128)}, u32[]{:S(2)}) copy-start(f32[8,2,64]{2,1,0:T(2,128)} %d_ref.1) | copy-start | bytes 12292
  0.7 9.2 %copy-start.7 = (f32[8,2,32]{2,1,0:T(2,128)S(1)}, f32[8,2,32]{2,1,0:T(2,128)}, u32[]{:S(2)}) copy-start(f32[8,2,32]{2,1,0:T(2,128)} %cg_ref.1) | copy-start | bytes 6148
  0.7 9.2 %copy-start.8 = (f32[2,64]{1,0:T(2,128)S(1)}, f32[2,64]{1,0:T(2,128)}, u32[]{:S(2)}) copy-start(f32[2,64]{1,0:T(2,128)} %x_ref.1) | copy-start | bytes 1540
  4.8 9.8 %copy-start = (f32[8,2,72,128]{3,2,1,0:T(8,128)S(1)}, f32[8,2,72,128]{3,2,1,0:T(8,128)}, u32[]{:S(2)}) copy-start(f32[8,2,72,128]{3,2,1,0:T(8,128)} %get-tuple-element.55.own_ref) | copy-start | bytes 1769476
  4.9 1.6 %collective-permute-start = (f32[2,72,128]{2,1,0:T(8,128)}, f32[2,72,128]{2,1,0:T(8,128)S(1)}, u32[]{:S(2)}, u32[]{:S(2)}) collective-permute-start(f32[2,72,128]{2,1,0:T(8,128)} %get-tuple-element.47.source_ref), channel_id=1, source_target_pairs={{0,1},{1,0},{2,3},{3,2},{4,5},{5,4},{6,7},{7,6},{8,9},{9,8},{10,11... | collective-permute-start | bytes 221192 | tf_op jit(solution)/shard_map/ppermute | solution.py:527
  5.4 0.9 %copy-start.4 = (f32[2,72,128]{2,1,0:T(8,128)S(1)}, f32[2,72,128]{2,1,0:T(8,128)}, u32[]{:S(2)}) copy-start(f32[2,72,128]{2,1,0:T(8,128)} %get-tuple-element.47.source_ref) | copy-start | bytes 221188
  6.9 5.5 %collective-permute-start.1 = (f32[2,72,128]{2,1,0:T(8,128)S(1)}, f32[2,72,128]{2,1,0:T(8,128)S(1)}, u32[]{:S(2)}, u32[]{:S(2)}) collective-permute-start(f32[2,72,128]{2,1,0:T(8,128)S(1)} %get-tuple-element.48.own_ref), channel_id=1, source_target_pairs={{0,2},{1,3},{2,0},{3,1},{4,6},{5,7},{6,4},{7,5},{8,10},{9,11},{10,... | collective-permute-start | bytes 221192 | tf_op jit(solution)/shard_map/ppermute | solution.py:527
  9.8 1.0 %copy-start.1 = (f32[8,64,128]{2,1,0:T(8,128)S(1)}, f32[8,64,128]{2,1,0:T(8,128)}, u32[]{:S(2)}) copy-start(f32[8,64,128]{2,1,0:T(8,128)} %get-tuple-element.50.at_ref) | copy-start | bytes 786436
  10.8 0.9 %copy-start.3 = (f32[8,32,128]{2,1,0:T(8,128)S(1)}, f32[8,32,128]{2,1,0:T(8,128)}, u32[]{:S(2)}) copy-start(f32[8,32,128]{2,1,0:T(8,128)} %get-tuple-element.51.btp_ref) | copy-start | bytes 393220
  12.8 4.4 %collective-permute-start.2 = (f32[2,72,128]{2,1,0:T(8,128)S(1)}, f32[2,72,128]{2,1,0:T(8,128)S(1)}, u32[]{:S(2)}, u32[]{:S(2)}) collective-permute-start(f32[2,72,128]{2,1,0:T(8,128)S(1)} %get-tuple-element.53.own_ref), channel_id=1, source_target_pairs={{0,4},{1,5},{2,6},{3,7},{4,0},{5,1},{6,2},{7,3},{8,12},{9,13},{10,... | collective-permute-start | bytes 221192 | tf_op jit(solution)/shard_map/ppermute | solution.py:527
  14.7 2.5 %copy-start.2 = (f32[72,128]{1,0:T(8,128)S(1)}, f32[72,128]{1,0:T(8,128)}, u32[]{:S(2)}) copy-start(f32[72,128]{1,0:T(8,128)} %get-tuple-element.46.term_ref) | copy-start | bytes 110596
  17.9 4.9 %collective-permute-start.3 = (f32[72,128]{1,0:T(8,128)S(1)}, f32[72,128]{1,0:T(8,128)S(1)}, u32[]{:S(2)}, u32[]{:S(2)}) collective-permute-start(f32[72,128]{1,0:T(8,128)S(1)} %get-tuple-element.56), channel_id=1, source_target_pairs={{0,8},{1,9},{2,10},{3,11},{4,12},{5,13},{6,14},{7,15},{8,0},{9,1},... | collective-permute-start | bytes 110600 | tf_op jit(solution)/shard_map/ppermute | solution.py:527
  26.3 1.3 %collective-permute-start.4 = (f32[80,128]{1,0:T(8,128)S(1)}, f32[80,128]{1,0:T(8,128)S(1)}, u32[]{:S(2)}, u32[]{:S(2)}) collective-permute-start(f32[80,128]{1,0:T(8,128)S(1)} %get-tuple-element.74.args_0_), channel_id=1, source_target_pairs={{0,1},{1,0},{2,3},{3,2},{4,5},{5,4},{6,7},{7,6},{8,9},{9,8},{10,11... | collective-permute-start | bytes 122888 | tf_op jit(solution)/shard_map/ppermute | solution.py:527
  27.8 4.1 %collective-permute-start.5 = (f32[80,128]{1,0:T(8,128)S(1)}, f32[80,128]{1,0:T(8,128)S(1)}, u32[]{:S(2)}, u32[]{:S(2)}) collective-permute-start(f32[80,128]{1,0:T(8,128)S(1)} %get-tuple-element.75.own_ref), channel_id=1, source_target_pairs={{0,2},{1,3},{2,0},{3,1},{4,6},{5,7},{6,4},{7,5},{8,10},{9,11},{10,... | collective-permute-start | bytes 122888 | tf_op jit(solution)/shard_map/ppermute | solution.py:527
  32.0 4.1 %collective-permute-start.6 = (f32[80,128]{1,0:T(8,128)S(1)}, f32[80,128]{1,0:T(8,128)S(1)}, u32[]{:S(2)}, u32[]{:S(2)}) collective-permute-start(f32[80,128]{1,0:T(8,128)S(1)} %get-tuple-element.77.own_ref), channel_id=1, source_target_pairs={{0,4},{1,5},{2,6},{3,7},{4,0},{5,1},{6,2},{7,3},{8,12},{9,13},{10,... | collective-permute-start | bytes 122888 | tf_op jit(solution)/shard_map/ppermute | solution.py:527
  36.4 4.6 %collective-permute-start.7 = (f32[16,128]{1,0:T(8,128)S(1)}, f32[16,128]{1,0:T(8,128)S(1)}, u32[]{:S(2)}, u32[]{:S(2)}) collective-permute-start(f32[16,128]{1,0:T(8,128)S(1)} %get-tuple-element.80.own_ref), channel_id=1, source_target_pairs={{0,8},{1,9},{2,10},{3,11},{4,12},{5,13},{6,14},{7,15},{8,0},{9,1},... | collective-permute-start | bytes 24584 | tf_op jit(solution)/shard_map/ppermute | solution.py:527

commit v3 on v2

--- a/solution.py
+++ b/solution.py
@@ -10,7 +10,6 @@
 
 F32 = jnp.float32
 LANES = 128
-VMEM = 60
 TAIL = 8
 
 
@@ -104,7 +103,9 @@
 def prefixes(items, joined):
     items, step = list(items), 1
     while step < len(items):
-        items = items[:step] + joined([(items[i - step], items[i]) for i in range(step, len(items))])
+        late = [i for i in range(len(items)) if i // step % 2]
+        for i, joint in zip(late, joined([(items[i // step * step - 1], items[i]) for i in late])):
+            items[i] = joint
         step *= 2
     return items
 
@@ -129,14 +130,12 @@
 
 
 def block_kernel(knots, *refs):
-    sources, (total_ref, *outs), held, kept, sems, out_sems = refs[:8], refs[8:13], refs[13:21], refs[21:25], *refs[25:]
+    sources, (total_ref, own_ref, term_ref, at_ref, btp_ref), held, sems = refs[:8], refs[8:13], refs[13:21], refs[21]
     copies = [pltpu.make_async_copy(a, b, sems.at[i]) for i, (a, b) in enumerate(zip(sources, held))]
     order = (7, 2, 1, 6, 3, 4, 5, 0)
     for i in order:
         copies[i].start()
-    leaving = [pltpu.make_async_copy(a, b, out_sems.at[i]) for i, (a, b) in enumerate(zip(kept, outs))]
     a_ref, bt_ref, g_ref, d_ref, sg_ref, cg_ref, cf_ref, rf_ref = held
-    own_ref, term_ref, at_ref, btp_ref = kept
     count, trajs, nu, width = bt_ref.shape
     both = trajs * width
     scale = 1.0 / math.sqrt(knots)
@@ -152,13 +151,11 @@
         btp = paired(bt_ref[t])
         btp_ref[t] = btp
         pushed.append(prod(gt, jnp.concatenate([spread(btp, trajs), root], axis=1)))
-    leaving[3].start()
     for i in (6, 3, 4, 5):
         copies[i].wait()
     term = term_of(cf_ref[...], trajs)
     run_q = term / knots
     term_ref[...] = join(term, jnp.zeros((TAIL, both), F32))
-    leaving[1].start()
     drift = side_by_side(d_ref[...], trajs) * scale
     grad = side_by_side(sg_ref[...], trajs) * scale
     cg = cg_ref[...]
@@ -176,19 +173,11 @@
         own_ref[t, 0] = x
         own_ref[t, 1] = y
         maps.append((x, y))
-    leaving[0].start()
-    leaving[2].start()
-    x, y = fold(maps, lambda pairs: compose_values(pairs, trajs, width))
-    total_ref[0] = x
-    total_ref[1] = y
-    for copy in leaving:
-        copy.wait()
-
-
-def copy_kernel(source_ref, out_ref, sem):
-    copy = pltpu.make_async_copy(source_ref, out_ref, sem)
-    copy.start()
-    copy.wait()
+    befores = prefixes([x for x, _ in maps], lambda pairs: compose_states(pairs, trajs, width))
+    nothing = jnp.zeros_like(maps[0][1])
+    parts = apply_values([(x, nothing) for x in befores[:-1]], [y for _, y in maps[1:]], trajs, width)
+    total_ref[0] = befores[-1]
+    total_ref[1] = functools.reduce(jnp.add, parts, maps[0][1])
 
 
 def suffix_kernel(own_ref, *refs, trajs, width):
@@ -200,19 +189,9 @@
         out_ref[count - 2 - i, 1] = y
 
 
-def reach_kernel(suffix_ref, seen_ref, left_ref, right_ref, y_ref, *, trajs, width):
-    count = suffix_ref.shape[0] + 1
-    seen = (seen_ref[0], seen_ref[1])
-    maps = compose_values([((suffix_ref[t, 0], suffix_ref[t, 1]), seen) for t in range(count - 1)], trajs, width)
-    for t, (x, y) in enumerate(maps + [seen]):
-        left_ref[t] = left_of(join(x, jnp.zeros((left_ref.shape[1] - x.shape[0], x.shape[1]), F32)))
-        right_ref[t] = right_of(spread(x[:width], trajs), flip=True)
-        y_ref[t] = y
-
-
 def prepare_kernel(
     knots, at_ref, btp_ref, d_ref, cg_ref, rf_ref, x_ref,
-    value_ref, hess_ref, cross_ref, gain_ref, bd_ref, ad_ref, run_r_ref, control_ref, init_ref,
+    left_ref, hess_ref, cross_ref, gain_ref, bd_ref, ad_ref, run_r_ref, control_ref, init_ref,
 ):
     count, nu, both = btp_ref.shape
     trajs, width = x_ref.shape
@@ -226,23 +205,59 @@
     lanes = lax.broadcasted_iota(jnp.int32, (nu, nu), 1)
     run_r = prod(rf, rf, flip=True) + jnp.where(rows == lanes, 1.0, 0.0)
     run_r_ref[...] = jnp.concatenate([run_r] * (LANES // nu), axis=1)
-    spare = jnp.zeros((value_ref.shape[1] - nu - TAIL, both), F32)
+    spare = jnp.zeros((left_ref.shape[1] - nu - TAIL - width, both), F32)
     bds = []
     for t in range(count):
         at, btp = at_ref[t], btp_ref[t]
         bd = spread(btp, trajs)
         bds.append(bd)
         tail = tail_of(drift[t : t + 1])
-        value_ref[t] = left_of(jnp.concatenate([btp, tail, spare], axis=0))
-        hess_ref[t] = right_of(
-            jnp.concatenate([bd if i == t % group else jnp.zeros_like(bd) for i in range(group)], axis=0), flip=True
-        )
-        cross_ref[t] = right_of(jnp.concatenate([at, jnp.zeros((-width % LANES, both), F32)], axis=0), flip=True)
+        left_ref[t] = left_of(jnp.concatenate([btp, tail, at, spare], axis=0))
+        hess_ref[t] = placed(bd, t % group, group)
+        cross_ref[t] = right_of(over(at), flip=True)
         bd_ref[t] = bd
         ad_ref[t] = join(at, tail)
         if len(bds) == group:
             gain_ref[t // group] = right_of(jnp.concatenate(bds, axis=0))
             bds = []
+
+
+def placed(bd, at, group):
+    return right_of(jnp.concatenate([bd if i == at else jnp.zeros_like(bd) for i in range(group)], axis=0), flip=True)
+
+
+def over(matrix):
+    return jnp.concatenate([matrix, jnp.zeros((-matrix.shape[0] % LANES, matrix.shape[1]), F32)], axis=0)
+
+
+def reach_kernel(
+    suffix_ref, seen_ref, left_ref, hess_ref, cross_ref, bd_ref, run_r_ref, control_ref,
+    value_out, hess_out, cross_out, bd_out, hess_base, cross_base, *, trajs, width,
+):
+    count, nu = left_ref.shape[0], run_r_ref.shape[0]
+    group = count // hess_base.shape[0]
+    seen = (seen_ref[0], seen_ref[1])
+    maps = compose_values([((suffix_ref[t, 0], suffix_ref[t, 1]), seen) for t in range(count - 1)], trajs, width)
+    maps.append(seen)
+    both = trajs * width
+    rows = value_out.shape[1]
+    firsts = [product_of(left_ref[t], right_of(spread(x[:width], trajs))) for t, (x, _) in enumerate(maps)]
+    us = [product_of(left_ref[t, :rows], right_of(spread(y[:width], trajs))) for t, (_, y) in enumerate(maps)]
+    hesses = [product_of(left_of(u[:nu]), hess_ref[t], flip=True) for t, u in enumerate(us)]
+    crosses = [product_of(left_of(spread(u[:nu], trajs)), cross_ref[t], flip=True) for t, u in enumerate(us)]
+    lin_lane = lax.broadcasted_iota(jnp.int32, crosses[0].shape, 1) == width
+    spare = jnp.zeros((rows - nu - TAIL, both), F32)
+    for t, (w, (x, y)) in enumerate(zip(firsts, maps)):
+        bd = spread(w[:nu], trajs)
+        value_out[t] = left_of(jnp.concatenate([w[:nu], w[nu : nu + TAIL] + x[width:], spare], axis=0))
+        hess_out[t] = placed(bd, t % group, group)
+        cross_out[t] = right_of(over(w[nu + TAIL : nu + TAIL + width]), flip=True)
+        bd_out[t] = bd
+        vector = us[t][nu : nu + 1] + y[width : width + 1]
+        lin = jnp.sum(bd_ref[t] * vector, axis=1, keepdims=True) + control_ref[:, t : t + 1]
+        cross_base[t] = jnp.where(lin_lane, lin, crosses[t])
+    for g in range(count // group):
+        hess_base[g] = functools.reduce(jnp.add, hesses[g * group : (g + 1) * group], run_r_ref[...])
 
 
 def upper(step):
@@ -281,23 +296,31 @@
     next_ref[1] = jnp.where(up, seen[1], sy)
 
 
-def inverses(packs, size):
+def factors(packs, size):
     block, step = 8, 4
     rows = lax.broadcasted_iota(jnp.int32, (block, LANES), 0)
     lanes = lax.broadcasted_iota(jnp.int32, (block, LANES), 1)
     inner = lanes % size
     first = lanes - inner
     packs = [[pack[i : i + block] for i in range(0, size, block)] for pack in packs]
+    ws = [[jnp.zeros((block, LANES), F32) for _ in pack] for pack in packs]
+    qs = [list(w) for w in ws]
     for k in range(0, size, step):
         at, r = k // block, k % block
         inside = (inner >= k) & (inner < k + step)
+        known = inner[:1] < k + step
         for number, pack in enumerate(packs):
-            columns = [[jnp.take_along_axis(x, first + (k + j), axis=1) for x in pack] for j in range(step)]
-            p = [[columns[j][at][r + i : r + i + 1] for j in range(step)] for i in range(step)]
+            columns = {
+                i: [jnp.take_along_axis(pack[i], first + (k + j), axis=1) for j in range(step)]
+                for i in range(at, len(pack))
+            }
+            p = [[columns[at][j][r + i : r + i + 1] for j in range(step)] for i in range(step)]
             z = [
                 jnp.where(inside[:1], jnp.where(inner[:1] == k + i, 1.0, 0.0), pack[at][r + i : r + i + 1])
                 for i in range(step)
             ]
+            for i in range(step):
+                ws[number][at] = jnp.where(rows == r + i, jnp.where(known, z[i], 0.0), ws[number][at])
             inverse = []
             for i in range(step):
                 inverse.append(1.0 / p[i][i])
@@ -312,56 +335,52 @@
                 for j in range(i + 1, step):
                     v = v - p[i][j] * q[j]
                 q[i] = v * inverse[i]
-            done = []
-            for i, x in enumerate(pack):
-                y = jnp.where(inside, 0.0, x)
+            for i in range(step):
+                qs[number][at] = jnp.where(rows == r + i, jnp.where(known, q[i], 0.0), qs[number][at])
+            for i in range(at if r + step < block else at + 1, len(pack)):
+                y = jnp.where(inside, 0.0, pack[i])
                 for j in range(step):
-                    y = y - columns[j][i] * q[j]
-                if i == at:
-                    for j in range(step):
-                        y = jnp.where(rows == r + j, q[j], y)
-                done.append(y)
-            packs[number] = done
-    return [jnp.concatenate(pack, axis=0) for pack in packs]
+                    y = y - columns[i][j] * q[j]
+                pack[i] = y
+    return [(jnp.concatenate(w, axis=0), jnp.concatenate(q, axis=0)) for w, q in zip(ws, qs)]
 
 
 def solve_kernel(
-    step, term_ref, end_ref, left_ref, right_ref, y_ref,
-    value_ref, hess_ref, cross_ref, gain_ref, bd_ref, ad_ref, run_r_ref, control_ref,
-    total_ref, own_ref, system_ref, inverse_ref,
+    step, term_ref, end_ref, value_ref, hess_ref, cross_ref, bd_ref, hess_base, cross_base, gain_ref, ad_ref,
+    total_ref, own_ref, half_ref, q_ref,
 ):
     count, stack, both = bd_ref.shape
     size = ad_ref.shape[1]
-    width, nu = size - TAIL, run_r_ref.shape[0]
-    trajs = both // width
-    group = LANES // stack
+    groups, nu, _ = hess_base.shape
+    width = size - TAIL
+    trajs, group = both // width, count // groups
+    rows = value_ref.shape[1]
     lin_lane = lax.broadcasted_iota(jnp.int32, (stack, LANES), 1) == width
 
     end = jnp.where(upper(step), term_ref[...], end_ref[...])
-    end_left = left_of(end)
-    ws = [product_of(end_left, right_ref[t], flip=True) for t in range(count)]
-    zs = [product_of(left_ref[t], right_of(spread(w[:width], trajs)))[:size] + y_ref[t] for t, w in enumerate(ws)]
-    values = [(z[:width], z[width : width + 1] + w[width : width + 1]) for z, w in zip(zs, ws)]
-
-    us = [product_of(value_ref[t], right_of(spread(p, trajs))) for t, (p, _) in enumerate(values)]
-    hesses = [product_of(left_of(u[:nu]), hess_ref[t], flip=True) for t, u in enumerate(us)]
-    crosses = [product_of(left_of(spread(u[:nu], trajs)), cross_ref[t], flip=True) for t, u in enumerate(us)]
-    hesses = [functools.reduce(jnp.add, hesses[t : t + group], run_r_ref[...]) for t in range(0, count, group)]
-    systems, columns = [], []
-    for t, (u, (_, vector)) in enumerate(zip(us, values)):
-        lin = jnp.sum(bd_ref[t] * (vector + u[nu : nu + 1]), axis=1, keepdims=True) + control_ref[:, t : t + 1]
-        systems.append(jnp.where(lin_lane, lin, crosses[t]))
-        columns.append(lin)
-
-    packs = inverses(hesses, nu)
+    w = product_of(value_ref[...].reshape(count * rows, 2 * both), right_of(spread(end[:width], trajs)))
+    us = [w[t * rows : t * rows + nu] for t in range(count)]
+    hesses = [product_of(left_of(u), hess_ref[t], flip=True) for t, u in enumerate(us)]
+    hesses = [functools.reduce(jnp.add, hesses[g * group : (g + 1) * group], hess_base[g]) for g in range(groups)]
+    pairs = factors(hesses, nu)
+    crosses = [product_of(left_of(spread(u, trajs)), cross_ref[t], flip=True) for t, u in enumerate(us)]
+    systems = []
+    for t, cross in enumerate(crosses):
+        vector = w[t * rows + nu : t * rows + nu + 1] + end[width : width + 1]
+        lin = jnp.sum(bd_ref[t] * vector, axis=1, keepdims=True)
+        systems.append(jnp.where(lin_lane, lin, cross) + cross_base[t])
+
+    flats = [jnp.concatenate(systems[t : t + group], axis=0).T[:size] for t in range(0, count, group)]
+    lefts = [left_of(flat) for flat in flats]
     lanes = lax.broadcasted_iota(jnp.int32, (1, LANES), 1)
-    flats = [jnp.concatenate(systems[t : t + group], axis=0).T[:size] for t in range(0, count, group)]
-    solved = [product_of(left_of(spread(pack, LANES // nu)), gain_ref[g]) for g, pack in enumerate(packs)]
+    spreads = [(spread(w, LANES // nu), spread(q, LANES // nu)) for w, q in pairs]
+    halves = [product_of(left, right_of(w, flip=True), flip=True) for left, (w, _) in zip(lefts, spreads)]
+    pushes = [product_of(left_of(q), gain_ref[g]) for g, (_, q) in enumerate(spreads)]
     maps = []
-    for g, flat in enumerate(flats):
-        left = left_of(flat)
+    for g, half in enumerate(halves):
+        left = left_of(half)
         for i in range(group):
-            mine = solved[g][i * stack : (i + 1) * stack]
+            mine = pushes[g][i * stack : (i + 1) * stack]
             pieces = [mine if k == i else jnp.zeros_like(mine) for k in range(group)]
             maps.append(ad_ref[g * group + i] - product_of(left, right_of(jnp.concatenate(pieces, axis=0))))
     total_ref[:size] = fold(maps, lambda pairs: compose_states(pairs, trajs, width))
@@ -369,16 +388,10 @@
         own_ref[t] = m
 
     decrease = jnp.zeros((1, LANES), F32)
-    for g, (pack, flat) in enumerate(zip(packs, flats)):
-        inverse_ref[g] = pack
-        system_ref[g] = flat
-        linear = jnp.zeros((nu, LANES), F32)
-        for i in range(group):
-            for j in range(trajs):
-                at = i * trajs + j
-                column = columns[g * group + i][j * nu : (j + 1) * nu]
-                linear = jnp.where((lanes >= at * nu) & (lanes < (at + 1) * nu), column, linear)
-        feed = -jnp.sum(linear * pack, axis=0, keepdims=True)
+    for g, (half, flat) in enumerate(zip(halves, flats)):
+        half_ref[g] = half
+        q_ref[g] = pairs[g][1]
+        feed = -prod(half[width:], spreads[g][1])[:1]
         feed_columns = jnp.broadcast_to(feed, (TAIL, LANES)).T
         weights = jnp.zeros((nu, LANES), F32)
         for at in range(LANES // nu):
@@ -390,13 +403,13 @@
 
 
 def expand_kernel(
-    own_ref, system_ref, inverse_ref, gain_ref, feed_ref, map_ref, *, trajs, width
+    own_ref, half_ref, q_ref, gain_ref, feed_ref, map_ref, *, trajs, width
 ):
     count, size, both = own_ref.shape
-    groups, nu, _ = inverse_ref.shape
+    groups, nu, _ = q_ref.shape
     group, stack = count // groups, trajs * nu
     gains = []
-    kts = [-prod(system_ref[g], spread(inverse_ref[g], LANES // nu)) for g in range(groups)]
+    kts = [-prod(half_ref[g], spread(q_ref[g], LANES // nu)) for g in range(groups)]
     for g, kt in enumerate(kts):
         spare = jnp.zeros((LANES - size, LANES), F32)
         natural = join(kt, spare).T
@@ -488,13 +501,13 @@
         decrease_ref[:, j : j + 1] = jnp.sum(jnp.where(lane == j, sums, 0.0), axis=1, keepdims=True)
 
 
-def call(body, outs, *args, vmem=32, **named):
+def call(body, outs, *args, **named):
     return pl.pallas_call(
         body,
         out_shape=[
             jax.ShapeDtypeStruct(shape, F32) if isinstance(shape, tuple) else shape for shape in outs
         ],
-        compiler_params=pltpu.CompilerParams(vmem_limit_bytes=vmem * 1024 * 1024),
+        compiler_params=pltpu.CompilerParams(vmem_limit_bytes=32 * 1024 * 1024),
         **named,
     )(*args)
 
@@ -530,28 +543,23 @@
     groups, up16 = count * stack // LANES, lambda n: -(-n // 16) * 16
     bt = jnp.swapaxes(dyn_b, 2, 3)
     inputs = (dyn_a, bt, gains, defects, state_grad, control_grad, cost_factor, control_factor)
-    outs = [(2, size, both), (count, 2, size, both), (size, both), (count, width, both), (count, nu, both)]
     total, own, term, at, btp = call(
-        functools.partial(block_kernel, knots), outs, *inputs,
-        vmem=VMEM,
-        in_specs=[pl.BlockSpec(memory_space=pl.ANY)] * len(inputs),
-        out_specs=[pl.BlockSpec(memory_space=pltpu.VMEM)] + [pl.BlockSpec(memory_space=pl.ANY)] * 4,
-        scratch_shapes=[pltpu.VMEM(x.shape, F32) for x in inputs] + [pltpu.VMEM(shape, F32) for shape in outs[1:]]
-        + [pltpu.SemaphoreType.DMA((len(inputs),)), pltpu.SemaphoreType.DMA((4,))],
+        functools.partial(block_kernel, knots),
+        [(2, size, both), (count, 2, size, both), (size, both), (count, width, both), (count, nu, both)],
+        *[pltpu.with_memory_space_constraint(x, pltpu.HBM) for x in inputs],
+        in_specs=[pl.BlockSpec(memory_space=pltpu.HBM)] * len(inputs),
+        scratch_shapes=[pltpu.VMEM(x.shape, F32) for x in inputs] + [pltpu.SemaphoreType.DMA((len(inputs),))],
     )
     suffix, = call(functools.partial(suffix_kernel, **sizes), [(count - 1, 2, size, both)], own)
-    *ready, init = call(
+    turned = (count, 2 * LANES, 2 * both)
+    left, hess, cross, gain, bd, ad, run_r, control, init = call(
         functools.partial(prepare_kernel, knots),
-        [halves(count, up16(nu + TAIL), 2 * both), halves(count, 2 * LANES, 2 * both),
-         halves(count, 2 * LANES, 2 * both), halves(groups, 2 * LANES, 2 * both), (count, stack, both),
-         (count, size, both), (nu, LANES), (stack, count), (TAIL, both)],
+        [halves(count, up16(nu + TAIL + width), 2 * both), halves(*turned), halves(*turned),
+         halves(groups, *turned[1:]), (count, stack, both), (count, size, both), (nu, LANES), (stack, count),
+         (TAIL, both)],
         at, btp, defects, control_grad, control_factor, init_state,
     )
     got = exchange(total, steps[0])
-    total, = call(
-        copy_kernel, [(2, size, both)], total,
-        in_specs=[pl.BlockSpec(memory_space=pl.ANY)], scratch_shapes=[pltpu.SemaphoreType.DMA],
-    )
     total, after = call(
         functools.partial(without(value_step_kernel, 3), steps[0], **sizes), [(2, size, both)] * 2, total, got
     )
@@ -568,18 +576,20 @@
     )
     reach = call(
         functools.partial(reach_kernel, **sizes),
-        [halves(count, up16(size), 2 * both), halves(count, 2 * both, 2 * both), (count, size, both)], suffix, after,
+        [halves(count, up16(nu + TAIL), 2 * both), halves(*turned), halves(*turned), (count, stack, both),
+         (groups, nu, LANES), (count, stack, LANES)],
+        suffix, after, left, hess, cross, bd, run_r, control,
     )
     value = exchange(value, steps[-1])
-    total, own, system, inverse = call(
+    total, own, half, q = call(
         functools.partial(solve_kernel, steps[-1]),
         [(size + TAIL, both), (count, size, both), (groups, size, LANES), (groups, nu, LANES)],
-        term, value, *reach, *ready,
+        term, value, *reach, gain, ad,
     )
     wide = both + -(-stack // LANES) * LANES
     new_gains, feedforward, maps = call(
         functools.partial(expand_kernel, **sizes),
-        [(count, trajs, nu, width), (count, trajs, nu), (count, size, wide)], own, system, inverse,
+        [(count, trajs, nu, width), (count, trajs, nu), (count, size, wide)], own, half, q,
     )
     seen = []
     for step in steps[:-2]:

time: 42.1 us -> 40.5 us (0.962)
  local copies, waits for them, and re-layouts: 2.76 us -> 0.68 us
  waiting for transfers between devices: 8.33 us -> 9.58 us
  Pallas kernels: 15.2 us -> 14.4 us
    unnamed x18 -> x8, local copies, waits for them, and re-layouts: 2.76 us -> 0.68 us
    ppermute x8, waiting for transfers between devices: 8.33 us -> 9.58 us  [exchange(): return lax.ppermute(value, 'tm', [(i, i ^ step) for i in range(devices)])]
    pallas_call x15 -> x14, Pallas kernels: 15.2 us -> 14.4 us  [call(): pl.pallas_call(body, out_shape=[jax.ShapeDtypeStruct(shape, F32) if isins...]
  transfers between devices with their start and end apart: 8 -> 8, of which waited for: 8 -> 8; matrix products, arithmetic and copies ran while one was open for 0% -> 0% of each run, Pallas kernels for 11% -> 13%
where the time goes in v3:
time: 40.5 us; the launch traced here: 40.3 us
  starting transfers between devices  14.9 us (37%)
  Pallas kernels  14.4 us (36%)
  waiting for transfers between devices  9.58 us (24%)
  between operations  0.72 us (2%)
  local copies, waits for them, and re-layouts  0.68 us (2%)
    ppermute x8, starting transfers between devices, exchange(): return lax.ppermute(value, 'tm', [(i, i ^ step) for i in range(devices)])  14.9 us
    pallas_call x14, Pallas kernels, call(): pl.pallas_call(body, out_shape=[jax.ShapeDtypeStruct(shape, F32) if isins...  14.4 us
    ppermute x8, waiting for transfers between devices, exchange(): return lax.ppermute(value, 'tm', [(i, i ^ step) for i in range(devices)])  9.58 us
  transfers between devices with their start and end apart: 8, of which 8 were waited for; matrix products, arithmetic and copies ran while one was open for 0% of the time, Pallas kernels for 13%

profile of v3, /device:TPU:0, one launch (start us, length us, event | category | flops | bytes accessed | tf_op | source)
XLA Modules:
  0.0 40.3 jit_solution(50360989846709670)
XLA Ops:
  0.6 3.3 %shard_map.128 = (f32[2,72,128]{2,1,0:T(8,128)S(1)}, f32[8,2,72,128]{3,2,1,0:T(8,128)S(1)}, f32[72,128]{1,0:T(8,128)S(1)}, f32[8,64,128]{2,1,0:T(8,128)S(1)}, f32[8,32,128]{2,1,0:T(8,128)S(1)}) custom-call(f32[8,2,64,64]{3,2,1,0:T(8,128)} %refs_0_.1, f32[8,2,32,64]{3,2,1,0:T(8,128)} %bitcast.2, f32[8,2,32,64]{3,2,1,0:T(8,128)} %refs_2_.1, ...), custom_call_target="tpu_custom_call" | custom-call | tf_op jit(solution)/shard_map/pallas_call | solution.py:505
  3.9 0.5 %collective-permute-start = (f32[2,72,128]{2,1,0:T(8,128)S(1)}, f32[2,72,128]{2,1,0:T(8,128)S(1)}, u32[]{:S(2)}, u32[]{:S(2)}) collective-permute-start(f32[2,72,128]{2,1,0:T(8,128)S(1)} %get-tuple-element.50.own_ref), channel_id=1, source_target_pairs={{0,1},{1,0},{2,3},{3,2},{4,5},{5,4},{6,7},{7,6},{8,9},{9,8},{10,11... | collective-permute-start | bytes 221192 | tf_op jit(solution)/shard_map/ppermute | solution.py:540
  4.4 0.9 %collective-permute-done.got_ref = f32[2,72,128]{2,1,0:T(8,128)S(1)} collective-permute-done((f32[2,72,128]{2,1,0:T(8,128)S(1)}, f32[2,72,128]{2,1,0:T(8,128)S(1)}, u32[]{:S(2)}, u32[]{:S(2)}) %collective-permute-start) | collective-permute-done | bytes 73760 | tf_op jit(solution)/shard_map/ppermute | solution.py:540
  5.7 2.9 %collective-permute-start.1 = (f32[2,72,128]{2,1,0:T(8,128)S(1)}, f32[2,72,128]{2,1,0:T(8,128)S(1)}, u32[]{:S(2)}, u32[]{:S(2)}) collective-permute-start(f32[2,72,128]{2,1,0:T(8,128)S(1)} %get-tuple-element.51.own_ref), channel_id=1, source_target_pairs={{0,2},{1,3},{2,0},{3,1},{4,6},{5,7},{6,4},{7,5},{8,10},{9,11},{10,... | collective-permute-start | bytes 221192 | tf_op jit(solution)/shard_map/ppermute | solution.py:540
  8.7 0.7 %copy-done.3 = f32[2,64]{1,0:T(2,128)S(1)} copy-done((f32[2,64]{1,0:T(2,128)S(1)}, f32[2,64]{1,0:T(2,128)}, u32[]{:S(2)}) %copy-start.3) | copy-done | bytes 536
  9.6 1.6 %collective-permute-done.1.got_ref = f32[2,72,128]{2,1,0:T(8,128)S(1)} collective-permute-done((f32[2,72,128]{2,1,0:T(8,128)S(1)}, f32[2,72,128]{2,1,0:T(8,128)S(1)}, u32[]{:S(2)}, u32[]{:S(2)}) %collective-permute-start.1) | collective-permute-done | bytes 73760 | tf_op jit(solution)/shard_map/ppermute | solution.py:540
  11.2 0.4 shard_map.131
  11.6 1.9 %collective-permute-start.2 = (f32[2,72,128]{2,1,0:T(8,128)S(1)}, f32[2,72,128]{2,1,0:T(8,128)S(1)}, u32[]{:S(2)}, u32[]{:S(2)}) collective-permute-start(f32[2,72,128]{2,1,0:T(8,128)S(1)} %get-tuple-element.56.own_ref), channel_id=1, source_target_pairs={{0,4},{1,5},{2,6},{3,7},{4,0},{5,1},{6,2},{7,3},{8,12},{9,13},{10,... | collective-permute-start | bytes 221192 | tf_op jit(solution)/shard_map/ppermute | solution.py:540
  13.5 1.1 %shard_map.132.refs_0_.suffix_ref = f32[7,2,72,128]{3,2,1,0:T(8,128)S(1)} custom-call(f32[8,2,72,128]{3,2,1,0:T(8,128)S(1)} %get-tuple-element.58.own_ref), custom_call_target="tpu_custom_call" | custom-call | tf_op jit(solution)/shard_map/pallas_call | solution.py:505
  14.6 1.4 %collective-permute-done.2.got_ref = f32[2,72,128]{2,1,0:T(8,128)S(1)} collective-permute-done((f32[2,72,128]{2,1,0:T(8,128)S(1)}, f32[2,72,128]{2,1,0:T(8,128)S(1)}, u32[]{:S(2)}, u32[]{:S(2)}) %collective-permute-start.2) | collective-permute-done | bytes 73760 | tf_op jit(solution)/shard_map/ppermute | solution.py:540
  16.1 0.6 %shard_map.133 = (f32[72,128]{1,0:T(8,128)S(1)}, f32[2,72,128]{2,1,0:T(8,128)S(1)}) custom-call(f32[2,72,128]{2,1,0:T(8,128)S(1)} %get-tuple-element.56.own_ref, f32[2,72,128]{2,1,0:T(8,128)S(1)} %collective-permute-done.2.got_ref, f32[2,72,128]{2,1,0:T(8,128)S(1)} %get-tuple-element.57.seen_ref, f32[72,128]{1,0:T(8,128)S(1)} %get-tuple-element.49.term_ref, ...), custom_call_target="tpu_custom_call" | custom-call | tf_op jit(solution)/shard_map/pallas_call | solution.py:505
  16.7 2.9 %collective-permute-start.3 = (f32[72,128]{1,0:T(8,128)S(1)}, f32[72,128]{1,0:T(8,128)S(1)}, u32[]{:S(2)}, u32[]{:S(2)}) collective-permute-start(f32[72,128]{1,0:T(8,128)S(1)} %get-tuple-element.59), channel_id=1, source_target_pairs={{0,8},{1,9},{2,10},{3,11},{4,12},{5,13},{6,14},{7,15},{8,0},{9,1},... | collective-permute-start | bytes 110600 | tf_op jit(solution)/shard_map/ppermute | solution.py:540
  19.6 1.7 %shard_map.134 = (bf16[8,48,256]{2,1,0:T(8,128)(2,1)S(1)}, bf16[8,256,256]{2,1,0:T(8,128)(2,1)S(1)}, bf16[8,256,256]{2,1,0:T(8,128)(2,1)S(1)}, f32[8,64,128]{2,1...) custom-call(f32[7,2,72,128]{3,2,1,0:T(8,128)S(1)} %shard_map.132.refs_0_.suffix_ref, ...), custom_call_target="tpu_custom_call" | custom-call | tf_op jit(solution)/shard_map/pallas_call | solution.py:505
  21.6 3.1 %shard_map.135 = (f32[80,128]{1,0:T(8,128)S(1)}, f32[8,72,128]{2,1,0:T(8,128)S(1)}, f32[4,72,128]{2,1,0:T(8,128)S(1)}, f32[4,32,128]{2,1,0:T(8,128)S(1)}) custom-call(f32[72,128]{1,0:T(8,128)S(1)} %get-tuple-element.49.term_ref, f32[72,128]{1,0:T(8,128)S(1)} %collective-permute-done.3.end_ref, bf16[8,48,256]{2,1,0:T(8,128)(2,1)S(1)} %get-tuple-element.67.value_ref, ...), custom_call_target="tpu_custom_call" | custom-call | tf_op jit(solution)/shard_map/pallas_call | solution.py:505
  24.8 1.2 %collective-permute-done.4.args_1_ = f32[80,128]{1,0:T(8,128)S(1)} collective-permute-done((f32[80,128]{1,0:T(8,128)S(1)}, f32[80,128]{1,0:T(8,128)S(1)}, u32[]{:S(2)}, u32[]{:S(2)}) %collective-permute-start.4) | collective-permute-done | bytes 40992 | tf_op jit(solution)/shard_map/ppermute | solution.py:540
  26.1 1.8 %collective-permute-start.5 = (f32[80,128]{1,0:T(8,128)S(1)}, f32[80,128]{1,0:T(8,128)S(1)}, u32[]{:S(2)}, u32[]{:S(2)}) collective-permute-start(f32[80,128]{1,0:T(8,128)S(1)} %get-tuple-element.81.own_ref), channel_id=1, source_target_pairs={{0,2},{1,3},{2,0},{3,1},{4,6},{5,7},{6,4},{7,5},{8,10},{9,11},{10,... | collective-permute-start | bytes 122888 | tf_op jit(solution)/shard_map/ppermute | solution.py:540
  28.0 2.2 %collective-permute-done.5.got_ref = f32[80,128]{1,0:T(8,128)S(1)} collective-permute-done((f32[80,128]{1,0:T(8,128)S(1)}, f32[80,128]{1,0:T(8,128)S(1)}, u32[]{:S(2)}, u32[]{:S(2)}) %collective-permute-start.5) | collective-permute-done | bytes 40992 | tf_op jit(solution)/shard_map/ppermute | solution.py:540
  30.4 1.9 %collective-permute-start.6 = (f32[80,128]{1,0:T(8,128)S(1)}, f32[80,128]{1,0:T(8,128)S(1)}, u32[]{:S(2)}, u32[]{:S(2)}) collective-permute-start(f32[80,128]{1,0:T(8,128)S(1)} %get-tuple-element.83.own_ref), channel_id=1, source_target_pairs={{0,4},{1,5},{2,6},{3,7},{4,0},{5,1},{6,2},{7,3},{8,12},{9,13},{10,... | collective-permute-start | bytes 122888 | tf_op jit(solution)/shard_map/ppermute | solution.py:540
  32.3 1.2 %shard_map.136 = (f32[8,2,32,64]{3,2,1,0:T(8,128)}, f32[8,2,32]{2,1,0:T(2,128)}, f32[8,72,256]{2,1,0:T(8,128)S(1)}) custom-call(f32[8,72,128]{2,1,0:T(8,128)S(1)} %get-tuple-element.75.own_ref, f32[4,72,128]{2,1,0:T(8,128)S(1)} %get-tuple-element.76.half_ref, f32[4,32,128]{2,1,0:T(8,128)S(1)} %get-tuple-element.77.q_ref), custom_call_target="tpu_custom_call" | custom-call | tf_op jit(solution)/shard_map/pallas_call | solution.py:505
  33.5 1.0 %collective-permute-done.6.got_ref = f32[80,128]{1,0:T(8,128)S(1)} collective-permute-done((f32[80,128]{1,0:T(8,128)S(1)}, f32[80,128]{1,0:T(8,128)S(1)}, u32[]{:S(2)}, u32[]{:S(2)}) %collective-permute-start.6) | collective-permute-done | bytes 40992 | tf_op jit(solution)/shard_map/ppermute | solution.py:540
  34.8 2.9 %collective-permute-start.7 = (f32[16,128]{1,0:T(8,128)S(1)}, f32[16,128]{1,0:T(8,128)S(1)}, u32[]{:S(2)}, u32[]{:S(2)}) collective-permute-start(f32[16,128]{1,0:T(8,128)S(1)} %get-tuple-element.86.own_ref), channel_id=1, source_target_pairs={{0,8},{1,9},{2,10},{3,11},{4,12},{5,13},{6,14},{7,15},{8,0},{9,1},... | collective-permute-start | bytes 24584 | tf_op jit(solution)/shard_map/ppermute | solution.py:540
  37.7 0.8 %shard_map.140 = (bf16[8,64,512]{2,1,0:T(8,128)(2,1)S(1)}, f32[8,8,256]{2,1,0:T(8,128)S(1)}) custom-call(f32[8,72,256]{2,1,0:T(8,128)S(1)} %get-tuple-element.85.refs_0_.map_ref, f32[72,128]{1,0:T(8,128)S(1)} %get-tuple-element.87.seen_ref), custom_call_target="tpu_custom_call" | custom-call | tf_op jit(solution)/shard_map/pallas_call | solution.py:505
  38.5 0.9 %collective-permute-done.7.got_ref = f32[16,128]{1,0:T(8,128)S(1)} collective-permute-done((f32[16,128]{1,0:T(8,128)S(1)}, f32[16,128]{1,0:T(8,128)S(1)}, u32[]{:S(2)}, u32[]{:S(2)}) %collective-permute-start.7) | collective-permute-done | bytes 8224 | tf_op jit(solution)/shard_map/ppermute | solution.py:540
  39.3 0.9 %shard_map.141 = (f32[8,2,64]{2,1,0:T(2,128)}, f32[8,2,32]{2,1,0:T(2,128)}, f32[1,2]{1,0:T(1,128)}) custom-call(f32[16,128]{1,0:T(8,128)S(1)} %get-tuple-element.86.own_ref, f32[16,128]{1,0:T(8,128)S(1)} %collective-permute-done.7.got_ref, f32[8,128]{1,0:T(8,128)S(1)} %get-tuple-element.55.refs_0_.init_ref, ...), custom_call_target="tpu_custom_call" | custom-call | tf_op jit(solution)/shard_map/pallas_call | solution.py:505
  (14 shorter events, 1.7 us)
Async XLA Ops:
  3.9 1.4 %collective-permute-start = (f32[2,72,128]{2,1,0:T(8,128)S(1)}, f32[2,72,128]{2,1,0:T(8,128)S(1)}, u32[]{:S(2)}, u32[]{:S(2)}) collective-permute-start(f32[2,72,128]{2,1,0:T(8,128)S(1)} %get-tuple-element.50.own_ref), channel_id=1, source_target_pairs={{0,1},{1,0},{2,3},{3,2},{4,5},{5,4},{6,7},{7,6},{8,9},{9,8},{10,11... | collective-permute-start | bytes 221192 | tf_op jit(solution)/shard_map/ppermute | solution.py:540
  5.3 3.3 %copy-start = (f32[32,32]{1,0:T(8,128)S(1)}, f32[32,32]{1,0:T(8,128)}, u32[]{:S(2)}) copy-start(f32[32,32]{1,0:T(8,128)} %rf_ref.1) | copy-start | bytes 12292
  5.3 3.3 %copy-start.1 = (f32[8,2,64]{2,1,0:T(2,128)S(1)}, f32[8,2,64]{2,1,0:T(2,128)}, u32[]{:S(2)}) copy-start(f32[8,2,64]{2,1,0:T(2,128)} %d_ref.1) | copy-start | bytes 12292
  5.3 3.3 %copy-start.2 = (f32[8,2,32]{2,1,0:T(2,128)S(1)}, f32[8,2,32]{2,1,0:T(2,128)}, u32[]{:S(2)}) copy-start(f32[8,2,32]{2,1,0:T(2,128)} %cg_ref.1) | copy-start | bytes 6148
  5.7 5.5 %collective-permute-start.1 = (f32[2,72,128]{2,1,0:T(8,128)S(1)}, f32[2,72,128]{2,1,0:T(8,128)S(1)}, u32[]{:S(2)}, u32[]{:S(2)}) collective-permute-start(f32[2,72,128]{2,1,0:T(8,128)S(1)} %get-tuple-element.51.own_ref), channel_id=1, source_target_pairs={{0,2},{1,3},{2,0},{3,1},{4,6},{5,7},{6,4},{7,5},{8,10},{9,11},{10,... | collective-permute-start | bytes 221192 | tf_op jit(solution)/shard_map/ppermute | solution.py:540
  8.6 0.7 %copy-start.3 = (f32[2,64]{1,0:T(2,128)S(1)}, f32[2,64]{1,0:T(2,128)}, u32[]{:S(2)}) copy-start(f32[2,64]{1,0:T(2,128)} %x_ref.1) | copy-start | bytes 1540
  11.6 4.4 %collective-permute-start.2 = (f32[2,72,128]{2,1,0:T(8,128)S(1)}, f32[2,72,128]{2,1,0:T(8,128)S(1)}, u32[]{:S(2)}, u32[]{:S(2)}) collective-permute-start(f32[2,72,128]{2,1,0:T(8,128)S(1)} %get-tuple-element.56.own_ref), channel_id=1, source_target_pairs={{0,4},{1,5},{2,6},{3,7},{4,0},{5,1},{6,2},{7,3},{8,12},{9,13},{10,... | collective-permute-start | bytes 221192 | tf_op jit(solution)/shard_map/ppermute | solution.py:540
  16.7 4.9 %collective-permute-start.3 = (f32[72,128]{1,0:T(8,128)S(1)}, f32[72,128]{1,0:T(8,128)S(1)}, u32[]{:S(2)}, u32[]{:S(2)}) collective-permute-start(f32[72,128]{1,0:T(8,128)S(1)} %get-tuple-element.59), channel_id=1, source_target_pairs={{0,8},{1,9},{2,10},{3,11},{4,12},{5,13},{6,14},{7,15},{8,0},{9,1},... | collective-permute-start | bytes 110600 | tf_op jit(solution)/shard_map/ppermute | solution.py:540
  24.7 1.3 %collective-permute-start.4 = (f32[80,128]{1,0:T(8,128)S(1)}, f32[80,128]{1,0:T(8,128)S(1)}, u32[]{:S(2)}, u32[]{:S(2)}) collective-permute-start(f32[80,128]{1,0:T(8,128)S(1)} %get-tuple-element.80.args_0_), channel_id=1, source_target_pairs={{0,1},{1,0},{2,3},{3,2},{4,5},{5,4},{6,7},{7,6},{8,9},{9,8},{10,11... | collective-permute-start | bytes 122888 | tf_op jit(solution)/shard_map/ppermute | solution.py:540
  26.1 4.1 %collective-permute-start.5 = (f32[80,128]{1,0:T(8,128)S(1)}, f32[80,128]{1,0:T(8,128)S(1)}, u32[]{:S(2)}, u32[]{:S(2)}) collective-permute-start(f32[80,128]{1,0:T(8,128)S(1)} %get-tuple-element.81.own_ref), channel_id=1, source_target_pairs={{0,2},{1,3},{2,0},{3,1},{4,6},{5,7},{6,4},{7,5},{8,10},{9,11},{10,... | collective-permute-start | bytes 122888 | tf_op jit(solution)/shard_map/ppermute | solution.py:540
  30.4 4.1 %collective-permute-start.6 = (f32[80,128]{1,0:T(8,128)S(1)}, f32[80,128]{1,0:T(8,128)S(1)}, u32[]{:S(2)}, u32[]{:S(2)}) collective-permute-start(f32[80,128]{1,0:T(8,128)S(1)} %get-tuple-element.83.own_ref), channel_id=1, source_target_pairs={{0,4},{1,5},{2,6},{3,7},{4,0},{5,1},{6,2},{7,3},{8,12},{9,13},{10,... | collective-permute-start | bytes 122888 | tf_op jit(solution)/shard_map/ppermute | solution.py:540
  34.8 4.6 %collective-permute-start.7 = (f32[16,128]{1,0:T(8,128)S(1)}, f32[16,128]{1,0:T(8,128)S(1)}, u32[]{:S(2)}, u32[]{:S(2)}) collective-permute-start(f32[16,128]{1,0:T(8,128)S(1)} %get-tuple-element.86.own_ref), channel_id=1, source_target_pairs={{0,8},{1,9},{2,10},{3,11},{4,12},{5,13},{6,14},{7,15},{8,0},{9,1},... | collective-permute-start | bytes 24584 | tf_op jit(solution)/shard_map/ppermute | solution.py:540

commit v4 on v3

--- a/solution.py
+++ b/solution.py
@@ -536,8 +536,9 @@
     sizes = dict(trajs=trajs, width=width)
     steps = [1 << i for i in range(devices.bit_length() - 1)]
 
-    def exchange(value, step):
-        return lax.ppermute(value, "tm", [(i, i ^ step) for i in range(devices)])
+    def exchange(value, step, turn=1):
+        apart = step ^ turn if step > 1 else step
+        return lax.ppermute(value, "tm", [(i, i ^ apart) for i in range(devices)])
 
     stack = trajs * nu
     groups, up16 = count * stack // LANES, lambda n: -(-n // 16) * 16
@@ -569,7 +570,7 @@
             functools.partial(value_step_kernel, step, **sizes), [(2, size, both)] * 2,
             total, got, after, *unread(i == 0, init),
         )
-    got = exchange(total, steps[-2])
+    got = exchange(total, steps[-2], turn=0)
     value, after = call(
         functools.partial(value_last_kernel, steps[-2], **sizes),
         [(size, both), (2, size, both)], total, got, after, term, suffix,

time: 40.5 us -> 38.3 us (0.946)
  starting transfers between devices: 14.9 us -> 13.5 us
  waiting for transfers between devices: 9.58 us -> 8.72 us
    ppermute x8, starting transfers between devices: 14.9 us -> 13.5 us  [exchange(): return lax.ppermute(value, 'tm', [(i, i ^ apart) for i in range(devices)])]
    ppermute x8, waiting for transfers between devices: 9.58 us -> 8.72 us  [exchange(): return lax.ppermute(value, 'tm', [(i, i ^ apart) for i in range(devices)])]
where the time goes in v4:
time: 38.3 us; the launch traced here: 38.1 us
  Pallas kernels  14.4 us (38%)
  starting transfers between devices  13.5 us (35%)
  waiting for transfers between devices  8.72 us (23%)
  between operations  0.71 us (2%)
  local copies, waits for them, and re-layouts  0.68 us (2%)
    pallas_call x14, Pallas kernels, call(): pl.pallas_call(body, out_shape=[jax.ShapeDtypeStruct(shape, F32) if isins...  14.4 us
    ppermute x8, starting transfers between devices, exchange(): return lax.ppermute(value, 'tm', [(i, i ^ apart) for i in range(devices)])  13.5 us
    ppermute x8, waiting for transfers between devices, exchange(): return lax.ppermute(value, 'tm', [(i, i ^ apart) for i in range(devices)])  8.72 us
  transfers between devices with their start and end apart: 8, of which 8 were waited for; matrix products, arithmetic and copies ran while one was open for 0% of the time, Pallas kernels for 13%

profile of v4, /device:TPU:0, one launch (start us, length us, event | category | flops | bytes accessed | tf_op | source)
XLA Modules:
  0.0 38.1 jit_solution(3744585523760828033)
XLA Ops:
  0.6 3.3 %shard_map.128 = (f32[2,72,128]{2,1,0:T(8,128)S(1)}, f32[8,2,72,128]{3,2,1,0:T(8,128)S(1)}, f32[72,128]{1,0:T(8,128)S(1)}, f32[8,64,128]{2,1,0:T(8,128)S(1)}, f32[8,32,128]{2,1,0:T(8,128)S(1)}) custom-call(f32[8,2,64,64]{3,2,1,0:T(8,128)} %refs_0_.1, f32[8,2,32,64]{3,2,1,0:T(8,128)} %bitcast.2, f32[8,2,32,64]{3,2,1,0:T(8,128)} %refs_2_.1, ...), custom_call_target="tpu_custom_call" | custom-call | tf_op jit(solution)/shard_map/pallas_call | solution.py:505
  3.9 0.5 %collective-permute-start = (f32[2,72,128]{2,1,0:T(8,128)S(1)}, f32[2,72,128]{2,1,0:T(8,128)S(1)}, u32[]{:S(2)}, u32[]{:S(2)}) collective-permute-start(f32[2,72,128]{2,1,0:T(8,128)S(1)} %get-tuple-element.50.own_ref), channel_id=1, source_target_pairs={{0,1},{1,0},{2,3},{3,2},{4,5},{5,4},{6,7},{7,6},{8,9},{9,8},{10,11... | collective-permute-start | bytes 221192 | tf_op jit(solution)/shard_map/ppermute | solution.py:541
  4.4 0.9 %collective-permute-done.got_ref = f32[2,72,128]{2,1,0:T(8,128)S(1)} collective-permute-done((f32[2,72,128]{2,1,0:T(8,128)S(1)}, f32[2,72,128]{2,1,0:T(8,128)S(1)}, u32[]{:S(2)}, u32[]{:S(2)}) %collective-permute-start) | collective-permute-done | bytes 73760 | tf_op jit(solution)/shard_map/ppermute | solution.py:541
  5.7 2.7 %collective-permute-start.1 = (f32[2,72,128]{2,1,0:T(8,128)S(1)}, f32[2,72,128]{2,1,0:T(8,128)S(1)}, u32[]{:S(2)}, u32[]{:S(2)}) collective-permute-start(f32[2,72,128]{2,1,0:T(8,128)S(1)} %get-tuple-element.51.own_ref), channel_id=1, source_target_pairs={{0,3},{1,2},{2,1},{3,0},{4,7},{5,6},{6,5},{7,4},{8,11},{9,10},{10,... | collective-permute-start | bytes 221192 | tf_op jit(solution)/shard_map/ppermute | solution.py:541
  8.4 0.7 %copy-done.3 = f32[2,64]{1,0:T(2,128)S(1)} copy-done((f32[2,64]{1,0:T(2,128)S(1)}, f32[2,64]{1,0:T(2,128)}, u32[]{:S(2)}) %copy-start.3) | copy-done | bytes 536
  9.4 1.4 %collective-permute-done.1.got_ref = f32[2,72,128]{2,1,0:T(8,128)S(1)} collective-permute-done((f32[2,72,128]{2,1,0:T(8,128)S(1)}, f32[2,72,128]{2,1,0:T(8,128)S(1)}, u32[]{:S(2)}, u32[]{:S(2)}) %collective-permute-start.1) | collective-permute-done | bytes 73760 | tf_op jit(solution)/shard_map/ppermute | solution.py:541
  11.2 2.2 %collective-permute-start.2 = (f32[2,72,128]{2,1,0:T(8,128)S(1)}, f32[2,72,128]{2,1,0:T(8,128)S(1)}, u32[]{:S(2)}, u32[]{:S(2)}) collective-permute-start(f32[2,72,128]{2,1,0:T(8,128)S(1)} %get-tuple-element.56.own_ref), channel_id=1, source_target_pairs={{0,4},{1,5},{2,6},{3,7},{4,0},{5,1},{6,2},{7,3},{8,12},{9,13},{10,... | collective-permute-start | bytes 221192 | tf_op jit(solution)/shard_map/ppermute | solution.py:541
  13.4 1.1 %shard_map.132.refs_0_.suffix_ref = f32[7,2,72,128]{3,2,1,0:T(8,128)S(1)} custom-call(f32[8,2,72,128]{3,2,1,0:T(8,128)S(1)} %get-tuple-element.58.own_ref), custom_call_target="tpu_custom_call" | custom-call | tf_op jit(solution)/shard_map/pallas_call | solution.py:505
  14.5 1.5 %collective-permute-done.2.got_ref = f32[2,72,128]{2,1,0:T(8,128)S(1)} collective-permute-done((f32[2,72,128]{2,1,0:T(8,128)S(1)}, f32[2,72,128]{2,1,0:T(8,128)S(1)}, u32[]{:S(2)}, u32[]{:S(2)}) %collective-permute-start.2) | collective-permute-done | bytes 73760 | tf_op jit(solution)/shard_map/ppermute | solution.py:541
  16.0 0.6 %shard_map.133 = (f32[72,128]{1,0:T(8,128)S(1)}, f32[2,72,128]{2,1,0:T(8,128)S(1)}) custom-call(f32[2,72,128]{2,1,0:T(8,128)S(1)} %get-tuple-element.56.own_ref, f32[2,72,128]{2,1,0:T(8,128)S(1)} %collective-permute-done.2.got_ref, f32[2,72,128]{2,1,0:T(8,128)S(1)} %get-tuple-element.57.seen_ref, f32[72,128]{1,0:T(8,128)S(1)} %get-tuple-element.49.term_ref, ...), custom_call_target="tpu_custom_call" | custom-call | tf_op jit(solution)/shard_map/pallas_call | solution.py:505
  16.6 1.5 %collective-permute-start.3 = (f32[72,128]{1,0:T(8,128)S(1)}, f32[72,128]{1,0:T(8,128)S(1)}, u32[]{:S(2)}, u32[]{:S(2)}) collective-permute-start(f32[72,128]{1,0:T(8,128)S(1)} %get-tuple-element.59), channel_id=1, source_target_pairs={{0,9},{1,8},{2,11},{3,10},{4,13},{5,12},{6,15},{7,14},{8,1},{9,0},... | collective-permute-start | bytes 110600 | tf_op jit(solution)/shard_map/ppermute | solution.py:541
  18.1 1.7 %shard_map.134 = (bf16[8,48,256]{2,1,0:T(8,128)(2,1)S(1)}, bf16[8,256,256]{2,1,0:T(8,128)(2,1)S(1)}, bf16[8,256,256]{2,1,0:T(8,128)(2,1)S(1)}, f32[8,64,128]{2,1...) custom-call(f32[7,2,72,128]{3,2,1,0:T(8,128)S(1)} %shard_map.132.refs_0_.suffix_ref, ...), custom_call_target="tpu_custom_call" | custom-call | tf_op jit(solution)/shard_map/pallas_call | solution.py:505
  19.8 1.2 %collective-permute-done.3.end_ref = f32[72,128]{1,0:T(8,128)S(1)} collective-permute-done((f32[72,128]{1,0:T(8,128)S(1)}, f32[72,128]{1,0:T(8,128)S(1)}, u32[]{:S(2)}, u32[]{:S(2)}) %collective-permute-start.3) | collective-permute-done | bytes 36896 | tf_op jit(solution)/shard_map/ppermute | solution.py:541
  21.0 3.1 %shard_map.135 = (f32[80,128]{1,0:T(8,128)S(1)}, f32[8,72,128]{2,1,0:T(8,128)S(1)}, f32[4,72,128]{2,1,0:T(8,128)S(1)}, f32[4,32,128]{2,1,0:T(8,128)S(1)}) custom-call(f32[72,128]{1,0:T(8,128)S(1)} %get-tuple-element.49.term_ref, f32[72,128]{1,0:T(8,128)S(1)} %collective-permute-done.3.end_ref, bf16[8,48,256]{2,1,0:T(8,128)(2,1)S(1)} %get-tuple-element.67.value_ref, ...), custom_call_target="tpu_custom_call" | custom-call | tf_op jit(solution)/shard_map/pallas_call | solution.py:505
  24.5 0.9 %collective-permute-done.4.args_1_ = f32[80,128]{1,0:T(8,128)S(1)} collective-permute-done((f32[80,128]{1,0:T(8,128)S(1)}, f32[80,128]{1,0:T(8,128)S(1)}, u32[]{:S(2)}, u32[]{:S(2)}) %collective-permute-start.4) | collective-permute-done | bytes 40992 | tf_op jit(solution)/shard_map/ppermute | solution.py:541
  25.5 1.7 %collective-permute-start.5 = (f32[80,128]{1,0:T(8,128)S(1)}, f32[80,128]{1,0:T(8,128)S(1)}, u32[]{:S(2)}, u32[]{:S(2)}) collective-permute-start(f32[80,128]{1,0:T(8,128)S(1)} %get-tuple-element.81.own_ref), channel_id=1, source_target_pairs={{0,3},{1,2},{2,1},{3,0},{4,7},{5,6},{6,5},{7,4},{8,11},{9,10},{10,... | collective-permute-start | bytes 122888 | tf_op jit(solution)/shard_map/ppermute | solution.py:541
  27.2 1.8 %collective-permute-done.5.got_ref = f32[80,128]{1,0:T(8,128)S(1)} collective-permute-done((f32[80,128]{1,0:T(8,128)S(1)}, f32[80,128]{1,0:T(8,128)S(1)}, u32[]{:S(2)}, u32[]{:S(2)}) %collective-permute-start.5) | collective-permute-done | bytes 40992 | tf_op jit(solution)/shard_map/ppermute | solution.py:541
  29.2 1.8 %collective-permute-start.6 = (f32[80,128]{1,0:T(8,128)S(1)}, f32[80,128]{1,0:T(8,128)S(1)}, u32[]{:S(2)}, u32[]{:S(2)}) collective-permute-start(f32[80,128]{1,0:T(8,128)S(1)} %get-tuple-element.83.own_ref), channel_id=1, source_target_pairs={{0,5},{1,4},{2,7},{3,6},{4,1},{5,0},{6,3},{7,2},{8,13},{9,12},{10,... | collective-permute-start | bytes 122888 | tf_op jit(solution)/shard_map/ppermute | solution.py:541
  31.0 1.2 %shard_map.136 = (f32[8,2,32,64]{3,2,1,0:T(8,128)}, f32[8,2,32]{2,1,0:T(2,128)}, f32[8,72,256]{2,1,0:T(8,128)S(1)}) custom-call(f32[8,72,128]{2,1,0:T(8,128)S(1)} %get-tuple-element.75.own_ref, f32[4,72,128]{2,1,0:T(8,128)S(1)} %get-tuple-element.76.half_ref, f32[4,32,128]{2,1,0:T(8,128)S(1)} %get-tuple-element.77.q_ref), custom_call_target="tpu_custom_call" | custom-call | tf_op jit(solution)/shard_map/pallas_call | solution.py:505
  32.2 0.5 %collective-permute-done.6.got_ref = f32[80,128]{1,0:T(8,128)S(1)} collective-permute-done((f32[80,128]{1,0:T(8,128)S(1)}, f32[80,128]{1,0:T(8,128)S(1)}, u32[]{:S(2)}, u32[]{:S(2)}) %collective-permute-start.6) | collective-permute-done | bytes 40992 | tf_op jit(solution)/shard_map/ppermute | solution.py:541
  33.0 2.7 %collective-permute-start.7 = (f32[16,128]{1,0:T(8,128)S(1)}, f32[16,128]{1,0:T(8,128)S(1)}, u32[]{:S(2)}, u32[]{:S(2)}) collective-permute-start(f32[16,128]{1,0:T(8,128)S(1)} %get-tuple-element.86.own_ref), channel_id=1, source_target_pairs={{0,9},{1,8},{2,11},{3,10},{4,13},{5,12},{6,15},{7,14},{8,1},{9,0},... | collective-permute-start | bytes 24584 | tf_op jit(solution)/shard_map/ppermute | solution.py:541
  35.7 0.8 %shard_map.140 = (bf16[8,64,512]{2,1,0:T(8,128)(2,1)S(1)}, f32[8,8,256]{2,1,0:T(8,128)S(1)}) custom-call(f32[8,72,256]{2,1,0:T(8,128)S(1)} %get-tuple-element.85.refs_0_.map_ref, f32[72,128]{1,0:T(8,128)S(1)} %get-tuple-element.87.seen_ref), custom_call_target="tpu_custom_call" | custom-call | tf_op jit(solution)/shard_map/pallas_call | solution.py:505
  36.5 0.6 %collective-permute-done.7.got_ref = f32[16,128]{1,0:T(8,128)S(1)} collective-permute-done((f32[16,128]{1,0:T(8,128)S(1)}, f32[16,128]{1,0:T(8,128)S(1)}, u32[]{:S(2)}, u32[]{:S(2)}) %collective-permute-start.7) | collective-permute-done | bytes 8224 | tf_op jit(solution)/shard_map/ppermute | solution.py:541
  37.1 0.9 %shard_map.141 = (f32[8,2,64]{2,1,0:T(2,128)}, f32[8,2,32]{2,1,0:T(2,128)}, f32[1,2]{1,0:T(1,128)}) custom-call(f32[16,128]{1,0:T(8,128)S(1)} %get-tuple-element.86.own_ref, f32[16,128]{1,0:T(8,128)S(1)} %collective-permute-done.7.got_ref, f32[8,128]{1,0:T(8,128)S(1)} %get-tuple-element.55.refs_0_.init_ref, ...), custom_call_target="tpu_custom_call" | custom-call | tf_op jit(solution)/shard_map/pallas_call | solution.py:505
  (14 shorter events, 2.2 us)
Async XLA Ops:
  3.9 1.4 %collective-permute-start = (f32[2,72,128]{2,1,0:T(8,128)S(1)}, f32[2,72,128]{2,1,0:T(8,128)S(1)}, u32[]{:S(2)}, u32[]{:S(2)}) collective-permute-start(f32[2,72,128]{2,1,0:T(8,128)S(1)} %get-tuple-element.50.own_ref), channel_id=1, source_target_pairs={{0,1},{1,0},{2,3},{3,2},{4,5},{5,4},{6,7},{7,6},{8,9},{9,8},{10,11... | collective-permute-start | bytes 221192 | tf_op jit(solution)/shard_map/ppermute | solution.py:541
  5.3 3.1 %copy-start = (f32[32,32]{1,0:T(8,128)S(1)}, f32[32,32]{1,0:T(8,128)}, u32[]{:S(2)}) copy-start(f32[32,32]{1,0:T(8,128)} %rf_ref.1) | copy-start | bytes 12292
  5.3 3.1 %copy-start.1 = (f32[8,2,64]{2,1,0:T(2,128)S(1)}, f32[8,2,64]{2,1,0:T(2,128)}, u32[]{:S(2)}) copy-start(f32[8,2,64]{2,1,0:T(2,128)} %d_ref.1) | copy-start | bytes 12292
  5.3 3.1 %copy-start.2 = (f32[8,2,32]{2,1,0:T(2,128)S(1)}, f32[8,2,32]{2,1,0:T(2,128)}, u32[]{:S(2)}) copy-start(f32[8,2,32]{2,1,0:T(2,128)} %cg_ref.1) | copy-start | bytes 6148
  5.7 5.1 %collective-permute-start.1 = (f32[2,72,128]{2,1,0:T(8,128)S(1)}, f32[2,72,128]{2,1,0:T(8,128)S(1)}, u32[]{:S(2)}, u32[]{:S(2)}) collective-permute-start(f32[2,72,128]{2,1,0:T(8,128)S(1)} %get-tuple-element.51.own_ref), channel_id=1, source_target_pairs={{0,3},{1,2},{2,1},{3,0},{4,7},{5,6},{6,5},{7,4},{8,11},{9,10},{10,... | collective-permute-start | bytes 221192 | tf_op jit(solution)/shard_map/ppermute | solution.py:541
  8.4 0.7 %copy-start.3 = (f32[2,64]{1,0:T(2,128)S(1)}, f32[2,64]{1,0:T(2,128)}, u32[]{:S(2)}) copy-start(f32[2,64]{1,0:T(2,128)} %x_ref.1) | copy-start | bytes 1540
  11.2 4.8 %collective-permute-start.2 = (f32[2,72,128]{2,1,0:T(8,128)S(1)}, f32[2,72,128]{2,1,0:T(8,128)S(1)}, u32[]{:S(2)}, u32[]{:S(2)}) collective-permute-start(f32[2,72,128]{2,1,0:T(8,128)S(1)} %get-tuple-element.56.own_ref), channel_id=1, source_target_pairs={{0,4},{1,5},{2,6},{3,7},{4,0},{5,1},{6,2},{7,3},{8,12},{9,13},{10,... | collective-permute-start | bytes 221192 | tf_op jit(solution)/shard_map/ppermute | solution.py:541
  16.6 4.3 %collective-permute-start.3 = (f32[72,128]{1,0:T(8,128)S(1)}, f32[72,128]{1,0:T(8,128)S(1)}, u32[]{:S(2)}, u32[]{:S(2)}) collective-permute-start(f32[72,128]{1,0:T(8,128)S(1)} %get-tuple-element.59), channel_id=1, source_target_pairs={{0,9},{1,8},{2,11},{3,10},{4,13},{5,12},{6,15},{7,14},{8,1},{9,0},... | collective-permute-start | bytes 110600 | tf_op jit(solution)/shard_map/ppermute | solution.py:541
  24.1 1.3 %collective-permute-start.4 = (f32[80,128]{1,0:T(8,128)S(1)}, f32[80,128]{1,0:T(8,128)S(1)}, u32[]{:S(2)}, u32[]{:S(2)}) collective-permute-start(f32[80,128]{1,0:T(8,128)S(1)} %get-tuple-element.80.args_0_), channel_id=1, source_target_pairs={{0,1},{1,0},{2,3},{3,2},{4,5},{5,4},{6,7},{7,6},{8,9},{9,8},{10,11... | collective-permute-start | bytes 122888 | tf_op jit(solution)/shard_map/ppermute | solution.py:541
  25.5 3.5 %collective-permute-start.5 = (f32[80,128]{1,0:T(8,128)S(1)}, f32[80,128]{1,0:T(8,128)S(1)}, u32[]{:S(2)}, u32[]{:S(2)}) collective-permute-start(f32[80,128]{1,0:T(8,128)S(1)} %get-tuple-element.81.own_ref), channel_id=1, source_target_pairs={{0,3},{1,2},{2,1},{3,0},{4,7},{5,6},{6,5},{7,4},{8,11},{9,10},{10,... | collective-permute-start | bytes 122888 | tf_op jit(solution)/shard_map/ppermute | solution.py:541
  29.2 3.5 %collective-permute-start.6 = (f32[80,128]{1,0:T(8,128)S(1)}, f32[80,128]{1,0:T(8,128)S(1)}, u32[]{:S(2)}, u32[]{:S(2)}) collective-permute-start(f32[80,128]{1,0:T(8,128)S(1)} %get-tuple-element.83.own_ref), channel_id=1, source_target_pairs={{0,5},{1,4},{2,7},{3,6},{4,1},{5,0},{6,3},{7,2},{8,13},{9,12},{10,... | collective-permute-start | bytes 122888 | tf_op jit(solution)/shard_map/ppermute | solution.py:541
  33.0 4.1 %collective-permute-start.7 = (f32[16,128]{1,0:T(8,128)S(1)}, f32[16,128]{1,0:T(8,128)S(1)}, u32[]{:S(2)}, u32[]{:S(2)}) collective-permute-start(f32[16,128]{1,0:T(8,128)S(1)} %get-tuple-element.86.own_ref), channel_id=1, source_target_pairs={{0,9},{1,8},{2,11},{3,10},{4,13},{5,12},{6,15},{7,14},{8,1},{9,0},... | collective-permute-start | bytes 24584 | tf_op jit(solution)/shard_map/ppermute | solution.py:541

commit v5 on v4

--- a/solution.py
+++ b/solution.py
@@ -71,6 +71,23 @@
     return jnp.where(lax.broadcasted_iota(jnp.int32, shape, 0) == 0, jnp.broadcast_to(row, shape), 0.0)
 
 
+def alone(tail):
+    return jnp.where(lax.broadcasted_iota(jnp.int32, tail.shape, 0) == 0, tail, 0.0)
+
+
+def with_second(tail, row):
+    return jnp.where(lax.broadcasted_iota(jnp.int32, tail.shape, 0) == 1, jnp.broadcast_to(row, tail.shape), tail)
+
+
+def one_piece(x, y, width):
+    return jnp.concatenate([x[:width], y[:width], with_second(x[width:], y[width : width + 1])], axis=0)
+
+
+def two_pieces(sent, width):
+    tail = sent[2 * width :]
+    return join(sent[:width], alone(tail)), join(sent[width : 2 * width], tail_of(tail[1:2]))
+
+
 def join(matrix, tail):
     return jnp.concatenate([matrix, tail], axis=0)
 
@@ -141,8 +158,8 @@
     scale = 1.0 / math.sqrt(knots)
     rows = lax.broadcasted_iota(jnp.int32, (nu, nu), 0)
     lanes = lax.broadcasted_iota(jnp.int32, (nu, nu), 1)
-    for i in (7, 2, 1):
-        copies[i].wait()
+    for c in copies:
+        c.wait()
     root = jnp.concatenate([jnp.where(rows == lanes, 1.0, 0.0), rf_ref[...]], axis=1)
     root = spread(jnp.concatenate([root] * trajs, axis=1), trajs)
     pushed = []
@@ -151,8 +168,6 @@
         btp = paired(bt_ref[t])
         btp_ref[t] = btp
         pushed.append(prod(gt, jnp.concatenate([spread(btp, trajs), root], axis=1)))
-    for i in (6, 3, 4, 5):
-        copies[i].wait()
     term = term_of(cf_ref[...], trajs)
     run_q = term / knots
     term_ref[...] = join(term, jnp.zeros((TAIL, both), F32))
@@ -164,7 +179,6 @@
     zs = [w[:, both:] for w in pushed]
     ys = [prod(join(z, tail_of(control[t : t + 1])), spread(z, trajs), flip=True) for t, z in enumerate(zs)]
     ys = [y + join(run_q, tail_of(grad[t : t + 1])) for t, y in enumerate(ys)]
-    copies[0].wait()
     maps = []
     for t, (w, y) in enumerate(zip(pushed, ys)):
         at = a_ref[t].reshape(both, width).T
@@ -176,8 +190,7 @@
     befores = prefixes([x for x, _ in maps], lambda pairs: compose_states(pairs, trajs, width))
     nothing = jnp.zeros_like(maps[0][1])
     parts = apply_values([(x, nothing) for x in befores[:-1]], [y for _, y in maps[1:]], trajs, width)
-    total_ref[0] = befores[-1]
-    total_ref[1] = functools.reduce(jnp.add, parts, maps[0][1])
+    total_ref[...] = one_piece(befores[-1], functools.reduce(jnp.add, parts, maps[0][1]), width)
 
 
 def suffix_kernel(own_ref, *refs, trajs, width):
@@ -231,12 +244,14 @@
 
 
 def reach_kernel(
-    suffix_ref, seen_ref, left_ref, hess_ref, cross_ref, bd_ref, run_r_ref, control_ref,
+    step, suffix_ref, got_ref, seen_ref, left_ref, hess_ref, cross_ref, bd_ref, run_r_ref, control_ref,
     value_out, hess_out, cross_out, bd_out, hess_base, cross_base, *, trajs, width,
 ):
     count, nu = left_ref.shape[0], run_r_ref.shape[0]
     group = count // hess_base.shape[0]
-    seen = (seen_ref[0], seen_ref[1])
+    seen, got = (seen_ref[0], seen_ref[1]), two_pieces(got_ref[...], width)
+    after, = compose_values([(seen, got)], trajs, width)
+    seen = tuple(jnp.where(upper(step), a, b) for a, b in zip(seen, after))
     maps = compose_values([((suffix_ref[t, 0], suffix_ref[t, 1]), seen) for t in range(count - 1)], trajs, width)
     maps.append(seen)
     both = trajs * width
@@ -267,33 +282,27 @@
 def value_step_kernel(step, own_ref, got_ref, seen_ref, *refs, trajs, width):
     total_ref, next_ref = refs[-2:]
     up = upper(step)
-    own, got = (own_ref[0], own_ref[1]), (got_ref[0], got_ref[1])
-    first = [jnp.where(up, g, o) for o, g in zip(own, got)]
-    second = [jnp.where(up, o, g) for o, g in zip(own, got)]
+    own, got = own_ref[...], got_ref[...]
+    first, second = two_pieces(jnp.where(up, got, own), width), two_pieces(jnp.where(up, own, got), width)
+    got = two_pieces(got, width)
     if seen_ref is None:
-        seen = (join(identity_pair(width, trajs), jnp.zeros((TAIL, trajs * width), F32)), jnp.zeros_like(own[0]))
+        seen = (join(identity_pair(width, trajs), jnp.zeros((TAIL, trajs * width), F32)), jnp.zeros_like(got[1]))
         (x, y), = compose_values([(first, second)], trajs, width)
         after = got
     else:
         seen = (seen_ref[0], seen_ref[1])
         (x, y), after = compose_values([(first, second), (seen, got)], trajs, width)
-    total_ref[0] = x
-    total_ref[1] = y
+    total_ref[...] = one_piece(x, y, width)
     next_ref[0] = jnp.where(up, seen[0], after[0])
     next_ref[1] = jnp.where(up, seen[1], after[1])
 
 
-def value_last_kernel(step, own_ref, got_ref, seen_ref, term_ref, *refs, trajs, width):
+def value_last_kernel(step, own_ref, got_ref, term_ref, *refs, trajs, width):
     up = upper(step)
-    own, got = (own_ref[0], own_ref[1]), (got_ref[0], got_ref[1])
-    first = [jnp.where(up, g, o) for o, g in zip(own, got)]
-    second = [jnp.where(up, o, g) for o, g in zip(own, got)]
-    value_ref, next_ref = refs[-2:]
-    seen, term = (seen_ref[0], seen_ref[1]), term_ref[...]
-    total, (sx, sy) = compose_values([(first, second), (seen, got)], trajs, width)
-    value_ref[...], = apply_values([total], [term], trajs, width)
-    next_ref[0] = jnp.where(up, seen[0], sx)
-    next_ref[1] = jnp.where(up, seen[1], sy)
+    own, got = own_ref[...], got_ref[...]
+    first, second = two_pieces(jnp.where(up, got, own), width), two_pieces(jnp.where(up, own, got), width)
+    total, = compose_values([(first, second)], trajs, width)
+    refs[-1][...], = apply_values([total], [term_ref[...]], trajs, width)
 
 
 def factors(packs, size):
@@ -383,10 +392,6 @@
             mine = pushes[g][i * stack : (i + 1) * stack]
             pieces = [mine if k == i else jnp.zeros_like(mine) for k in range(group)]
             maps.append(ad_ref[g * group + i] - product_of(left, right_of(jnp.concatenate(pieces, axis=0))))
-    total_ref[:size] = fold(maps, lambda pairs: compose_states(pairs, trajs, width))
-    for t, m in enumerate(maps):
-        own_ref[t] = m
-
     decrease = jnp.zeros((1, LANES), F32)
     for g, (half, flat) in enumerate(zip(halves, flats)):
         half_ref[g] = half
@@ -399,7 +404,10 @@
             weights = jnp.where((lanes >= at * nu) & (lanes < (at + 1) * nu), column, weights)
         pushed = jnp.sum(weights * hesses[g], axis=0, keepdims=True)
         decrease = decrease + feed * flat[width : width + 1] + 0.5 * (feed * pushed)
-    total_ref[size:] = tail_of(decrease)
+    total = fold(maps, lambda pairs: compose_states(pairs, trajs, width))
+    total_ref[...] = join(total[:width], with_second(total[width:], decrease))
+    for t, m in enumerate(maps):
+        own_ref[t] = m
 
 
 def expand_kernel(
@@ -429,8 +437,11 @@
         map_ref[t] = jnp.concatenate([m, control, jnp.zeros((size, -stack % LANES), F32)], axis=1)
 
 
-def reach_state_kernel(map_ref, seen_ref, out_ref, offset_ref, *, trajs, width, nu):
+def reach_state_kernel(step, map_ref, got_ref, seen_ref, out_ref, offset_ref, *, trajs, width, nu):
     seen = seen_ref[...]
+    got = join(got_ref[:width], alone(got_ref[width:]))
+    after, = compose_states([(got, seen)], trajs, width)
+    seen = jnp.where(upper(step), after, seen)
     rows = jnp.concatenate([seen[:, j * width : (j + 1) * width] for j in range(trajs)], axis=0)
     size, both = seen.shape
     tails = map_ref[:, width:]
@@ -445,33 +456,31 @@
         offset_ref[t] = full[width:] + tails[t]
 
 
+def state_pair(step, own_ref, got_ref, width):
+    up, own, got = upper(step), own_ref[...], got_ref[...]
+    ride = own[width + 1 : width + 2] + got[width + 1 : width + 2]
+    own, got = join(own[:width], alone(own[width:])), join(got[:width], alone(got[width:]))
+    return (jnp.where(up, got, own), jnp.where(up, own, got)), got, ride
+
+
 def state_step_kernel(step, own_ref, got_ref, seen_ref, total_ref, next_ref, *, trajs, width):
-    up = upper(step)
-    size = width + TAIL
-    own, got = own_ref[:size], got_ref[:size]
-    total_ref[size:] = own_ref[size:] + got_ref[size:]
-    pair = (jnp.where(up, got, own), jnp.where(up, own, got))
+    pair, got, ride = state_pair(step, own_ref, got_ref, width)
     if seen_ref is None:
         seen = join(identity_pair(width, trajs), jnp.zeros((TAIL, trajs * width), F32))
-        total_ref[:size], = compose_states([pair], trajs, width)
+        total, = compose_states([pair], trajs, width)
         after = got
     else:
         seen = seen_ref[...]
-        total_ref[:size], after = compose_states([pair, (got, seen)], trajs, width)
-    next_ref[...] = jnp.where(up, after, seen)
-
-
-def state_last_kernel(step, own_ref, got_ref, seen_ref, init_ref, *refs, trajs, width):
-    sent_ref, next_ref = refs[-2:]
-    up = upper(step)
-    size = width + TAIL
-    own, got = own_ref[:size], got_ref[:size]
-    seen = seen_ref[...]
-    pair = (jnp.where(up, got, own), jnp.where(up, own, got))
-    total, after = compose_states([pair, (got, seen)], trajs, width)
-    sent_ref[:TAIL] = prod(init_ref[...], spread(total[:width], trajs)) + total[width:]
-    sent_ref[TAIL:] = own_ref[size:] + got_ref[size:]
-    next_ref[...] = jnp.where(up, after, seen)
+        total, after = compose_states([pair, (got, seen)], trajs, width)
+    total_ref[...] = join(total[:width], with_second(total[width:], ride))
+    next_ref[...] = jnp.where(upper(step), after, seen)
+
+
+def state_last_kernel(step, own_ref, got_ref, init_ref, *refs, trajs, width):
+    pair, _, ride = state_pair(step, own_ref, got_ref, width)
+    total, = compose_states([pair], trajs, width)
+    state = prod(init_ref[...], spread(total[:width], trajs)) + total[width:]
+    refs[-1][...] = with_second(state, ride)
 
 
 def rows_times(row, right, trajs):
@@ -495,7 +504,7 @@
         for j in range(trajs):
             state_ref[t : t + 1, j] = w[j : j + 1, j * width : (j + 1) * width]
             control_ref[t : t + 1, j] = w[j : j + 1, both + j * nu : both + (j + 1) * nu]
-    sums = (own_ref[TAIL : TAIL + 1] + got_ref[TAIL : TAIL + 1]) / knots
+    sums = (own_ref[1:2] + got_ref[1:2]) / knots
     lane = lax.broadcasted_iota(jnp.int32, sums.shape, 1) // nu % trajs
     for j in range(trajs):
         decrease_ref[:, j : j + 1] = jnp.sum(jnp.where(lane == j, sums, 0.0), axis=1, keepdims=True)
@@ -546,7 +555,7 @@
     inputs = (dyn_a, bt, gains, defects, state_grad, control_grad, cost_factor, control_factor)
     total, own, term, at, btp = call(
         functools.partial(block_kernel, knots),
-        [(2, size, both), (count, 2, size, both), (size, both), (count, width, both), (count, nu, both)],
+        [(width + size, both), (count, 2, size, both), (size, both), (count, width, both), (count, nu, both)],
         *[pltpu.with_memory_space_constraint(x, pltpu.HBM) for x in inputs],
         in_specs=[pl.BlockSpec(memory_space=pltpu.HBM)] * len(inputs),
         scratch_shapes=[pltpu.VMEM(x.shape, F32) for x in inputs] + [pltpu.SemaphoreType.DMA((len(inputs),))],
@@ -562,29 +571,29 @@
     )
     got = exchange(total, steps[0])
     total, after = call(
-        functools.partial(without(value_step_kernel, 3), steps[0], **sizes), [(2, size, both)] * 2, total, got
+        functools.partial(without(value_step_kernel, 3), steps[0], **sizes),
+        [(width + size, both), (2, size, both)], total, got
     )
     for i, step in enumerate(steps[1:-2]):
         got = exchange(total, step)
         total, after = call(
-            functools.partial(value_step_kernel, step, **sizes), [(2, size, both)] * 2,
+            functools.partial(value_step_kernel, step, **sizes), [(width + size, both), (2, size, both)],
             total, got, after, *unread(i == 0, init),
         )
     got = exchange(total, steps[-2], turn=0)
-    value, after = call(
-        functools.partial(value_last_kernel, steps[-2], **sizes),
-        [(size, both), (2, size, both)], total, got, after, term, suffix,
+    value, = call(
+        functools.partial(value_last_kernel, steps[-2], **sizes), [(size, both)], total, got, term, suffix
     )
     reach = call(
-        functools.partial(reach_kernel, **sizes),
+        functools.partial(reach_kernel, steps[-2], **sizes),
         [halves(count, up16(nu + TAIL), 2 * both), halves(*turned), halves(*turned), (count, stack, both),
          (groups, nu, LANES), (count, stack, LANES)],
-        suffix, after, left, hess, cross, bd, run_r, control,
+        suffix, got, after, left, hess, cross, bd, run_r, control,
     )
     value = exchange(value, steps[-1])
     total, own, half, q = call(
         functools.partial(solve_kernel, steps[-1]),
-        [(size + TAIL, both), (count, size, both), (groups, size, LANES), (groups, nu, LANES)],
+        [(size, both), (count, size, both), (groups, size, LANES), (groups, nu, LANES)],
         term, value, *reach, gain, ad,
     )
     wide = both + -(-stack // LANES) * LANES
@@ -597,17 +606,16 @@
         body = state_step_kernel if seen else without(state_step_kernel, 3)
         got = exchange(total, step)
         total, after = call(
-            functools.partial(body, step, **sizes), [(size + TAIL, both), (size, both)], total, got, *seen
+            functools.partial(body, step, **sizes), [(size, both), (size, both)], total, got, *seen
         )
         seen = [after]
     got = exchange(total, steps[-2])
-    sent, after = call(
-        functools.partial(state_last_kernel, steps[-2], **sizes),
-        [(2 * TAIL, both), (size, both)], total, got, *seen, init, maps,
+    sent, = call(
+        functools.partial(state_last_kernel, steps[-2], **sizes), [(TAIL, both)], total, got, init, maps
     )
     maps, offsets = call(
-        functools.partial(reach_state_kernel, **sizes, nu=nu),
-        [halves(count, width, 2 * wide), (count, TAIL, wide)], maps, after,
+        functools.partial(reach_state_kernel, steps[-2], **sizes, nu=nu),
+        [halves(count, width, 2 * wide), (count, TAIL, wide)], maps, got, *seen,
     )
     got = exchange(sent, steps[-1])
     states, controls, decrease = call(

time: 38.3 us -> 37.6 us (0.982)
  transfers between devices with their start and end apart: 8 -> 8, of which waited for: 8 -> 8; matrix products, arithmetic and copies ran while one was open for 0% -> 0% of each run, Pallas kernels for 13% -> 15%
where the time goes in v5:
time: 37.6 us; the launch traced here: 37.4 us
  Pallas kernels  14.4 us (38%)
  starting transfers between devices  13.2 us (35%)
  waiting for transfers between devices  8.47 us (23%)
  between operations  0.71 us (2%)
  local copies, waits for them, and re-layouts  0.68 us (2%)
    pallas_call x14, Pallas kernels, call(): pl.pallas_call(body, out_shape=[jax.ShapeDtypeStruct(shape, F32) if isins...  14.4 us
    ppermute x8, starting transfers between devices, exchange(): return lax.ppermute(value, 'tm', [(i, i ^ apart) for i in range(devices)])  13.2 us
    ppermute x8, waiting for transfers between devices, exchange(): return lax.ppermute(value, 'tm', [(i, i ^ apart) for i in range(devices)])  8.47 us
  transfers between devices with their start and end apart: 8, of which 8 were waited for; matrix products, arithmetic and copies ran while one was open for 0% of the time, Pallas kernels for 15%

profile of v5, /device:TPU:0, one launch (start us, length us, event | category | flops | bytes accessed | tf_op | source)
XLA Modules:
  0.0 37.4 jit_solution(298547158427359605)
XLA Ops:
  0.6 3.1 %shard_map.128 = (f32[136,128]{1,0:T(8,128)S(1)}, f32[8,2,72,128]{3,2,1,0:T(8,128)S(1)}, f32[72,128]{1,0:T(8,128)S(1)}, f32[8,64,128]{2,1,0:T(8,128)S(1)}, f32[8,32,128]{2,1,0:T(8,128)S(1)}) custom-call(f32[8,2,64,64]{3,2,1,0:T(8,128)} %refs_0_.1, f32[8,2,32,64]{3,2,1,0:T(8,128)} %bitcast.2, f32[8,2,32,64]{3,2,1,0:T(8,128)} %refs_2_.1, f32[8,2,64]{2,1,0:T(2,128)} %d_ref.1, ...), custom_call_target="tpu_custom_call" | custom-call | tf_op jit(solution)/shard_map/pallas_call | solution.py:514
  4.2 0.9 %collective-permute-done.got_ref = f32[136,128]{1,0:T(8,128)S(1)} collective-permute-done((f32[136,128]{1,0:T(8,128)S(1)}, f32[136,128]{1,0:T(8,128)S(1)}, u32[]{:S(2)}, u32[]{:S(2)}) %collective-permute-start) | collective-permute-done | bytes 69664 | tf_op jit(solution)/shard_map/ppermute | solution.py:550
  5.5 2.7 %collective-permute-start.1 = (f32[136,128]{1,0:T(8,128)S(1)}, f32[136,128]{1,0:T(8,128)S(1)}, u32[]{:S(2)}, u32[]{:S(2)}) collective-permute-start(f32[136,128]{1,0:T(8,128)S(1)} %get-tuple-element.47.own_ref), channel_id=1, source_target_pairs={{0,3},{1,2},{2,1},{3,0},{4,7},{5,6},{6,5},{7,4},{8,11},{9,10},{10,... | collective-permute-start | bytes 208904 | tf_op jit(solution)/shard_map/ppermute | solution.py:550
  8.3 0.7 %copy-done.3 = f32[2,64]{1,0:T(2,128)S(1)} copy-done((f32[2,64]{1,0:T(2,128)S(1)}, f32[2,64]{1,0:T(2,128)}, u32[]{:S(2)}) %copy-start.3) | copy-done | bytes 536
  9.2 1.3 %collective-permute-done.1.got_ref = f32[136,128]{1,0:T(8,128)S(1)} collective-permute-done((f32[136,128]{1,0:T(8,128)S(1)}, f32[136,128]{1,0:T(8,128)S(1)}, u32[]{:S(2)}, u32[]{:S(2)}) %collective-permute-start.1) | collective-permute-done | bytes 69664 | tf_op jit(solution)/shard_map/ppermute | solution.py:550
  10.9 2.2 %collective-permute-start.2 = (f32[136,128]{1,0:T(8,128)S(1)}, f32[136,128]{1,0:T(8,128)S(1)}, u32[]{:S(2)}, u32[]{:S(2)}) collective-permute-start(f32[136,128]{1,0:T(8,128)S(1)} %get-tuple-element.52.own_ref), channel_id=1, source_target_pairs={{0,4},{1,5},{2,6},{3,7},{4,0},{5,1},{6,2},{7,3},{8,12},{9,13},{10,... | collective-permute-start | bytes 208904 | tf_op jit(solution)/shard_map/ppermute | solution.py:550
  13.1 1.1 %shard_map.132.refs_0_.suffix_ref = f32[7,2,72,128]{3,2,1,0:T(8,128)S(1)} custom-call(f32[8,2,72,128]{3,2,1,0:T(8,128)S(1)} %get-tuple-element.53.own_ref), custom_call_target="tpu_custom_call" | custom-call | tf_op jit(solution)/shard_map/pallas_call | solution.py:514
  14.2 1.4 %collective-permute-done.2.got_ref = f32[136,128]{1,0:T(8,128)S(1)} collective-permute-done((f32[136,128]{1,0:T(8,128)S(1)}, f32[136,128]{1,0:T(8,128)S(1)}, u32[]{:S(2)}, u32[]{:S(2)}) %collective-permute-start.2) | collective-permute-done | bytes 69664 | tf_op jit(solution)/shard_map/ppermute | solution.py:550
  15.6 0.5 %shard_map.133 = f32[72,128]{1,0:T(8,128)S(1)} custom-call(f32[136,128]{1,0:T(8,128)S(1)} %get-tuple-element.52.own_ref, f32[136,128]{1,0:T(8,128)S(1)} %collective-permute-done.2.got_ref, f32[72,128]{1,0:T(8,128)S(1)} %get-tuple-element.45.term_ref, f32[7,2,72,128]{3,2,1,0:T(8,128)S(1)} %shard_map.132.refs_0_.suffix_ref), custom_call_target="tpu_custom_call" | custom-call | tf_op jit(solution)/shard_map/pallas_call | solution.py:514
  16.2 1.5 %collective-permute-start.3 = (f32[72,128]{1,0:T(8,128)S(1)}, f32[72,128]{1,0:T(8,128)S(1)}, u32[]{:S(2)}, u32[]{:S(2)}) collective-permute-start(f32[72,128]{1,0:T(8,128)S(1)} %shard_map.133), channel_id=1, source_target_pairs={{0,9},{1,8},{2,11},{3,10},{4,13},{5,12},{6,15},{7,14},{8,1},{9,0},... | collective-permute-start | bytes 110600 | tf_op jit(solution)/shard_map/ppermute | solution.py:550
  17.7 2.0 %shard_map.134 = (bf16[8,48,256]{2,1,0:T(8,128)(2,1)S(1)}, bf16[8,256,256]{2,1,0:T(8,128)(2,1)S(1)}, bf16[8,256,256]{2,1,0:T(8,128)(2,1)S(1)}, f32[8,64,128]{2,1...) custom-call(f32[7,2,72,128]{3,2,1,0:T(8,128)S(1)} %shard_map.132.refs_0_.suffix_ref, ...), custom_call_target="tpu_custom_call" | custom-call | tf_op jit(solution)/shard_map/pallas_call | solution.py:514
  19.7 0.8 %collective-permute-done.3.end_ref = f32[72,128]{1,0:T(8,128)S(1)} collective-permute-done((f32[72,128]{1,0:T(8,128)S(1)}, f32[72,128]{1,0:T(8,128)S(1)}, u32[]{:S(2)}, u32[]{:S(2)}) %collective-permute-start.3) | collective-permute-done | bytes 36896 | tf_op jit(solution)/shard_map/ppermute | solution.py:550
  20.5 2.8 %shard_map.135 = (f32[72,128]{1,0:T(8,128)S(1)}, f32[8,72,128]{2,1,0:T(8,128)S(1)}, f32[4,72,128]{2,1,0:T(8,128)S(1)}, f32[4,32,128]{2,1,0:T(8,128)S(1)}) custom-call(f32[72,128]{1,0:T(8,128)S(1)} %get-tuple-element.45.term_ref, f32[72,128]{1,0:T(8,128)S(1)} %collective-permute-done.3.end_ref, bf16[8,48,256]{2,1,0:T(8,128)(2,1)S(1)} %get-tuple-element.61.value_ref, ...), custom_call_target="tpu_custom_call" | custom-call | tf_op jit(solution)/shard_map/pallas_call | solution.py:514
  23.3 0.8 %collective-permute-start.4 = (f32[72,128]{1,0:T(8,128)S(1)}, f32[72,128]{1,0:T(8,128)S(1)}, u32[]{:S(2)}, u32[]{:S(2)}) collective-permute-start(f32[72,128]{1,0:T(8,128)S(1)} %get-tuple-element.74.args_0_), channel_id=1, source_target_pairs={{0,1},{1,0},{2,3},{3,2},{4,5},{5,4},{6,7},{7,6},{8,9},{9,8},{10,11... | collective-permute-start | bytes 110600 | tf_op jit(solution)/shard_map/ppermute | solution.py:550
  24.1 0.9 %collective-permute-done.4.args_1_ = f32[72,128]{1,0:T(8,128)S(1)} collective-permute-done((f32[72,128]{1,0:T(8,128)S(1)}, f32[72,128]{1,0:T(8,128)S(1)}, u32[]{:S(2)}, u32[]{:S(2)}) %collective-permute-start.4) | collective-permute-done | bytes 36896 | tf_op jit(solution)/shard_map/ppermute | solution.py:550
  25.1 1.5 %collective-permute-start.5 = (f32[72,128]{1,0:T(8,128)S(1)}, f32[72,128]{1,0:T(8,128)S(1)}, u32[]{:S(2)}, u32[]{:S(2)}) collective-permute-start(f32[72,128]{1,0:T(8,128)S(1)} %get-tuple-element.75.own_ref), channel_id=1, source_target_pairs={{0,3},{1,2},{2,1},{3,0},{4,7},{5,6},{6,5},{7,4},{8,11},{9,10},{10,... | collective-permute-start | bytes 110600 | tf_op jit(solution)/shard_map/ppermute | solution.py:550
  26.7 1.9 %collective-permute-done.5.got_ref = f32[72,128]{1,0:T(8,128)S(1)} collective-permute-done((f32[72,128]{1,0:T(8,128)S(1)}, f32[72,128]{1,0:T(8,128)S(1)}, u32[]{:S(2)}, u32[]{:S(2)}) %collective-permute-start.5) | collective-permute-done | bytes 36896 | tf_op jit(solution)/shard_map/ppermute | solution.py:550
  28.8 1.6 %collective-permute-start.6 = (f32[72,128]{1,0:T(8,128)S(1)}, f32[72,128]{1,0:T(8,128)S(1)}, u32[]{:S(2)}, u32[]{:S(2)}) collective-permute-start(f32[72,128]{1,0:T(8,128)S(1)} %get-tuple-element.77.own_ref), channel_id=1, source_target_pairs={{0,5},{1,4},{2,7},{3,6},{4,1},{5,0},{6,3},{7,2},{8,13},{9,12},{10,... | collective-permute-start | bytes 110600 | tf_op jit(solution)/shard_map/ppermute | solution.py:550
  30.4 1.2 %shard_map.136 = (f32[8,2,32,64]{3,2,1,0:T(8,128)}, f32[8,2,32]{2,1,0:T(2,128)}, f32[8,72,256]{2,1,0:T(8,128)S(1)}) custom-call(f32[8,72,128]{2,1,0:T(8,128)S(1)} %get-tuple-element.69.own_ref, f32[4,72,128]{2,1,0:T(8,128)S(1)} %get-tuple-element.70.half_ref, f32[4,32,128]{2,1,0:T(8,128)S(1)} %get-tuple-element.71.q_ref), custom_call_target="tpu_custom_call" | custom-call | tf_op jit(solution)/shard_map/pallas_call | solution.py:514
  31.6 0.7 %collective-permute-done.6.got_ref = f32[72,128]{1,0:T(8,128)S(1)} collective-permute-done((f32[72,128]{1,0:T(8,128)S(1)}, f32[72,128]{1,0:T(8,128)S(1)}, u32[]{:S(2)}, u32[]{:S(2)}) %collective-permute-start.6) | collective-permute-done | bytes 36896 | tf_op jit(solution)/shard_map/ppermute | solution.py:550
  32.5 2.4 %collective-permute-start.7 = (f32[8,128]{1,0:T(8,128)S(1)}, f32[8,128]{1,0:T(8,128)S(1)}, u32[]{:S(2)}, u32[]{:S(2)}) collective-permute-start(f32[8,128]{1,0:T(8,128)S(1)} %shard_map.139.own_ref), channel_id=1, source_target_pairs={{0,9},{1,8},{2,11},{3,10},{4,13},{5,12},{6,15},{7,14},{8,1},{9,0},... | collective-permute-start | bytes 12296 | tf_op jit(solution)/shard_map/ppermute | solution.py:550
  34.9 1.0 %shard_map.140 = (bf16[8,64,512]{2,1,0:T(8,128)(2,1)S(1)}, f32[8,8,256]{2,1,0:T(8,128)S(1)}) custom-call(f32[8,72,256]{2,1,0:T(8,128)S(1)} %get-tuple-element.78.refs_0_.map_ref, f32[72,128]{1,0:T(8,128)S(1)} %collective-permute-done.6.got_ref, f32[72,128]{1,0:T(8,128)S(1)} %get-tuple-element.79.seen_ref), custom_call_target="tpu_custom_call" | custom-call | tf_op jit(solution)/shard_map/pallas_call | solution.py:514
  35.9 0.6 %collective-permute-done.7.got_ref = f32[8,128]{1,0:T(8,128)S(1)} collective-permute-done((f32[8,128]{1,0:T(8,128)S(1)}, f32[8,128]{1,0:T(8,128)S(1)}, u32[]{:S(2)}, u32[]{:S(2)}) %collective-permute-start.7) | collective-permute-done | bytes 4128 | tf_op jit(solution)/shard_map/ppermute | solution.py:550
  36.5 0.9 %shard_map.141 = (f32[8,2,64]{2,1,0:T(2,128)}, f32[8,2,32]{2,1,0:T(2,128)}, f32[1,2]{1,0:T(1,128)}) custom-call(f32[8,128]{1,0:T(8,128)S(1)} %shard_map.139.own_ref, f32[8,128]{1,0:T(8,128)S(1)} %collective-permute-done.7.got_ref, f32[8,128]{1,0:T(8,128)S(1)} %get-tuple-element.51.refs_0_.init_ref, bf16[8,64,512]{2,1,0:T(8,128)(2,1)S(1)} %get-tuple-element.80.map_ref, ...), custom_call_target="tpu_custom_call" | custom-call | tf_op jit(solution)/shard_map/pallas_call | solution.py:514
  (14 shorter events, 2.2 us)
Async XLA Ops:
  3.7 1.4 %collective-permute-start = (f32[136,128]{1,0:T(8,128)S(1)}, f32[136,128]{1,0:T(8,128)S(1)}, u32[]{:S(2)}, u32[]{:S(2)}) collective-permute-start(f32[136,128]{1,0:T(8,128)S(1)} %get-tuple-element.46.own_ref), channel_id=1, source_target_pairs={{0,1},{1,0},{2,3},{3,2},{4,5},{5,4},{6,7},{7,6},{8,9},{9,8},{10,11... | collective-permute-start | bytes 208904 | tf_op jit(solution)/shard_map/ppermute | solution.py:550
  5.2 3.1 %copy-start = (f32[32,32]{1,0:T(8,128)S(1)}, f32[32,32]{1,0:T(8,128)}, u32[]{:S(2)}) copy-start(f32[32,32]{1,0:T(8,128)} %rf_ref.1) | copy-start | bytes 12292
  5.2 3.1 %copy-start.1 = (f32[8,2,64]{2,1,0:T(2,128)S(1)}, f32[8,2,64]{2,1,0:T(2,128)}, u32[]{:S(2)}) copy-start(f32[8,2,64]{2,1,0:T(2,128)} %d_ref.1) | copy-start | bytes 12292
  5.2 3.1 %copy-start.2 = (f32[8,2,32]{2,1,0:T(2,128)S(1)}, f32[8,2,32]{2,1,0:T(2,128)}, u32[]{:S(2)}) copy-start(f32[8,2,32]{2,1,0:T(2,128)} %cg_ref.1) | copy-start | bytes 6148
  5.5 5.0 %collective-permute-start.1 = (f32[136,128]{1,0:T(8,128)S(1)}, f32[136,128]{1,0:T(8,128)S(1)}, u32[]{:S(2)}, u32[]{:S(2)}) collective-permute-start(f32[136,128]{1,0:T(8,128)S(1)} %get-tuple-element.47.own_ref), channel_id=1, source_target_pairs={{0,3},{1,2},{2,1},{3,0},{4,7},{5,6},{6,5},{7,4},{8,11},{9,10},{10,... | collective-permute-start | bytes 208904 | tf_op jit(solution)/shard_map/ppermute | solution.py:550
  8.2 0.7 %copy-start.3 = (f32[2,64]{1,0:T(2,128)S(1)}, f32[2,64]{1,0:T(2,128)}, u32[]{:S(2)}) copy-start(f32[2,64]{1,0:T(2,128)} %x_ref.1) | copy-start | bytes 1540
  10.9 4.7 %collective-permute-start.2 = (f32[136,128]{1,0:T(8,128)S(1)}, f32[136,128]{1,0:T(8,128)S(1)}, u32[]{:S(2)}, u32[]{:S(2)}) collective-permute-start(f32[136,128]{1,0:T(8,128)S(1)} %get-tuple-element.52.own_ref), channel_id=1, source_target_pairs={{0,4},{1,5},{2,6},{3,7},{4,0},{5,1},{6,2},{7,3},{8,12},{9,13},{10,... | collective-permute-start | bytes 208904 | tf_op jit(solution)/shard_map/ppermute | solution.py:550
  16.2 4.3 %collective-permute-start.3 = (f32[72,128]{1,0:T(8,128)S(1)}, f32[72,128]{1,0:T(8,128)S(1)}, u32[]{:S(2)}, u32[]{:S(2)}) collective-permute-start(f32[72,128]{1,0:T(8,128)S(1)} %shard_map.133), channel_id=1, source_target_pairs={{0,9},{1,8},{2,11},{3,10},{4,13},{5,12},{6,15},{7,14},{8,1},{9,0},... | collective-permute-start | bytes 110600 | tf_op jit(solution)/shard_map/ppermute | solution.py:550
  23.3 1.6 %collective-permute-start.4 = (f32[72,128]{1,0:T(8,128)S(1)}, f32[72,128]{1,0:T(8,128)S(1)}, u32[]{:S(2)}, u32[]{:S(2)}) collective-permute-start(f32[72,128]{1,0:T(8,128)S(1)} %get-tuple-element.74.args_0_), channel_id=1, source_target_pairs={{0,1},{1,0},{2,3},{3,2},{4,5},{5,4},{6,7},{7,6},{8,9},{9,8},{10,11... | collective-permute-start | bytes 110600 | tf_op jit(solution)/shard_map/ppermute | solution.py:550
  25.1 3.4 %collective-permute-start.5 = (f32[72,128]{1,0:T(8,128)S(1)}, f32[72,128]{1,0:T(8,128)S(1)}, u32[]{:S(2)}, u32[]{:S(2)}) collective-permute-start(f32[72,128]{1,0:T(8,128)S(1)} %get-tuple-element.75.own_ref), channel_id=1, source_target_pairs={{0,3},{1,2},{2,1},{3,0},{4,7},{5,6},{6,5},{7,4},{8,11},{9,10},{10,... | collective-permute-start | bytes 110600 | tf_op jit(solution)/shard_map/ppermute | solution.py:550
  28.8 3.4 %collective-permute-start.6 = (f32[72,128]{1,0:T(8,128)S(1)}, f32[72,128]{1,0:T(8,128)S(1)}, u32[]{:S(2)}, u32[]{:S(2)}) collective-permute-start(f32[72,128]{1,0:T(8,128)S(1)} %get-tuple-element.77.own_ref), channel_id=1, source_target_pairs={{0,5},{1,4},{2,7},{3,6},{4,1},{5,0},{6,3},{7,2},{8,13},{9,12},{10,... | collective-permute-start | bytes 110600 | tf_op jit(solution)/shard_map/ppermute | solution.py:550
  32.5 3.9 %collective-permute-start.7 = (f32[8,128]{1,0:T(8,128)S(1)}, f32[8,128]{1,0:T(8,128)S(1)}, u32[]{:S(2)}, u32[]{:S(2)}) collective-permute-start(f32[8,128]{1,0:T(8,128)S(1)} %shard_map.139.own_ref), channel_id=1, source_target_pairs={{0,9},{1,8},{2,11},{3,10},{4,13},{5,12},{6,15},{7,14},{8,1},{9,0},... | collective-permute-start | bytes 12296 | tf_op jit(solution)/shard_map/ppermute | solution.py:550

commit v6 on v5

--- a/solution.py
+++ b/solution.py
@@ -486,7 +486,8 @@
 def rows_times(row, right, trajs):
     width = right.shape[0]
     rows = jnp.concatenate([row[:1, j * width : (j + 1) * width] for j in range(trajs)], axis=0)
-    left = jnp.concatenate(split(rows), axis=0)
+    high = rows.astype(jnp.bfloat16).astype(F32)
+    left = jnp.concatenate([high, rows - high], axis=0).astype(jnp.bfloat16)
     w = lax.dot_general(left, right, (((1,), (0,)), ((), ())), preferred_element_type=F32)
     w = w[:trajs] + w[trajs:]
     full = w.shape[1] // 2

time: 37.6 us -> 37.6 us (level)
  no operation moved by 1% of the time
where the time goes in v6:
time: 37.6 us; the launch traced here: 37.4 us
  Pallas kernels  14.4 us (38%)
  starting transfers between devices  13.2 us (35%)
  waiting for transfers between devices  8.47 us (23%)
  between operations  0.71 us (2%)
  local copies, waits for them, and re-layouts  0.68 us (2%)
    pallas_call x14, Pallas kernels, call(): pl.pallas_call(body, out_shape=[jax.ShapeDtypeStruct(shape, F32) if isins...  14.4 us
    ppermute x8, starting transfers between devices, exchange(): return lax.ppermute(value, 'tm', [(i, i ^ apart) for i in range(devices)])  13.2 us
    ppermute x8, waiting for transfers between devices, exchange(): return lax.ppermute(value, 'tm', [(i, i ^ apart) for i in range(devices)])  8.47 us
  transfers between devices with their start and end apart: 8, of which 8 were waited for; matrix products, arithmetic and copies ran while one was open for 0% of the time, Pallas kernels for 15%

profile of v6, /device:TPU:0, one launch (start us, length us, event | category | flops | bytes accessed | tf_op | source)
XLA Modules:
  0.0 37.4 jit_solution(16161930536300727638)
XLA Ops:
  0.6 3.1 %shard_map.128 = (f32[136,128]{1,0:T(8,128)S(1)}, f32[8,2,72,128]{3,2,1,0:T(8,128)S(1)}, f32[72,128]{1,0:T(8,128)S(1)}, f32[8,64,128]{2,1,0:T(8,128)S(1)}, f32[8,32,128]{2,1,0:T(8,128)S(1)}) custom-call(f32[8,2,64,64]{3,2,1,0:T(8,128)} %refs_0_.1, f32[8,2,32,64]{3,2,1,0:T(8,128)} %bitcast.2, f32[8,2,32,64]{3,2,1,0:T(8,128)} %refs_2_.1, f32[8,2,64]{2,1,0:T(2,128)} %d_ref.1, ...), custom_call_target="tpu_custom_call" | custom-call | tf_op jit(solution)/shard_map/pallas_call | solution.py:515
  4.2 0.9 %collective-permute-done.got_ref = f32[136,128]{1,0:T(8,128)S(1)} collective-permute-done((f32[136,128]{1,0:T(8,128)S(1)}, f32[136,128]{1,0:T(8,128)S(1)}, u32[]{:S(2)}, u32[]{:S(2)}) %collective-permute-start) | collective-permute-done | bytes 69664 | tf_op jit(solution)/shard_map/ppermute | solution.py:551
  5.5 2.7 %collective-permute-start.1 = (f32[136,128]{1,0:T(8,128)S(1)}, f32[136,128]{1,0:T(8,128)S(1)}, u32[]{:S(2)}, u32[]{:S(2)}) collective-permute-start(f32[136,128]{1,0:T(8,128)S(1)} %get-tuple-element.47.own_ref), channel_id=1, source_target_pairs={{0,3},{1,2},{2,1},{3,0},{4,7},{5,6},{6,5},{7,4},{8,11},{9,10},{10,... | collective-permute-start | bytes 208904 | tf_op jit(solution)/shard_map/ppermute | solution.py:551
  8.3 0.7 %copy-done.3 = f32[2,64]{1,0:T(2,128)S(1)} copy-done((f32[2,64]{1,0:T(2,128)S(1)}, f32[2,64]{1,0:T(2,128)}, u32[]{:S(2)}) %copy-start.3) | copy-done | bytes 536
  9.2 1.3 %collective-permute-done.1.got_ref = f32[136,128]{1,0:T(8,128)S(1)} collective-permute-done((f32[136,128]{1,0:T(8,128)S(1)}, f32[136,128]{1,0:T(8,128)S(1)}, u32[]{:S(2)}, u32[]{:S(2)}) %collective-permute-start.1) | collective-permute-done | bytes 69664 | tf_op jit(solution)/shard_map/ppermute | solution.py:551
  10.9 2.2 %collective-permute-start.2 = (f32[136,128]{1,0:T(8,128)S(1)}, f32[136,128]{1,0:T(8,128)S(1)}, u32[]{:S(2)}, u32[]{:S(2)}) collective-permute-start(f32[136,128]{1,0:T(8,128)S(1)} %get-tuple-element.52.own_ref), channel_id=1, source_target_pairs={{0,4},{1,5},{2,6},{3,7},{4,0},{5,1},{6,2},{7,3},{8,12},{9,13},{10,... | collective-permute-start | bytes 208904 | tf_op jit(solution)/shard_map/ppermute | solution.py:551
  13.1 1.1 %shard_map.132.refs_0_.suffix_ref = f32[7,2,72,128]{3,2,1,0:T(8,128)S(1)} custom-call(f32[8,2,72,128]{3,2,1,0:T(8,128)S(1)} %get-tuple-element.53.own_ref), custom_call_target="tpu_custom_call" | custom-call | tf_op jit(solution)/shard_map/pallas_call | solution.py:515
  14.2 1.4 %collective-permute-done.2.got_ref = f32[136,128]{1,0:T(8,128)S(1)} collective-permute-done((f32[136,128]{1,0:T(8,128)S(1)}, f32[136,128]{1,0:T(8,128)S(1)}, u32[]{:S(2)}, u32[]{:S(2)}) %collective-permute-start.2) | collective-permute-done | bytes 69664 | tf_op jit(solution)/shard_map/ppermute | solution.py:551
  15.6 0.5 %shard_map.133 = f32[72,128]{1,0:T(8,128)S(1)} custom-call(f32[136,128]{1,0:T(8,128)S(1)} %get-tuple-element.52.own_ref, f32[136,128]{1,0:T(8,128)S(1)} %collective-permute-done.2.got_ref, f32[72,128]{1,0:T(8,128)S(1)} %get-tuple-element.45.term_ref, f32[7,2,72,128]{3,2,1,0:T(8,128)S(1)} %shard_map.132.refs_0_.suffix_ref), custom_call_target="tpu_custom_call" | custom-call | tf_op jit(solution)/shard_map/pallas_call | solution.py:515
  16.2 1.5 %collective-permute-start.3 = (f32[72,128]{1,0:T(8,128)S(1)}, f32[72,128]{1,0:T(8,128)S(1)}, u32[]{:S(2)}, u32[]{:S(2)}) collective-permute-start(f32[72,128]{1,0:T(8,128)S(1)} %shard_map.133), channel_id=1, source_target_pairs={{0,9},{1,8},{2,11},{3,10},{4,13},{5,12},{6,15},{7,14},{8,1},{9,0},... | collective-permute-start | bytes 110600 | tf_op jit(solution)/shard_map/ppermute | solution.py:551
  17.7 2.0 %shard_map.134 = (bf16[8,48,256]{2,1,0:T(8,128)(2,1)S(1)}, bf16[8,256,256]{2,1,0:T(8,128)(2,1)S(1)}, bf16[8,256,256]{2,1,0:T(8,128)(2,1)S(1)}, f32[8,64,128]{2,1...) custom-call(f32[7,2,72,128]{3,2,1,0:T(8,128)S(1)} %shard_map.132.refs_0_.suffix_ref, ...), custom_call_target="tpu_custom_call" | custom-call | tf_op jit(solution)/shard_map/pallas_call | solution.py:515
  19.7 0.8 %collective-permute-done.3.end_ref = f32[72,128]{1,0:T(8,128)S(1)} collective-permute-done((f32[72,128]{1,0:T(8,128)S(1)}, f32[72,128]{1,0:T(8,128)S(1)}, u32[]{:S(2)}, u32[]{:S(2)}) %collective-permute-start.3) | collective-permute-done | bytes 36896 | tf_op jit(solution)/shard_map/ppermute | solution.py:551
  20.5 2.8 %shard_map.135 = (f32[72,128]{1,0:T(8,128)S(1)}, f32[8,72,128]{2,1,0:T(8,128)S(1)}, f32[4,72,128]{2,1,0:T(8,128)S(1)}, f32[4,32,128]{2,1,0:T(8,128)S(1)}) custom-call(f32[72,128]{1,0:T(8,128)S(1)} %get-tuple-element.45.term_ref, f32[72,128]{1,0:T(8,128)S(1)} %collective-permute-done.3.end_ref, bf16[8,48,256]{2,1,0:T(8,128)(2,1)S(1)} %get-tuple-element.61.value_ref, ...), custom_call_target="tpu_custom_call" | custom-call | tf_op jit(solution)/shard_map/pallas_call | solution.py:515
  23.3 0.8 %collective-permute-start.4 = (f32[72,128]{1,0:T(8,128)S(1)}, f32[72,128]{1,0:T(8,128)S(1)}, u32[]{:S(2)}, u32[]{:S(2)}) collective-permute-start(f32[72,128]{1,0:T(8,128)S(1)} %get-tuple-element.74.args_0_), channel_id=1, source_target_pairs={{0,1},{1,0},{2,3},{3,2},{4,5},{5,4},{6,7},{7,6},{8,9},{9,8},{10,11... | collective-permute-start | bytes 110600 | tf_op jit(solution)/shard_map/ppermute | solution.py:551
  24.1 0.9 %collective-permute-done.4.args_1_ = f32[72,128]{1,0:T(8,128)S(1)} collective-permute-done((f32[72,128]{1,0:T(8,128)S(1)}, f32[72,128]{1,0:T(8,128)S(1)}, u32[]{:S(2)}, u32[]{:S(2)}) %collective-permute-start.4) | collective-permute-done | bytes 36896 | tf_op jit(solution)/shard_map/ppermute | solution.py:551
  25.1 1.5 %collective-permute-start.5 = (f32[72,128]{1,0:T(8,128)S(1)}, f32[72,128]{1,0:T(8,128)S(1)}, u32[]{:S(2)}, u32[]{:S(2)}) collective-permute-start(f32[72,128]{1,0:T(8,128)S(1)} %get-tuple-element.75.own_ref), channel_id=1, source_target_pairs={{0,3},{1,2},{2,1},{3,0},{4,7},{5,6},{6,5},{7,4},{8,11},{9,10},{10,... | collective-permute-start | bytes 110600 | tf_op jit(solution)/shard_map/ppermute | solution.py:551
  26.7 1.9 %collective-permute-done.5.got_ref = f32[72,128]{1,0:T(8,128)S(1)} collective-permute-done((f32[72,128]{1,0:T(8,128)S(1)}, f32[72,128]{1,0:T(8,128)S(1)}, u32[]{:S(2)}, u32[]{:S(2)}) %collective-permute-start.5) | collective-permute-done | bytes 36896 | tf_op jit(solution)/shard_map/ppermute | solution.py:551
  28.8 1.6 %collective-permute-start.6 = (f32[72,128]{1,0:T(8,128)S(1)}, f32[72,128]{1,0:T(8,128)S(1)}, u32[]{:S(2)}, u32[]{:S(2)}) collective-permute-start(f32[72,128]{1,0:T(8,128)S(1)} %get-tuple-element.77.own_ref), channel_id=1, source_target_pairs={{0,5},{1,4},{2,7},{3,6},{4,1},{5,0},{6,3},{7,2},{8,13},{9,12},{10,... | collective-permute-start | bytes 110600 | tf_op jit(solution)/shard_map/ppermute | solution.py:551
  30.4 1.2 %shard_map.136 = (f32[8,2,32,64]{3,2,1,0:T(8,128)}, f32[8,2,32]{2,1,0:T(2,128)}, f32[8,72,256]{2,1,0:T(8,128)S(1)}) custom-call(f32[8,72,128]{2,1,0:T(8,128)S(1)} %get-tuple-element.69.own_ref, f32[4,72,128]{2,1,0:T(8,128)S(1)} %get-tuple-element.70.half_ref, f32[4,32,128]{2,1,0:T(8,128)S(1)} %get-tuple-element.71.q_ref), custom_call_target="tpu_custom_call" | custom-call | tf_op jit(solution)/shard_map/pallas_call | solution.py:515
  31.6 0.7 %collective-permute-done.6.got_ref = f32[72,128]{1,0:T(8,128)S(1)} collective-permute-done((f32[72,128]{1,0:T(8,128)S(1)}, f32[72,128]{1,0:T(8,128)S(1)}, u32[]{:S(2)}, u32[]{:S(2)}) %collective-permute-start.6) | collective-permute-done | bytes 36896 | tf_op jit(solution)/shard_map/ppermute | solution.py:551
  32.5 2.4 %collective-permute-start.7 = (f32[8,128]{1,0:T(8,128)S(1)}, f32[8,128]{1,0:T(8,128)S(1)}, u32[]{:S(2)}, u32[]{:S(2)}) collective-permute-start(f32[8,128]{1,0:T(8,128)S(1)} %shard_map.139.own_ref), channel_id=1, source_target_pairs={{0,9},{1,8},{2,11},{3,10},{4,13},{5,12},{6,15},{7,14},{8,1},{9,0},... | collective-permute-start | bytes 12296 | tf_op jit(solution)/shard_map/ppermute | solution.py:551
  34.9 1.0 %shard_map.140 = (bf16[8,64,512]{2,1,0:T(8,128)(2,1)S(1)}, f32[8,8,256]{2,1,0:T(8,128)S(1)}) custom-call(f32[8,72,256]{2,1,0:T(8,128)S(1)} %get-tuple-element.78.refs_0_.map_ref, f32[72,128]{1,0:T(8,128)S(1)} %collective-permute-done.6.got_ref, f32[72,128]{1,0:T(8,128)S(1)} %get-tuple-element.79.seen_ref), custom_call_target="tpu_custom_call" | custom-call | tf_op jit(solution)/shard_map/pallas_call | solution.py:515
  35.9 0.6 %collective-permute-done.7.got_ref = f32[8,128]{1,0:T(8,128)S(1)} collective-permute-done((f32[8,128]{1,0:T(8,128)S(1)}, f32[8,128]{1,0:T(8,128)S(1)}, u32[]{:S(2)}, u32[]{:S(2)}) %collective-permute-start.7) | collective-permute-done | bytes 4128 | tf_op jit(solution)/shard_map/ppermute | solution.py:551
  36.5 0.9 %shard_map.141 = (f32[8,2,64]{2,1,0:T(2,128)}, f32[8,2,32]{2,1,0:T(2,128)}, f32[1,2]{1,0:T(1,128)}) custom-call(f32[8,128]{1,0:T(8,128)S(1)} %shard_map.139.own_ref, f32[8,128]{1,0:T(8,128)S(1)} %collective-permute-done.7.got_ref, f32[8,128]{1,0:T(8,128)S(1)} %get-tuple-element.51.refs_0_.init_ref, bf16[8,64,512]{2,1,0:T(8,128)(2,1)S(1)} %get-tuple-element.80.map_ref, ...), custom_call_target="tpu_custom_call" | custom-call | tf_op jit(solution)/shard_map/pallas_call | solution.py:515
  (14 shorter events, 2.2 us)
Async XLA Ops:
  3.7 1.4 %collective-permute-start = (f32[136,128]{1,0:T(8,128)S(1)}, f32[136,128]{1,0:T(8,128)S(1)}, u32[]{:S(2)}, u32[]{:S(2)}) collective-permute-start(f32[136,128]{1,0:T(8,128)S(1)} %get-tuple-element.46.own_ref), channel_id=1, source_target_pairs={{0,1},{1,0},{2,3},{3,2},{4,5},{5,4},{6,7},{7,6},{8,9},{9,8},{10,11... | collective-permute-start | bytes 208904 | tf_op jit(solution)/shard_map/ppermute | solution.py:551
  5.2 3.1 %copy-start = (f32[32,32]{1,0:T(8,128)S(1)}, f32[32,32]{1,0:T(8,128)}, u32[]{:S(2)}) copy-start(f32[32,32]{1,0:T(8,128)} %rf_ref.1) | copy-start | bytes 12292
  5.2 3.1 %copy-start.1 = (f32[8,2,64]{2,1,0:T(2,128)S(1)}, f32[8,2,64]{2,1,0:T(2,128)}, u32[]{:S(2)}) copy-start(f32[8,2,64]{2,1,0:T(2,128)} %d_ref.1) | copy-start | bytes 12292
  5.2 3.1 %copy-start.2 = (f32[8,2,32]{2,1,0:T(2,128)S(1)}, f32[8,2,32]{2,1,0:T(2,128)}, u32[]{:S(2)}) copy-start(f32[8,2,32]{2,1,0:T(2,128)} %cg_ref.1) | copy-start | bytes 6148
  5.5 5.0 %collective-permute-start.1 = (f32[136,128]{1,0:T(8,128)S(1)}, f32[136,128]{1,0:T(8,128)S(1)}, u32[]{:S(2)}, u32[]{:S(2)}) collective-permute-start(f32[136,128]{1,0:T(8,128)S(1)} %get-tuple-element.47.own_ref), channel_id=1, source_target_pairs={{0,3},{1,2},{2,1},{3,0},{4,7},{5,6},{6,5},{7,4},{8,11},{9,10},{10,... | collective-permute-start | bytes 208904 | tf_op jit(solution)/shard_map/ppermute | solution.py:551
  8.2 0.7 %copy-start.3 = (f32[2,64]{1,0:T(2,128)S(1)}, f32[2,64]{1,0:T(2,128)}, u32[]{:S(2)}) copy-start(f32[2,64]{1,0:T(2,128)} %x_ref.1) | copy-start | bytes 1540
  10.9 4.7 %collective-permute-start.2 = (f32[136,128]{1,0:T(8,128)S(1)}, f32[136,128]{1,0:T(8,128)S(1)}, u32[]{:S(2)}, u32[]{:S(2)}) collective-permute-start(f32[136,128]{1,0:T(8,128)S(1)} %get-tuple-element.52.own_ref), channel_id=1, source_target_pairs={{0,4},{1,5},{2,6},{3,7},{4,0},{5,1},{6,2},{7,3},{8,12},{9,13},{10,... | collective-permute-start | bytes 208904 | tf_op jit(solution)/shard_map/ppermute | solution.py:551
  16.2 4.3 %collective-permute-start.3 = (f32[72,128]{1,0:T(8,128)S(1)}, f32[72,128]{1,0:T(8,128)S(1)}, u32[]{:S(2)}, u32[]{:S(2)}) collective-permute-start(f32[72,128]{1,0:T(8,128)S(1)} %shard_map.133), channel_id=1, source_target_pairs={{0,9},{1,8},{2,11},{3,10},{4,13},{5,12},{6,15},{7,14},{8,1},{9,0},... | collective-permute-start | bytes 110600 | tf_op jit(solution)/shard_map/ppermute | solution.py:551
  23.3 1.6 %collective-permute-start.4 = (f32[72,128]{1,0:T(8,128)S(1)}, f32[72,128]{1,0:T(8,128)S(1)}, u32[]{:S(2)}, u32[]{:S(2)}) collective-permute-start(f32[72,128]{1,0:T(8,128)S(1)} %get-tuple-element.74.args_0_), channel_id=1, source_target_pairs={{0,1},{1,0},{2,3},{3,2},{4,5},{5,4},{6,7},{7,6},{8,9},{9,8},{10,11... | collective-permute-start | bytes 110600 | tf_op jit(solution)/shard_map/ppermute | solution.py:551
  25.1 3.4 %collective-permute-start.5 = (f32[72,128]{1,0:T(8,128)S(1)}, f32[72,128]{1,0:T(8,128)S(1)}, u32[]{:S(2)}, u32[]{:S(2)}) collective-permute-start(f32[72,128]{1,0:T(8,128)S(1)} %get-tuple-element.75.own_ref), channel_id=1, source_target_pairs={{0,3},{1,2},{2,1},{3,0},{4,7},{5,6},{6,5},{7,4},{8,11},{9,10},{10,... | collective-permute-start | bytes 110600 | tf_op jit(solution)/shard_map/ppermute | solution.py:551
  28.8 3.4 %collective-permute-start.6 = (f32[72,128]{1,0:T(8,128)S(1)}, f32[72,128]{1,0:T(8,128)S(1)}, u32[]{:S(2)}, u32[]{:S(2)}) collective-permute-start(f32[72,128]{1,0:T(8,128)S(1)} %get-tuple-element.77.own_ref), channel_id=1, source_target_pairs={{0,5},{1,4},{2,7},{3,6},{4,1},{5,0},{6,3},{7,2},{8,13},{9,12},{10,... | collective-permute-start | bytes 110600 | tf_op jit(solution)/shard_map/ppermute | solution.py:551
  32.5 3.9 %collective-permute-start.7 = (f32[8,128]{1,0:T(8,128)S(1)}, f32[8,128]{1,0:T(8,128)S(1)}, u32[]{:S(2)}, u32[]{:S(2)}) collective-permute-start(f32[8,128]{1,0:T(8,128)S(1)} %shard_map.139.own_ref), channel_id=1, source_target_pairs={{0,9},{1,8},{2,11},{3,10},{4,13},{5,12},{6,15},{7,14},{8,1},{9,0},... | collective-permute-start | bytes 12296 | tf_op jit(solution)/shard_map/ppermute | solution.py:551
